TPU v7x, 256 devices: a whole 4x4x8 slice. The times are simulated.
256 devices in a mesh: blk: 128 (over y, z, x_hi, core), rep: 2 (over x_lo).
Axes of the slice: x: 4 (x_hi: 2, x_lo: 2; x = x_hi * 2 + x_lo), y: 4, z: 8, core: 2. Of those that a mesh axis runs over, the one named last changes fastest.
Arguments:
- points: float32 [32, 262144], P(None, 'blk'), may hold values from -6 to 6
- inv_length: float32 [32], replicated, may hold values from 0.08 to 0.3
- direction: float32 [32, 262144], P(None, 'blk'), may hold values from -6 to 6
- residual: float32 [32, 262144], P(None, 'blk'), may hold values from -6 to 6
- solution: float32 [32, 262144], P(None, 'blk'), may hold values from -6 to 6
- active: int32 [32], replicated, may hold values 0 or 1
Outputs:
- solution_next: float32 [32, 262144], P(None, 'blk')
- residual_next: float32 [32, 262144], P(None, 'blk')
- direction_next: float32 [32, 262144], P(None, 'blk')
All inputs are finite; a program needn't handle non-finite values.
Results may differ from a plain program's by a relative error of at most 0.0001.
Values sent between devices are 32-bit elements; how exact they have to be, the bound alone decides.
No kernel may reach another device: no remote copies, remote signals or barrier semaphores. Data moves between devices by JAX's collectives and lax.ppermute only.
A program may use at most 64 MiB of HBM per device.

v0:
```python
import math

import jax
import jax.numpy as jnp
from jax import lax
from jax.sharding import PartitionSpec as P

ROOT_FIVE = math.sqrt(5.0)
NOISE = 0.5


def from_behind(value, axis, by):
    peers = lax.axis_size(axis)
    return lax.ppermute(value, axis, [(i, (i + by) % peers) for i in range(peers)])


def matern(left_pts, right_pts):
    cross = lax.dot_general(
        left_pts, right_pts, (((0,), (0,)), ((), ())), precision=lax.Precision.HIGHEST
    )
    sq_dist = (
        jnp.sum(left_pts * left_pts, 0)[:, None]
        + jnp.sum(right_pts * right_pts, 0)[None, :]
        - 2.0 * cross
    )
    scaled_dist = ROOT_FIVE * jnp.sqrt(jnp.maximum(sq_dist, 0.0))
    return (1.0 + scaled_dist + scaled_dist * scaled_dist / 3.0) * jnp.exp(-scaled_dist)


def apply_left(vectors, kernel):
    return lax.dot_general(
        vectors, kernel, (((1,), (1,)), ((), ())), precision=lax.Precision.HIGHEST
    )


def apply_right(vectors, kernel):
    return jnp.dot(vectors, kernel, precision=lax.Precision.HIGHEST)


def one_sided(own_pts, other_pts, other_dir):
    row_total = own_pts.shape[1]
    row_piece = min(512, row_total)
    turns = row_total // row_piece

    def one_advance(position, result):
        row_start = position * row_piece
        rows_pts = lax.dynamic_slice_in_dim(own_pts, row_start, row_piece, 1)
        kernel = matern(rows_pts, other_pts)
        return lax.dynamic_update_slice_in_dim(result, apply_left(other_dir, kernel), row_start, 1)

    initial = jnp.zeros((other_dir.shape[0], row_total), jnp.float32)
    return lax.fori_loop(0, turns, one_advance, initial)


def two_sided(own_pts, own_dir, other_pts, other_dir):
    row_total = own_pts.shape[1]
    row_piece = min(512, row_total)
    turns = row_total // row_piece

    def two_advance(position, carried):
        result, returned = carried
        row_start = position * row_piece
        rows_pts = lax.dynamic_slice_in_dim(own_pts, row_start, row_piece, 1)
        rows_dir = lax.dynamic_slice_in_dim(own_dir, row_start, row_piece, 1)
        kernel = matern(rows_pts, other_pts)
        result = lax.dynamic_update_slice_in_dim(
            result, apply_left(other_dir, kernel), row_start, 1
        )
        return (result, returned + apply_right(rows_dir, kernel))

    initial = jnp.zeros((other_dir.shape[0], row_total), jnp.float32)
    return lax.fori_loop(0, turns, two_advance, (initial, jnp.zeros_like(initial)))


def on_device(points, inv_length, direction, residual, solution, active):
    scaled_pts = points * inv_length[:, None]
    columns = scaled_pts.shape[1]
    halfway = columns // 2
    offset_step = 2 * (lax.axis_size("blk") // 4) + 1
    local_norm = jnp.sum(residual * residual, 1)
    norm_old = lax.psum(local_norm, "blk")
    far_pts, far_dir = from_behind((scaled_pts, direction), ("blk", "rep"), offset_step)
    own_part, back_part = two_sided(scaled_pts, direction, far_pts, far_dir)
    gained = own_part + from_behind(back_part, ("blk", "rep"), -offset_step)
    row_start = lax.axis_index("rep") * halfway
    rows_pts = lax.dynamic_slice_in_dim(scaled_pts, row_start, halfway, 1)
    diagonal_part = 4.0 * one_sided(rows_pts, scaled_pts, direction)
    placed = lax.dynamic_update_slice_in_dim(jnp.zeros_like(direction), diagonal_part, row_start, 1)
    image = lax.psum(gained + placed, "rep") + NOISE * direction
    local_curve = jnp.sum(direction * image, 1)
    curvature = lax.psum(local_curve, "blk")
    live = active.astype(jnp.float32)
    alpha_vals = live * norm_old / curvature
    solution_next = solution + alpha_vals[:, None] * direction
    residual_next = residual - alpha_vals[:, None] * image
    norm_new = lax.psum(jnp.sum(residual_next * residual_next, 1), "blk")
    updated = residual_next + (norm_new / norm_old)[:, None] * direction
    direction_next = jnp.where(active[:, None] == 1, updated, direction)
    return (solution_next, residual_next, direction_next)


def solution(mesh):
    placed = (P(None, "blk"), P(), P(None, "blk"), P(None, "blk"), P(None, "blk"), P())
    return jax.shard_map(
        on_device,
        mesh=mesh,
        in_specs=placed,
        out_specs=(P(None, "blk"), P(None, "blk"), P(None, "blk")),
        check_vma=False,
    )
```

profile of v0, /device:TPU:1, one launch (start us, length us, event | category | flops | bytes accessed | tf_op | source)
XLA Modules:
  0.0 816.0 jit_solution(15904008074756856083)
XLA Ops:
  14.2 3.3 collective-permute-done
  17.5 4.6 collective-permute-done.1
  22.1 65.9 %while.34 = (s32[]{:T(128)}, f32[32,2048]{1,0:T(8,128)S(1)}, f32[32,2048]{1,0:T(8,128)S(1)}, f32[32,2048]{1,0:T(8,128)S(1)}, f32[2048]{0:T(1024)S(1)}, /*index=5...) while((s32[]{:T(128)}, f32[32,2048]{1,0:T(8,128)S(1)}, ...), condition=%wide.region_5.0_spmd.clone, body=%wide.region_3.5_spmd.clone.sunk | while | flops 1219657216 | bytes 30683352 | solution.py:72
  22.2 7.6 exponential_multiply_fusion.2
  29.8 4.9 convolution_add_fusion.2
  34.7 3.9 fusion.71
  38.7 7.6 exponential_multiply_fusion.2
  46.3 4.9 convolution_add_fusion.2
  51.2 3.9 fusion.71
  55.1 7.6 exponential_multiply_fusion.2
  62.8 4.9 convolution_add_fusion.2
  67.7 3.9 fusion.71
  71.6 7.6 exponential_multiply_fusion.2
  79.3 4.9 convolution_add_fusion.2
  84.1 3.9 fusion.71
  88.1 6.1 collective-permute-start.2
  94.2 20.2 %while.33 = (s32[]{:T(128)}, f32[32,1024]{1,0:T(8,128)S(1)}, f32[32,1024]{1,0:T(8,128)S(1)}, f32[2048]{0:T(1024)S(1)}, f32[32,2048]{1,0:T(8,128)S(1)}, /*index=5...) while((s32[]{:T(128)}, f32[32,1024]{1,0:T(8,128)S(1)}, f32[32,1024]{1,0:T(8,128)S(1)}, ...), condition=%wide.region_9.0_spmd, body=%wide.region_7.9_spmd.sunk | while | flops 816872960 | bytes 10170555 | solution.py:52
  94.3 3.5 fusion.63
  97.8 6.5 fusion.64
  104.4 3.5 fusion.63
  108.0 6.5 fusion.64
  115.5 34.3 %all-reduce.3.cloned.1.call-done = f32[32,2048]{1,0:T(8,128)} async-done(((f32[32,2048]{1,0:T(8,128)}), f32[32,2048]{1,0:T(8,128)}) %all-reduce.3.cloned.1.call-update) | async-done | bytes 262160 | tf_op jit(solution)/shard_map/psum | solution.py:89
  150.9 324.5 %all-reduce = (f32[32]{0:T(128)S(1)}, f32[32]{0:T(128)S(1)}) all-reduce(f32[32]{0:T(128)S(1)} %multiply_reduce_fusion.3, f32[32]{0:T(128)S(1)} %multiply_reduce_fusion.6), channel_id=1, replica_groups=mesh['blk'=128,'rep'=2] {'blk'}, use_global_device_ids=true, to_apply=%region_12.0 | all-reduce | flops 64 | bytes 512 | tf_op jit(solution)/shard_map/psum | solution.py:91
  477.4 330.0 %psum.31 = f32[32]{0:T(128)S(1)} all-reduce(f32[32]{0:T(128)S(1)} %get-tuple-element.372), channel_id=1, replica_groups=mesh['blk'=128,'rep'=2] {'blk'}, use_global_device_ids=true, to_apply=%region_14.0 | all-reduce | flops 32 | bytes 256 | tf_op jit(solution)/shard_map/psum | solution.py:96
  (48 shorter events, 13.1 us)
Async XLA Ops:
  7.2 142.6 %all-reduce.3.cloned.1.call-start = ((), (), s32[]{:S(2)}) async-start(), calls=%async_computation | async-start | bytes 524288 | tf_op jit(solution)/shard_map/psum | solution.py:89
  8.3 9.2 %collective-permute-start = (f32[32,2048]{1,0:T(8,128)S(1)}, f32[32,2048]{1,0:T(8,128)S(1)}, u32[]{:S(2)}, u32[]{:S(2)}) collective-permute-start(f32[32,2048]{1,0:T(8,128)S(1)} %get-tuple-element.503), channel_id=1, source_target_pairs={{0,65},{1,66},{2,67},{3,68},{4,69},{5,70},{6,71},{7,72},{8,73},{9,... | collective-permute-start | bytes 786440 | tf_op jit(solution)/shard_map/ppermute | solution.py:14
  11.4 10.7 %collective-permute-start.1 = (f32[32,2048]{1,0:T(8,128)}, f32[32,2048]{1,0:T(8,128)S(1)}, u32[]{:S(2)}, u32[]{:S(2)}) collective-permute-start(f32[32,2048]{1,0:T(8,128)} %param.12), channel_id=1, source_target_pairs={{0,65},{1,66},{2,67},{3,68},{4,69},{5,70},{6,71},{7,72},{8,73},{9,... | collective-permute-start | bytes 786440 | tf_op jit(solution)/shard_map/ppermute | solution.py:14
  29.8 4.9 copy-start
  46.3 4.9 copy-start
  62.8 4.9 copy-start
  79.2 4.9 copy-start
  88.1 26.4 %collective-permute-start.2 = (f32[32,2048]{1,0:T(8,128)S(1)}, f32[32,2048]{1,0:T(8,128)S(1)}, u32[]{:S(2)}, u32[]{:S(2)}) collective-permute-start(f32[32,2048]{1,0:T(8,128)S(1)} %get-tuple-element.313), channel_id=1, source_target_pairs={{0,191},{1,192},{2,193},{3,194},{4,195},{5,196},{6,197},{7,198},{8... | collective-permute-start | bytes 786440 | tf_op jit(solution)/shard_map/ppermute | solution.py:14
  94.2 21.1 %copy-start.3 = (f32[32,2048]{1,0:T(8,128)S(1)}, f32[32,2048]{1,0:T(8,128)}, u32[]{:S(2)}) copy-start(f32[32,2048]{1,0:T(8,128)} %param.13) | copy-start | bytes 786436
  94.2 21.2 %copy-start.6 = (s32[32]{0:T(128)S(1)}, s32[32]{0:T(128)}, u32[]{:S(2)}) copy-start(s32[32]{0:T(128)} %param.15) | copy-start | bytes 388
  94.2 381.2 %copy-start.5 = (f32[32,2048]{1,0:T(8,128)S(1)}, f32[32,2048]{1,0:T(8,128)}, u32[]{:S(2)}) copy-start(f32[32,2048]{1,0:T(8,128)} %param.14) | copy-start | bytes 786436
  94.3 3.6 copy-start.1
  104.4 3.6 copy-start.1
  114.6 0.7 copy-start.2
  477.4 331.8 %copy-start.4 = (f32[32,2048]{1,0:T(8,128)}, f32[32,2048]{1,0:T(8,128)S(1)}, u32[]{:S(2)}) copy-start(f32[32,2048]{1,0:T(8,128)S(1)} %get-tuple-element.373) | copy-start | bytes 786436
Sparse Core Ops, SparseCore 0:
  115.4 34.3 all-reduce.2
where the time goes:
time: 816 us
  blocking collectives  654 us (80%)
  matrix products  85.6 us (10%)
  waiting for transfers between devices  42.2 us (5%)
  between operations  14.1 us (2%)
  starting transfers between devices  12.1 us (1%)
    psum x1, blocking collectives, on_device(): norm_new = lax.psum(jnp.sum(residual_next * residual_next, 1), 'blk')  330 us
    psum x1, blocking collectives, on_device(): curvature = lax.psum(local_curve, 'blk')  324 us
    dot_general x6, matrix products, matern(): lax.dot_general(left_pts, right_pts, (((0,), (0,)), ((), ())), precision=...  37.5 us
    psum x1, waiting for transfers between devices, on_device(): image = lax.psum(gained + placed, 'rep') + NOISE * direction  34.3 us
    dot_general x6, matrix products, apply_left(): lax.dot_general(vectors, kernel, (((1,), (1,)), ((), ())), precision=lax....  28.7 us
    dot_general x4, matrix products, apply_right(): return jnp.dot(vectors, kernel, precision=lax.Precision.HIGHEST)  19.5 us
  transfers between devices with their start and end apart: 4, of which 3 were waited for; matrix products, arithmetic and copies ran while one was open for 2% of the time, Pallas kernels for 0%

commit v1 on v0

v1 whole, which is shorter than its diff:
```python
import functools
import math

import jax
import jax.numpy as jnp
from jax import lax
from jax.experimental import pallas as pl
from jax.experimental.pallas import tpu as pltpu
from jax.sharding import PartitionSpec as P

F32, BF16 = jnp.float32, jnp.bfloat16
ROOT_FIVE = math.sqrt(5.0)
LOG2_E = 1.4426950408889634
NOISE = 0.5
BLOCK = 2048
DIM = 32
RHS = 32
TILE = 512
STEPS = BLOCK // TILE
DEPTH = 256
AXES = ("blk", "rep")
NT = (((1,), (1,)), ((), ()))


def pieces(value, count):
    out = []
    for _ in range(count):
        head = value.astype(BF16)
        out.append(head)
        value = value - head.astype(F32)
    return out


def norm_rows(points):
    return [part.astype(F32) for part in pieces(jnp.sum(points * points, 0, keepdims=True), 3)]


def left_side(points):
    n = points.shape[1]
    p = pieces(points, 3)
    m = norm_rows(points)
    row = lax.broadcasted_iota(jnp.int32, (16, n), 0)
    tail = jnp.where(row < 6, 1.0, 0.0)
    for i in range(3):
        tail = jnp.where(row == i, m[i], tail)
    rest = jnp.zeros((DEPTH - 6 * DIM - 16, n), BF16)
    return jnp.concatenate([p[0], p[0], p[1], p[1], p[0], p[2], tail.astype(BF16), rest], 0)


def right_side(points):
    n = points.shape[1]
    p = [(-2.0 * part.astype(F32)).astype(BF16) for part in pieces(points, 3)]
    m = norm_rows(points)
    row = lax.broadcasted_iota(jnp.int32, (16, n), 0)
    tail = jnp.where(row < 3, 1.0, 0.0)
    for i in range(3):
        tail = jnp.where(row == 3 + i, m[i], tail)
    rest = jnp.zeros((DEPTH - 6 * DIM - 16, n), BF16)
    return jnp.concatenate([p[0], p[1], p[0], p[1], p[2], p[0], tail.astype(BF16), rest], 0)


def both_pieces(vectors):
    return jnp.concatenate(pieces(vectors, 2), 0)


def matern_tile(left, right):
    sq = jnp.dot(left, right, preferred_element_type=F32)
    sq = jnp.maximum(sq, 1e-30)
    dist = sq * lax.rsqrt(sq)
    kernel = (dist * (dist + 3.0) + 3.0) * jnp.exp2(dist * -LOG2_E)
    head = kernel.astype(BF16)
    return head, (kernel - head.astype(F32)).astype(BF16)


def to_rows(vectors, kernel):
    return sum(lax.dot_general(vectors, k, NT, preferred_element_type=F32) for k in kernel)


def to_columns(vectors, kernel):
    return sum(jnp.dot(vectors, k, preferred_element_type=F32) for k in kernel)


def folded(total, scale):
    return (total[:RHS] + total[RHS:]) * scale


def own_kernel(pts_ref, len_ref, dir_ref, out_ref, left, right, vecs, total):
    points = pts_ref[...] * len_ref[...] * ROOT_FIVE
    left[...] = left_side(points).T
    right[...] = right_side(points)
    vecs[...] = both_pieces(dir_ref[...])
    total[...] = jnp.zeros_like(total)
    half = lax.axis_index("rep")

    def span(index):
        return pl.ds(pl.multiple_of(index * TILE, TILE), TILE)

    def pair(i, j):
        rows, cols = span(i), span(j)
        kernel = matern_tile(left[rows, :], right[:, cols])
        total[:, rows] += to_rows(vecs[:, cols], kernel)
        total[:, cols] += to_columns(vecs[:, rows], kernel)

    for k in range(STEPS // 2):
        i = half * (STEPS // 2) + k
        rows = span(i)
        kernel = matern_tile(left[rows, :], right[:, rows])
        total[:, rows] += to_columns(vecs[:, rows], kernel)
        pair(i, lax.rem(i + 1, STEPS))
    pair(half, half + STEPS // 2)
    out_ref[...] = folded(total[...], 4.0 / 3.0)


def cross_kernel(
    pts_ref, dir_ref, far_pts_ref, far_dir_ref, len_ref, diag_ref, own_ref, back_ref,
    left, right, vecs, far_vecs, own_total, back_total,
):
    scale = len_ref[...]
    left[...] = left_side(pts_ref[...] * scale * ROOT_FIVE).T
    right[...] = right_side(far_pts_ref[...] * scale * ROOT_FIVE)
    vecs[...] = both_pieces(dir_ref[...])
    far_vecs[...] = both_pieces(far_dir_ref[...])
    back_total[...] = jnp.zeros_like(back_total)

    def some_rows(position, carry):
        rows = pl.ds(pl.multiple_of(position * TILE, TILE), TILE)
        part = jnp.zeros((2 * RHS, TILE), F32)
        for c in range(STEPS):
            cols = slice(c * TILE, (c + 1) * TILE)
            kernel = matern_tile(left[rows, :], right[:, cols])
            part = part + to_rows(far_vecs[:, cols], kernel)
            back_total[:, cols] += to_columns(vecs[:, rows], kernel)
        own_total[:, rows] = part
        return carry

    lax.fori_loop(0, STEPS, some_rows, 0)
    own_ref[...] = folded(own_total[...], 1.0 / 3.0) + diag_ref[...]
    back_ref[...] = folded(back_total[...], 1.0 / 3.0)


def sums_kernel(own_ref, other_ref, dir_ref, res_ref, image_ref, sums_ref):
    vecs, res = dir_ref[...], res_ref[...]
    image = (own_ref[...] + other_ref[...]) + NOISE * vecs
    image_ref[...] = image
    lane = lax.broadcasted_iota(jnp.int32, (RHS, 128), 1)
    table = jnp.zeros((RHS, 128), F32)
    for i, (a, b) in enumerate(((res, res), (vecs, image), (res, image), (image, image))):
        table = jnp.where(lane == i, jnp.sum(a * b, 1, keepdims=True), table)
    table = jnp.concatenate([table, jnp.zeros((128 - RHS, 128), F32)], 0)
    sums_ref[...] = table.T[:8]


def update_kernel(sums_ref, active_ref, image_ref, dir_ref, res_ref, sol_ref, sol_out, res_out, dir_out):
    table = jnp.concatenate([sums_ref[...], jnp.zeros((120, 128), F32)], 0).T
    norm_old, curvature = table[:RHS, 0:1], table[:RHS, 1:2]
    res_image, image_image = table[:RHS, 2:3], table[:RHS, 3:4]
    active = active_ref[...]
    alpha = active.astype(F32) * norm_old / curvature
    norm_new = norm_old - 2.0 * alpha * res_image + alpha * alpha * image_image
    vecs = dir_ref[...]
    sol_out[...] = sol_ref[...] + alpha * vecs
    res_next = res_ref[...] - alpha * image_ref[...]
    res_out[...] = res_next
    dir_out[...] = jnp.where(active == 1, res_next + (norm_new / norm_old) * vecs, vecs)


def place(index):
    rep = index % 2
    core = index // 2 % 2
    x_hi = index // 4 % 2
    z = index // 8 % 8
    return index // 64, z, x_hi, core, rep


def index_of(y, z, x_hi, core, rep):
    return (((y % 4 * 8 + z % 8) * 2 + x_hi % 2) * 2 + core) * 2 + rep


def partner_pairs():
    pairs = []
    for index in range(256):
        block, rep = index // 2, index % 2
        if block % 2 == rep:
            pairs.append((index, (block + 32) % 128 * 2 + rep))
        else:
            pairs.append((index, (block - 33) % 128 * 2 + 1 - rep))
    return pairs


def moved(value, change):
    return lax.ppermute(value, AXES, [(i, index_of(*change(*place(i)))) for i in range(256)])


def all_blocks(value):
    value = value + moved(value, lambda y, z, x, c, r: (y, z, x, 1 - c, r))
    value = value + moved(value, lambda y, z, x, c, r: (y, z, 1 - x, c, 1 - r))
    for step in (1, 2, 4):
        value = value + moved(value, lambda y, z, x, c, r: (y, z ^ step, x, c, r))
    for step in (1, 2):
        value = value + moved(value, lambda y, z, x, c, r: (y ^ step, z, x, c, r))
    return value


def call(kernel, outs, scratch=(), name=None):
    vmem = pl.BlockSpec(memory_space=pltpu.VMEM)
    return pl.pallas_call(
        kernel,
        out_shape=tuple(jax.ShapeDtypeStruct(shape, F32) for shape in outs),
        out_specs=(vmem,) * len(outs),
        scratch_shapes=scratch,
        compiler_params=pltpu.CompilerParams(vmem_limit_bytes=40 * 2**20),
        name=name,
    )


def on_device(points, inv_length, direction, residual, solution, active):
    lengths = inv_length.reshape(DIM, 1)
    there = partner_pairs()
    far_pts = lax.ppermute(points, AXES, there)
    far_dir = lax.ppermute(direction, AXES, there)
    whole = (RHS, BLOCK)
    sides = [pltpu.VMEM((BLOCK, DEPTH), BF16), pltpu.VMEM((DEPTH, BLOCK), BF16)]
    two = pltpu.VMEM((2 * RHS, BLOCK), BF16)
    acc = pltpu.VMEM((2 * RHS, BLOCK), F32)
    (diag,) = call(own_kernel, [whole], sides + [two, acc], "own_tile")(points, lengths, direction)
    own, back = call(cross_kernel, [whole, whole], sides + [two, two, acc, acc], "cross_tile")(
        points, direction, far_pts, far_dir, lengths, diag
    )
    own = own + lax.ppermute(back, AXES, [(d, s) for s, d in there])
    other = moved(own, lambda y, z, x, c, r: (y, z, x, c, 1 - r))
    image, sums = call(sums_kernel, [whole, (8, 128)], name="sums")(own, other, direction, residual)
    sums = all_blocks(sums)
    return call(update_kernel, [whole] * 3, name="update")(
        sums, active.reshape(RHS, 1), image, direction, residual, solution
    )


def solution(mesh):
    placed = (P(None, "blk"), P(), P(None, "blk"), P(None, "blk"), P(None, "blk"), P())
    return jax.shard_map(
        on_device,
        mesh=mesh,
        in_specs=placed,
        out_specs=(P(None, "blk"), P(None, "blk"), P(None, "blk")),
        check_vma=False,
    )
```

time: 816 us -> 81 us (0.10)
  the two profiles are of different devices: /device:TPU:1 before, /device:TPU:16 now
where the time goes in v1:
time: 81 us; the launch traced here: 80.9 us
  waiting for transfers between devices  39.1 us (48%)
  Pallas kernels  21.4 us (26%)
  starting transfers between devices  17.5 us (22%)
  local copies, waits for them, and re-layouts  2.09 us (3%)
    ppermute x8, waiting for transfers between devices, moved(): lax.ppermute(value, AXES, [(i, index_of(*change(*place(i)))) for i in ran...  32.8 us
    pallas_call x1, Pallas kernels, on_device(): call(cross_kernel, [whole, whole], sides + [two, two, acc, acc], 'cross_t...  15.4 us
    ppermute x8, starting transfers between devices, moved(): lax.ppermute(value, AXES, [(i, index_of(*change(*place(i)))) for i in ran...  14 us
    ppermute x1, waiting for transfers between devices, on_device(): own = own + lax.ppermute(back, AXES, [(d, s) for s, d in there])  6.26 us
    pallas_call x1, Pallas kernels, on_device(): call(own_kernel, [whole], sides + [two, acc], 'own_tile')  4.65 us
    ppermute x1, starting transfers between devices, on_device(): far_dir = lax.ppermute(direction, AXES, there)  1.96 us
    unnamed x14, local copies, waits for them, and re-layouts  1.92 us
  transfers between devices with their start and end apart: 11, of which 9 were waited for; matrix products, arithmetic and copies ran while one was open for 0% of the time, Pallas kernels for 6%

profile of v1, /device:TPU:16, one launch (start us, length us, event | category | flops | bytes accessed | tf_op | source)
XLA Modules:
  0.0 80.9 jit_solution(16944187569150107286)
XLA Ops:
  0.6 1.4 %collective-permute-start = (f32[32,2048]{1,0:T(8,128)}, f32[32,2048]{1,0:T(8,128)S(1)}, u32[]{:S(2)}, u32[]{:S(2)}) collective-permute-start(f32[32,2048]{1,0:T(8,128)} %pts_ref.3), channel_id=1, source_target_pairs={{0,64},{1,190},{2,193},{3,67},{4,68},{5,194},{6,197},{7,71},{8,72}... | collective-permute-start | bytes 786440 | tf_op jit(solution)/shard_map/ppermute | solution.py:219
  2.0 2.0 %collective-permute-start.1 = (f32[32,2048]{1,0:T(8,128)}, f32[32,2048]{1,0:T(8,128)S(1)}, u32[]{:S(2)}, u32[]{:S(2)}) collective-permute-start(f32[32,2048]{1,0:T(8,128)} %dir_ref.7), channel_id=1, source_target_pairs={{0,64},{1,190},{2,193},{3,67},{4,68},{5,194},{6,197},{7,71},{8,72}... | collective-permute-start | bytes 786440 | tf_op jit(solution)/shard_map/ppermute | solution.py:220
  4.0 0.1 copy.10.len_ref
  4.1 0.9 %copy-done = f32[32,2048]{1,0:T(8,128)S(1)} copy-done((f32[32,2048]{1,0:T(8,128)S(1)}, f32[32,2048]{1,0:T(8,128)}, u32[]{:S(2)}) %copy-start) | copy-done | bytes 262168
  5.0 0.9 %copy-done.2 = f32[32,2048]{1,0:T(8,128)S(1)} copy-done((f32[32,2048]{1,0:T(8,128)S(1)}, f32[32,2048]{1,0:T(8,128)}, u32[]{:S(2)}) %copy-start.2) | copy-done | bytes 262168
  6.0 4.6 %own_tile.1.diag_ref = f32[32,2048]{1,0:T(8,128)S(1)} custom-call(f32[32,2048]{1,0:T(8,128)S(1)} %copy-done.2, f32[32,1]{1,0:T(8,128)S(1)} %copy.10.len_ref, f32[32,2048]{1,0:T(8,128)S(1)} %copy-done), custom_call_target="tpu_custom_call" | custom-call | tf_op jit(solution)/shard_map/own_tile/pallas_call | solution.py:225
  10.6 15.4 %cross_tile.1 = (f32[32,2048]{1,0:T(8,128)S(1)}, f32[32,2048]{1,0:T(8,128)S(1)}) custom-call(f32[32,2048]{1,0:T(8,128)S(1)} %copy-done.2, f32[32,2048]{1,0:T(8,128)S(1)} %copy-done, f32[32,2048]{1,0:T(8,128)S(1)} %collective-permute-done.far_pts_ref, f32[32,2048]{1,0:T(8,128)S(1)} %collective-permute-done.1.far_dir_ref, f32[32,1]{1,0:T(8,128)S(1)} %copy.10.len_ref, ...), custom_call_target="tpu_custom_call" | custom-call | tf_op jit(solution)/shard_map/cross_tile/pallas_call | solution.py:226
  26.0 0.2 collective-permute-start.2
  26.2 6.3 %collective-permute-done.2 = f32[32,2048]{1,0:T(8,128)S(1)} collective-permute-done((f32[32,2048]{1,0:T(8,128)S(1)}, f32[32,2048]{1,0:T(8,128)S(1)}, u32[]{:S(2)}, u32[]{:S(2)}) %collective-permute-start.2) | collective-permute-done | bytes 262176 | tf_op jit(solution)/shard_map/ppermute | solution.py:229
  32.5 12.2 %collective-permute-start.3 = (f32[32,2048]{1,0:T(8,128)S(1)}, f32[32,2048]{1,0:T(8,128)S(1)}, u32[]{:S(2)}, u32[]{:S(2)}) collective-permute-start(f32[32,2048]{1,0:T(8,128)S(1)} %add.24.own_ref), channel_id=1, source_target_pairs={{0,1},{1,0},{2,3},{3,2},{4,5},{5,4},{6,7},{7,6},{8,9},{9,8},{10,11... | collective-permute-start | bytes 786440 | tf_op jit(solution)/shard_map/ppermute | solution.py:191
  44.8 4.4 %collective-permute-done.3.other_ref = f32[32,2048]{1,0:T(8,128)S(1)} collective-permute-done((f32[32,2048]{1,0:T(8,128)S(1)}, f32[32,2048]{1,0:T(8,128)S(1)}, u32[]{:S(2)}, u32[]{:S(2)}) %collective-permute-start.3) | collective-permute-done | bytes 262176 | tf_op jit(solution)/shard_map/ppermute | solution.py:191
  49.1 0.2 sums.1
  49.3 0.0 collective-permute-start.4
  49.4 1.2 %collective-permute-done.4 = f32[8,128]{1,0:T(8,128)S(1)} collective-permute-done((f32[8,128]{1,0:T(8,128)S(1)}, f32[8,128]{1,0:T(8,128)S(1)}, u32[]{:S(2)}, u32[]{:S(2)}) %collective-permute-start.4) | collective-permute-done | bytes 4128 | tf_op jit(solution)/shard_map/ppermute | solution.py:191
  50.5 4.8 %collective-permute-done.5 = f32[8,128]{1,0:T(8,128)S(1)} collective-permute-done((f32[8,128]{1,0:T(8,128)S(1)}, f32[8,128]{1,0:T(8,128)S(1)}, u32[]{:S(2)}, u32[]{:S(2)}) %collective-permute-start.5) | collective-permute-done | bytes 4128 | tf_op jit(solution)/shard_map/ppermute | solution.py:191
  55.4 3.6 %collective-permute-done.6 = f32[8,128]{1,0:T(8,128)S(1)} collective-permute-done((f32[8,128]{1,0:T(8,128)S(1)}, f32[8,128]{1,0:T(8,128)S(1)}, u32[]{:S(2)}, u32[]{:S(2)}) %collective-permute-start.6) | collective-permute-done | bytes 4128 | tf_op jit(solution)/shard_map/ppermute | solution.py:191
  59.0 4.5 %collective-permute-done.7 = f32[8,128]{1,0:T(8,128)S(1)} collective-permute-done((f32[8,128]{1,0:T(8,128)S(1)}, f32[8,128]{1,0:T(8,128)S(1)}, u32[]{:S(2)}, u32[]{:S(2)}) %collective-permute-start.7) | collective-permute-done | bytes 4128 | tf_op jit(solution)/shard_map/ppermute | solution.py:191
  63.5 0.5 collective-permute-start.8
  64.0 7.0 %collective-permute-done.8 = f32[8,128]{1,0:T(8,128)S(1)} collective-permute-done((f32[8,128]{1,0:T(8,128)S(1)}, f32[8,128]{1,0:T(8,128)S(1)}, u32[]{:S(2)}, u32[]{:S(2)}) %collective-permute-start.8) | collective-permute-done | bytes 4128 | tf_op jit(solution)/shard_map/ppermute | solution.py:191
  71.0 3.6 %collective-permute-done.9 = f32[8,128]{1,0:T(8,128)S(1)} collective-permute-done((f32[8,128]{1,0:T(8,128)S(1)}, f32[8,128]{1,0:T(8,128)S(1)}, u32[]{:S(2)}, u32[]{:S(2)}) %collective-permute-start.9) | collective-permute-done | bytes 4128 | tf_op jit(solution)/shard_map/ppermute | solution.py:191
  74.6 1.3 %collective-permute-start.10 = (f32[8,128]{1,0:T(8,128)S(1)}, f32[8,128]{1,0:T(8,128)S(1)}, u32[]{:S(2)}, u32[]{:S(2)}) collective-permute-start(f32[8,128]{1,0:T(8,128)S(1)} %add.30), channel_id=1, source_target_pairs={{0,128},{1,129},{2,130},{3,131},{4,132},{5,133},{6,134},{7,135},{8... | collective-permute-start | bytes 12296 | tf_op jit(solution)/shard_map/ppermute | solution.py:191
  75.9 0.1 copy.11.active_ref
  76.0 3.7 %collective-permute-done.10 = f32[8,128]{1,0:T(8,128)S(1)} collective-permute-done((f32[8,128]{1,0:T(8,128)S(1)}, f32[8,128]{1,0:T(8,128)S(1)}, u32[]{:S(2)}, u32[]{:S(2)}) %collective-permute-start.10) | collective-permute-done | bytes 4128 | tf_op jit(solution)/shard_map/ppermute | solution.py:191
  79.7 1.1 %update.1 = (f32[32,2048]{1,0:T(8,128)}, f32[32,2048]{1,0:T(8,128)}, f32[32,2048]{1,0:T(8,128)}) custom-call(f32[8,128]{1,0:T(8,128)S(1)} %add.31.sums_ref, s32[32,1]{1,0:T(8,128)S(1)} %copy.11.active_ref, f32[32,2048]{1,0:T(8,128)S(1)} %get-tuple-element.10.image_ref, f32[32,2048]{1,0:T(8,128)S(1)} %copy-done.1, f32[32,2048]{1,0:T(8,128)S(1)} %copy-done.3, ...), custom_call_target="tpu_custom_call" | custom-call | tf_op jit(solution)/shard_map/update/pallas_call | solution.py:233
  (26 shorter events, 0.1 us)
Async XLA Ops:
  0.6 3.3 %copy-start.5 = (f32[32]{0:T(128)S(1)}, f32[32]{0:T(128)}, u32[]{:S(2)}) copy-start(f32[32]{0:T(128)} %param.7) | copy-start | bytes 388
  0.6 10.0 %collective-permute-start = (f32[32,2048]{1,0:T(8,128)}, f32[32,2048]{1,0:T(8,128)S(1)}, u32[]{:S(2)}, u32[]{:S(2)}) collective-permute-start(f32[32,2048]{1,0:T(8,128)} %pts_ref.3), channel_id=1, source_target_pairs={{0,64},{1,190},{2,193},{3,67},{4,68},{5,194},{6,197},{7,71},{8,72}... | collective-permute-start | bytes 786440 | tf_op jit(solution)/shard_map/ppermute | solution.py:219
  2.0 8.6 %collective-permute-start.1 = (f32[32,2048]{1,0:T(8,128)}, f32[32,2048]{1,0:T(8,128)S(1)}, u32[]{:S(2)}, u32[]{:S(2)}) collective-permute-start(f32[32,2048]{1,0:T(8,128)} %dir_ref.7), channel_id=1, source_target_pairs={{0,64},{1,190},{2,193},{3,67},{4,68},{5,194},{6,197},{7,71},{8,72}... | collective-permute-start | bytes 786440 | tf_op jit(solution)/shard_map/ppermute | solution.py:220
  4.0 1.0 %copy-start = (f32[32,2048]{1,0:T(8,128)S(1)}, f32[32,2048]{1,0:T(8,128)}, u32[]{:S(2)}) copy-start(f32[32,2048]{1,0:T(8,128)} %dir_ref.7) | copy-start | bytes 786436
  5.0 0.9 %copy-start.2 = (f32[32,2048]{1,0:T(8,128)S(1)}, f32[32,2048]{1,0:T(8,128)}, u32[]{:S(2)}) copy-start(f32[32,2048]{1,0:T(8,128)} %pts_ref.3) | copy-start | bytes 786436
  26.0 6.4 %collective-permute-start.2 = (f32[32,2048]{1,0:T(8,128)S(1)}, f32[32,2048]{1,0:T(8,128)S(1)}, u32[]{:S(2)}, u32[]{:S(2)}) collective-permute-start(f32[32,2048]{1,0:T(8,128)S(1)} %get-tuple-element.8), channel_id=1, source_target_pairs={{64,0},{190,1},{193,2},{67,3},{68,4},{194,5},{197,6},{71,7},{72,8}... | collective-permute-start | bytes 786440 | tf_op jit(solution)/shard_map/ppermute | solution.py:229
  32.5 16.6 %copy-start.1 = (f32[32,2048]{1,0:T(8,128)S(1)}, f32[32,2048]{1,0:T(8,128)}, u32[]{:S(2)}) copy-start(f32[32,2048]{1,0:T(8,128)} %dir_ref.7) | copy-start | bytes 786436
  32.5 16.6 %copy-start.3 = (f32[32,2048]{1,0:T(8,128)S(1)}, f32[32,2048]{1,0:T(8,128)}, u32[]{:S(2)}) copy-start(f32[32,2048]{1,0:T(8,128)} %res_ref.3) | copy-start | bytes 786436
  32.5 16.6 %collective-permute-start.3 = (f32[32,2048]{1,0:T(8,128)S(1)}, f32[32,2048]{1,0:T(8,128)S(1)}, u32[]{:S(2)}, u32[]{:S(2)}) collective-permute-start(f32[32,2048]{1,0:T(8,128)S(1)} %add.24.own_ref), channel_id=1, source_target_pairs={{0,1},{1,0},{2,3},{3,2},{4,5},{5,4},{6,7},{7,6},{8,9},{9,8},{10,11... | collective-permute-start | bytes 786440 | tf_op jit(solution)/shard_map/ppermute | solution.py:191
  49.1 30.6 %copy-start.4 = (f32[32,2048]{1,0:T(8,128)S(1)}, f32[32,2048]{1,0:T(8,128)}, u32[]{:S(2)}) copy-start(f32[32,2048]{1,0:T(8,128)} %sol_ref.1) | copy-start | bytes 786436
  49.3 1.2 %collective-permute-start.4 = (f32[8,128]{1,0:T(8,128)S(1)}, f32[8,128]{1,0:T(8,128)S(1)}, u32[]{:S(2)}, u32[]{:S(2)}) collective-permute-start(f32[8,128]{1,0:T(8,128)S(1)} %get-tuple-element.9), channel_id=1, source_target_pairs={{0,2},{1,3},{2,0},{3,1},{4,6},{5,7},{6,4},{7,5},{8,10},{9,11},{10,... | collective-permute-start | bytes 12296 | tf_op jit(solution)/shard_map/ppermute | solution.py:191
  50.5 4.8 %collective-permute-start.5 = (f32[8,128]{1,0:T(8,128)S(1)}, f32[8,128]{1,0:T(8,128)S(1)}, u32[]{:S(2)}, u32[]{:S(2)}) collective-permute-start(f32[8,128]{1,0:T(8,128)S(1)} %add.25), channel_id=1, source_target_pairs={{0,5},{1,4},{2,7},{3,6},{4,1},{5,0},{6,3},{7,2},{8,13},{9,12},{10,... | collective-permute-start | bytes 12296 | tf_op jit(solution)/shard_map/ppermute | solution.py:191
  55.4 3.6 %collective-permute-start.6 = (f32[8,128]{1,0:T(8,128)S(1)}, f32[8,128]{1,0:T(8,128)S(1)}, u32[]{:S(2)}, u32[]{:S(2)}) collective-permute-start(f32[8,128]{1,0:T(8,128)S(1)} %add.26), channel_id=1, source_target_pairs={{0,8},{1,9},{2,10},{3,11},{4,12},{5,13},{6,14},{7,15},{8,0},{9,1},... | collective-permute-start | bytes 12296 | tf_op jit(solution)/shard_map/ppermute | solution.py:191
  59.0 4.5 %collective-permute-start.7 = (f32[8,128]{1,0:T(8,128)S(1)}, f32[8,128]{1,0:T(8,128)S(1)}, u32[]{:S(2)}, u32[]{:S(2)}) collective-permute-start(f32[8,128]{1,0:T(8,128)S(1)} %add.27), channel_id=1, source_target_pairs={{0,16},{1,17},{2,18},{3,19},{4,20},{5,21},{6,22},{7,23},{8,24},{9,... | collective-permute-start | bytes 12296 | tf_op jit(solution)/shard_map/ppermute | solution.py:191
  63.5 7.5 %collective-permute-start.8 = (f32[8,128]{1,0:T(8,128)S(1)}, f32[8,128]{1,0:T(8,128)S(1)}, u32[]{:S(2)}, u32[]{:S(2)}) collective-permute-start(f32[8,128]{1,0:T(8,128)S(1)} %add.28), channel_id=1, source_target_pairs={{0,32},{1,33},{2,34},{3,35},{4,36},{5,37},{6,38},{7,39},{8,40},{9,... | collective-permute-start | bytes 12296 | tf_op jit(solution)/shard_map/ppermute | solution.py:191
  71.0 3.6 %collective-permute-start.9 = (f32[8,128]{1,0:T(8,128)S(1)}, f32[8,128]{1,0:T(8,128)S(1)}, u32[]{:S(2)}, u32[]{:S(2)}) collective-permute-start(f32[8,128]{1,0:T(8,128)S(1)} %add.29), channel_id=1, source_target_pairs={{0,64},{1,65},{2,66},{3,67},{4,68},{5,69},{6,70},{7,71},{8,72},{9,... | collective-permute-start | bytes 12296 | tf_op jit(solution)/shard_map/ppermute | solution.py:191
  74.6 1.3 %copy-start.6 = (s32[32]{0:T(128)S(1)}, s32[32]{0:T(128)}, u32[]{:S(2)}) copy-start(s32[32]{0:T(128)} %param.11) | copy-start | bytes 388
  74.6 5.1 %collective-permute-start.10 = (f32[8,128]{1,0:T(8,128)S(1)}, f32[8,128]{1,0:T(8,128)S(1)}, u32[]{:S(2)}, u32[]{:S(2)}) collective-permute-start(f32[8,128]{1,0:T(8,128)S(1)} %add.30), channel_id=1, source_target_pairs={{0,128},{1,129},{2,130},{3,131},{4,132},{5,133},{6,134},{7,135},{8... | collective-permute-start | bytes 12296 | tf_op jit(solution)/shard_map/ppermute | solution.py:191

commit v2 on v1

--- a/solution.py
+++ b/solution.py
@@ -84,13 +84,18 @@
     return (total[:RHS] + total[RHS:]) * scale
 
 
-def own_kernel(pts_ref, len_ref, dir_ref, out_ref, left, right, vecs, total):
-    points = pts_ref[...] * len_ref[...] * ROOT_FIVE
+def handles_own_block():
+    return lax.rem(lax.axis_index("blk"), 2) == lax.axis_index("rep")
+
+
+def own_kernel(pts_ref, swap_pts_ref, len_ref, dir_ref, swap_dir_ref, out_ref, left, vecs, right, total):
+    mine = handles_own_block()
+    points = jnp.where(mine, pts_ref[...], swap_pts_ref[...]) * len_ref[...] * ROOT_FIVE
     left[...] = left_side(points).T
     right[...] = right_side(points)
-    vecs[...] = both_pieces(dir_ref[...])
+    vecs[...] = both_pieces(jnp.where(mine, dir_ref[...], swap_dir_ref[...]))
     total[...] = jnp.zeros_like(total)
-    half = lax.axis_index("rep")
+    half = lax.rem(lax.axis_index("blk"), 2)
 
     def span(index):
         return pl.ds(pl.multiple_of(index * TILE, TILE), TILE)
@@ -112,13 +117,10 @@
 
 
 def cross_kernel(
-    pts_ref, dir_ref, far_pts_ref, far_dir_ref, len_ref, diag_ref, own_ref, back_ref,
-    left, right, vecs, far_vecs, own_total, back_total,
+    left, vecs, far_pts_ref, far_dir_ref, len_ref, diag_ref, own_ref, back_ref,
+    right, far_vecs, own_total, back_total,
 ):
-    scale = len_ref[...]
-    left[...] = left_side(pts_ref[...] * scale * ROOT_FIVE).T
-    right[...] = right_side(far_pts_ref[...] * scale * ROOT_FIVE)
-    vecs[...] = both_pieces(dir_ref[...])
+    right[...] = right_side(far_pts_ref[...] * len_ref[...] * ROOT_FIVE)
     far_vecs[...] = both_pieces(far_dir_ref[...])
     back_total[...] = jnp.zeros_like(back_total)
 
@@ -140,72 +142,89 @@
 
 def sums_kernel(own_ref, other_ref, dir_ref, res_ref, image_ref, sums_ref):
     vecs, res = dir_ref[...], res_ref[...]
-    image = (own_ref[...] + other_ref[...]) + NOISE * vecs
-    image_ref[...] = image
+    product = own_ref[...] + other_ref[...]
+    image_ref[...] = product
+    image = product + NOISE * vecs
     lane = lax.broadcasted_iota(jnp.int32, (RHS, 128), 1)
     table = jnp.zeros((RHS, 128), F32)
     for i, (a, b) in enumerate(((res, res), (vecs, image), (res, image), (image, image))):
         table = jnp.where(lane == i, jnp.sum(a * b, 1, keepdims=True), table)
+    table = jnp.where(handles_own_block(), table, 0.0)
     table = jnp.concatenate([table, jnp.zeros((128 - RHS, 128), F32)], 0)
     sums_ref[...] = table.T[:8]
 
 
-def update_kernel(sums_ref, active_ref, image_ref, dir_ref, res_ref, sol_ref, sol_out, res_out, dir_out):
-    table = jnp.concatenate([sums_ref[...], jnp.zeros((120, 128), F32)], 0).T
+def update_kernel(
+    sums_ref, active_ref, image_ref, other_ref, dir_ref, res_ref, sol_ref, sol_out, res_out, dir_out
+):
+    table = sums_ref[0]
+    for i in range(1, sums_ref.shape[0]):
+        table = table + sums_ref[i]
+    table = jnp.concatenate([table, jnp.zeros((120, 128), F32)], 0).T
     norm_old, curvature = table[:RHS, 0:1], table[:RHS, 1:2]
     res_image, image_image = table[:RHS, 2:3], table[:RHS, 3:4]
     active = active_ref[...]
     alpha = active.astype(F32) * norm_old / curvature
     norm_new = norm_old - 2.0 * alpha * res_image + alpha * alpha * image_image
     vecs = dir_ref[...]
+    image = jnp.where(handles_own_block(), image_ref[...], other_ref[...]) + NOISE * vecs
     sol_out[...] = sol_ref[...] + alpha * vecs
-    res_next = res_ref[...] - alpha * image_ref[...]
+    res_next = res_ref[...] - alpha * image
     res_out[...] = res_next
     dir_out[...] = jnp.where(active == 1, res_next + (norm_new / norm_old) * vecs, vecs)
 
 
-def place(index):
-    rep = index % 2
-    core = index // 2 % 2
-    x_hi = index // 4 % 2
-    z = index // 8 % 8
-    return index // 64, z, x_hi, core, rep
-
-
-def index_of(y, z, x_hi, core, rep):
-    return (((y % 4 * 8 + z % 8) * 2 + x_hi % 2) * 2 + core) * 2 + rep
-
-
-def partner_pairs():
+def permuted(value, change):
     pairs = []
     for index in range(256):
         block, rep = index // 2, index % 2
-        if block % 2 == rep:
-            pairs.append((index, (block + 32) % 128 * 2 + rep))
-        else:
-            pairs.append((index, (block - 33) % 128 * 2 + 1 - rep))
-    return pairs
-
-
-def moved(value, change):
-    return lax.ppermute(value, AXES, [(i, index_of(*change(*place(i)))) for i in range(256)])
-
-
-def all_blocks(value):
-    value = value + moved(value, lambda y, z, x, c, r: (y, z, x, 1 - c, r))
-    value = value + moved(value, lambda y, z, x, c, r: (y, z, 1 - x, c, 1 - r))
-    for step in (1, 2, 4):
-        value = value + moved(value, lambda y, z, x, c, r: (y, z ^ step, x, c, r))
-    for step in (1, 2):
-        value = value + moved(value, lambda y, z, x, c, r: (y ^ step, z, x, c, r))
-    return value
+        to = change(block, block % 2, rep)
+        if to is not None:
+            pairs.append((index, to[0] % 128 * 2 + to[1]))
+    return lax.ppermute(value, AXES, pairs)
+
+
+def to_partner(block, core, rep):
+    if core == rep:
+        return block + 32, rep
+    return block - 32 - 2 * rep, rep
+
+
+def to_home(block, core, rep):
+    if core == rep:
+        return block - 32, rep
+    return block + 31 + 4 * rep, 1 - rep
+
+
+def swap_core(block, core, rep):
+    return block ^ 1, rep
+
+
+def swap_rep(block, core, rep):
+    return block, 1 - rep
+
+
+def swap_near(block, core, rep):
+    return block ^ 2, 1 - rep
+
+
+def to_twin(block, core, rep):
+    return (block, 1 - rep) if core == rep else None
+
+
+def over_y_and_z(value):
+    groups = []
+    for low in range(8):
+        groups.append([high * 8 + low for high in range(32)])
+    copies = jnp.broadcast_to(value[None], (32,) + value.shape)
+    return lax.all_to_all(copies, AXES, 0, 0, axis_index_groups=groups)
 
 
 def call(kernel, outs, scratch=(), name=None):
     vmem = pl.BlockSpec(memory_space=pltpu.VMEM)
     return pl.pallas_call(
         kernel,
-        out_shape=tuple(jax.ShapeDtypeStruct(shape, F32) for shape in outs),
+        out_shape=tuple(jax.ShapeDtypeStruct(*(out if isinstance(out[0], tuple) else (out, F32))) for out in outs),
         out_specs=(vmem,) * len(outs),
         scratch_shapes=scratch,
         compiler_params=pltpu.CompilerParams(vmem_limit_bytes=40 * 2**20),
@@ -215,23 +234,28 @@
 
 def on_device(points, inv_length, direction, residual, solution, active):
     lengths = inv_length.reshape(DIM, 1)
-    there = partner_pairs()
-    far_pts = lax.ppermute(points, AXES, there)
-    far_dir = lax.ppermute(direction, AXES, there)
+    far_pts = permuted(points, to_partner)
+    far_dir = permuted(direction, to_partner)
+    swap_pts = permuted(points, swap_core)
+    swap_dir = permuted(direction, swap_core)
     whole = (RHS, BLOCK)
-    sides = [pltpu.VMEM((BLOCK, DEPTH), BF16), pltpu.VMEM((DEPTH, BLOCK), BF16)]
+    side = pltpu.VMEM((DEPTH, BLOCK), BF16)
     two = pltpu.VMEM((2 * RHS, BLOCK), BF16)
     acc = pltpu.VMEM((2 * RHS, BLOCK), F32)
-    (diag,) = call(own_kernel, [whole], sides + [two, acc], "own_tile")(points, lengths, direction)
-    own, back = call(cross_kernel, [whole, whole], sides + [two, two, acc, acc], "cross_tile")(
-        points, direction, far_pts, far_dir, lengths, diag
-    )
-    own = own + lax.ppermute(back, AXES, [(d, s) for s, d in there])
-    other = moved(own, lambda y, z, x, c, r: (y, z, x, c, 1 - r))
-    image, sums = call(sums_kernel, [whole, (8, 128)], name="sums")(own, other, direction, residual)
-    sums = all_blocks(sums)
+    diag, left, vecs = call(
+        own_kernel, [whole, ((BLOCK, DEPTH), BF16), ((2 * RHS, BLOCK), BF16)], [side, acc], "own_tile"
+    )(points, swap_pts, lengths, direction, swap_dir)
+    own, back = call(cross_kernel, [whole, whole], [side, two, acc, acc], "cross_tile")(
+        left, vecs, far_pts, far_dir, lengths, diag
+    )
+    own = own + permuted(back, to_home)
+    other = permuted(own, swap_core)
+    product, sums = call(sums_kernel, [whole, (8, 128)], name="sums")(own, other, direction, residual)
+    for change in (swap_core, swap_rep, swap_near):
+        sums = sums + permuted(sums, change)
+    twin = permuted(product, to_twin)
     return call(update_kernel, [whole] * 3, name="update")(
-        sums, active.reshape(RHS, 1), image, direction, residual, solution
+        over_y_and_z(sums), active.reshape(RHS, 1), product, twin, direction, residual, solution
     )
 
 

time: 81 us -> 73.9 us (0.912)
  the two profiles are of different devices: /device:TPU:16 before, /device:TPU:32 now
where the time goes in v2:
time: 73.9 us; the launch traced here: 73.7 us
  starting transfers between devices  27.1 us (37%)
  Pallas kernels  21.3 us (29%)
  waiting for transfers between devices  21.2 us (29%)
  local copies, waits for them, and re-layouts  3.4 us (5%)
  between operations  0.74 us (1%)
    ppermute x10, starting transfers between devices, permuted(): return lax.ppermute(value, AXES, pairs)  17.6 us
    pallas_call x1, Pallas kernels, on_device(): call(cross_kernel, [whole, whole], [side, two, acc, acc], 'cross_tile')  15.2 us
    ppermute x10, waiting for transfers between devices, permuted(): return lax.ppermute(value, AXES, pairs)  12.1 us
    all_to_all x1, starting transfers between devices, over_y_and_z(): return lax.all_to_all(copies, AXES, 0, 0, axis_index_groups=groups)  9.48 us
    all_to_all x1, waiting for transfers between devices, over_y_and_z(): return lax.all_to_all(copies, AXES, 0, 0, axis_index_groups=groups)  9.03 us
    pallas_call x1, Pallas kernels, on_device(): call(own_kernel, [whole, ((BLOCK, DEPTH), BF16), ((2 * RHS, BLOCK), BF16)...  4.67 us
    unnamed x14, local copies, waits for them, and re-layouts  2.56 us
  transfers between devices with their start and end apart: 11, of which 6 were waited for; matrix products, arithmetic and copies ran while one was open for 1% of the time, Pallas kernels for 6%

profile of v2, /device:TPU:32, one launch (start us, length us, event | category | flops | bytes accessed | tf_op | source)
XLA Modules:
  0.0 73.7 jit_solution(9677146799164877301)
XLA Ops:
  0.6 0.1 collective-permute-start
  0.7 0.5 collective-permute-start.1
  1.2 1.6 %collective-permute-start.2 = (f32[32,2048]{1,0:T(8,128)}, f32[32,2048]{1,0:T(8,128)S(1)}, u32[]{:S(2)}, u32[]{:S(2)}) collective-permute-start(f32[32,2048]{1,0:T(8,128)} %pts_ref.1), channel_id=1, source_target_pairs={{0,64},{1,189},{2,194},{3,67},{4,68},{5,193},{6,198},{7,71},{8,72}... | collective-permute-start | bytes 786440 | tf_op jit(solution)/shard_map/ppermute | solution.py:184
  2.8 1.6 %collective-permute-start.3 = (f32[32,2048]{1,0:T(8,128)}, f32[32,2048]{1,0:T(8,128)S(1)}, u32[]{:S(2)}, u32[]{:S(2)}) collective-permute-start(f32[32,2048]{1,0:T(8,128)} %dir_ref.5), channel_id=1, source_target_pairs={{0,64},{1,189},{2,194},{3,67},{4,68},{5,193},{6,198},{7,71},{8,72}... | collective-permute-start | bytes 786440 | tf_op jit(solution)/shard_map/ppermute | solution.py:184
  4.5 0.9 %copy-done = f32[32,2048]{1,0:T(8,128)S(1)} copy-done((f32[32,2048]{1,0:T(8,128)S(1)}, f32[32,2048]{1,0:T(8,128)}, u32[]{:S(2)}) %copy-start) | copy-done | bytes 262168
  5.4 0.9 %copy-done.3 = f32[32,2048]{1,0:T(8,128)S(1)} copy-done((f32[32,2048]{1,0:T(8,128)S(1)}, f32[32,2048]{1,0:T(8,128)}, u32[]{:S(2)}) %copy-start.3) | copy-done | bytes 262168
  6.4 4.7 %own_tile.1 = (f32[32,2048]{1,0:T(8,128)S(1)}, bf16[2048,256]{1,0:T(8,128)(2,1)S(1)}, bf16[64,2048]{1,0:T(8,128)(2,1)S(1)}) custom-call(f32[32,2048]{1,0:T(8,128)S(1)} %copy-done.3, f32[32,2048]{1,0:T(8,128)S(1)} %collective-permute-done.swap_pts_ref, f32[32,1]{1,0:T(8,128)S(1)} %copy.9.len_ref, f32[32,2048]{1,0:T(8,128)S(1)} %copy-done, ...), custom_call_target="tpu_custom_call" | custom-call | tf_op jit(solution)/shard_map/own_tile/pallas_call | solution.py:245
  11.1 0.8 %collective-permute-done.3.far_dir_ref = f32[32,2048]{1,0:T(8,128)S(1)} collective-permute-done((f32[32,2048]{1,0:T(8,128)}, f32[32,2048]{1,0:T(8,128)S(1)}, u32[]{:S(2)}, u32[]{:S(2)}) %collective-permute-start.3) | collective-permute-done | bytes 262176 | tf_op jit(solution)/shard_map/ppermute | solution.py:184
  11.8 15.2 %cross_tile.1 = (f32[32,2048]{1,0:T(8,128)S(1)}, f32[32,2048]{1,0:T(8,128)S(1)}) custom-call(bf16[2048,256]{1,0:T(8,128)(2,1)S(1)} %get-tuple-element.10.left, bf16[64,2048]{1,0:T(8,128)(2,1)S(1)} %get-tuple-element.11.vecs, f32[32,2048]{1,0:T(8,128)S(1)} %collective-permute-done.2.far_pts_ref, f32[32,2048]{1,0:T(8,128)S(1)} %collective-permute-done.3.far_dir_ref, ...), custom_call_target="tpu_custom_call" | custom-call | tf_op jit(solution)/shard_map/cross_tile/pallas_call | solution.py:248
  27.0 1.9 %collective-permute-start.4 = (f32[32,2048]{1,0:T(8,128)S(1)}, f32[32,2048]{1,0:T(8,128)S(1)}, u32[]{:S(2)}, u32[]{:S(2)}) collective-permute-start(f32[32,2048]{1,0:T(8,128)S(1)} %get-tuple-element.14), channel_id=1, source_target_pairs={{0,192},{1,70},{2,65},{3,195},{4,196},{5,74},{6,69},{7,199},{8,200... | collective-permute-start | bytes 786440 | tf_op jit(solution)/shard_map/ppermute | solution.py:184
  28.9 4.6 %collective-permute-done.4 = f32[32,2048]{1,0:T(8,128)S(1)} collective-permute-done((f32[32,2048]{1,0:T(8,128)S(1)}, f32[32,2048]{1,0:T(8,128)S(1)}, u32[]{:S(2)}, u32[]{:S(2)}) %collective-permute-start.4) | collective-permute-done | bytes 262176 | tf_op jit(solution)/shard_map/ppermute | solution.py:184
  33.5 7.5 %collective-permute-start.5 = (f32[32,2048]{1,0:T(8,128)S(1)}, f32[32,2048]{1,0:T(8,128)S(1)}, u32[]{:S(2)}, u32[]{:S(2)}) collective-permute-start(f32[32,2048]{1,0:T(8,128)S(1)} %add.12.own_ref), channel_id=1, source_target_pairs={{0,2},{1,3},{2,0},{3,1},{4,6},{5,7},{6,4},{7,5},{8,10},{9,11},{10,... | collective-permute-start | bytes 786440 | tf_op jit(solution)/shard_map/ppermute | solution.py:184
  41.0 1.2 %collective-permute-done.5.other_ref = f32[32,2048]{1,0:T(8,128)S(1)} collective-permute-done((f32[32,2048]{1,0:T(8,128)S(1)}, f32[32,2048]{1,0:T(8,128)S(1)}, u32[]{:S(2)}, u32[]{:S(2)}) %collective-permute-start.5) | collective-permute-done | bytes 262176 | tf_op jit(solution)/shard_map/ppermute | solution.py:184
  42.2 0.2 sums.1
  42.4 0.4 collective-permute-start.6
  42.9 0.8 %collective-permute-done.6 = f32[8,128]{1,0:T(8,128)S(1)} collective-permute-done((f32[8,128]{1,0:T(8,128)S(1)}, f32[8,128]{1,0:T(8,128)S(1)}, u32[]{:S(2)}, u32[]{:S(2)}) %collective-permute-start.6) | collective-permute-done | bytes 4128 | tf_op jit(solution)/shard_map/ppermute | solution.py:184
  43.7 3.9 %collective-permute-start.9 = (f32[32,2048]{1,0:T(8,128)S(1)}, f32[32,2048]{1,0:T(8,128)S(1)}, u32[]{:S(2)}, u32[]{:S(2)}) collective-permute-start(f32[32,2048]{1,0:T(8,128)S(1)} %get-tuple-element.16.image_ref), channel_id=1, source_target_pairs={{0,1},{3,2},{4,5},{7,6},{8,9},{11,10},{12,13},{15,14},{16,17},{19,... | collective-permute-start | bytes 786440 | tf_op jit(solution)/shard_map/ppermute | solution.py:184
  47.7 0.1 collective-permute-start.8
  47.8 4.8 %collective-permute-done.8 = f32[8,128]{1,0:T(8,128)S(1)} collective-permute-done((f32[8,128]{1,0:T(8,128)S(1)}, f32[8,128]{1,0:T(8,128)S(1)}, u32[]{:S(2)}, u32[]{:S(2)}) %collective-permute-start.8) | collective-permute-done | bytes 4128 | tf_op jit(solution)/shard_map/ppermute | solution.py:184
  52.6 0.7 broadcast_in_dim.2
  53.2 9.5 %all-to-all-start = ((f32[32,8,128]{2,1,0:T(8,128)}), f32[32,8,128]{2,1,0:T(8,128)S(1)}, u32[]{:S(2)}, u32[]{:S(2)}) async-start(f32[32,8,128]{2,1,0:T(8,128)} %broadcast_in_dim.2), calls=%async_computation | async-start | bytes 262144 | tf_op jit(solution)/shard_map/all_to_all | solution.py:220
  62.7 0.6 copy-done.6
  63.5 9.0 %all-to-all-done.sums_ref = f32[32,8,128]{2,1,0:T(8,128)S(1)} async-done(((f32[32,8,128]{2,1,0:T(8,128)}), f32[32,8,128]{2,1,0:T(8,128)S(1)}, u32[]{:S(2)}, u32[]{:S(2)}) %all-to-all-start) | async-done | bytes 131104 | tf_op jit(solution)/shard_map/all_to_all | solution.py:220
  72.5 1.2 %update.1 = (f32[32,2048]{1,0:T(8,128)}, f32[32,2048]{1,0:T(8,128)}, f32[32,2048]{1,0:T(8,128)}) custom-call(f32[32,8,128]{2,1,0:T(8,128)S(1)} %all-to-all-done.sums_ref, s32[32,1]{1,0:T(8,128)S(1)} %copy.11.active_ref, f32[32,2048]{1,0:T(8,128)S(1)} %get-tuple-element.16.image_ref, f32[32,2048]{1,0:T(8,128)S(1)} %collective-permute-done.9.other_ref, ...), custom_call_target="tpu_custom_call" | custom-call | tf_op jit(solution)/shard_map/update/pallas_call | solution.py:257
  (23 shorter events, 0.3 us)
Async XLA Ops:
  0.6 3.8 %copy-start.5 = (f32[32]{0:T(128)S(1)}, f32[32]{0:T(128)}, u32[]{:S(2)}) copy-start(f32[32]{0:T(128)} %param.7) | copy-start | bytes 388
  0.6 3.8 %collective-permute-start = (f32[32,2048]{1,0:T(8,128)}, f32[32,2048]{1,0:T(8,128)S(1)}, u32[]{:S(2)}, u32[]{:S(2)}) collective-permute-start(f32[32,2048]{1,0:T(8,128)} %pts_ref.1), channel_id=1, source_target_pairs={{0,2},{1,3},{2,0},{3,1},{4,6},{5,7},{6,4},{7,5},{8,10},{9,11},{10,... | collective-permute-start | bytes 786440 | tf_op jit(solution)/shard_map/ppermute | solution.py:184
  0.7 3.7 %collective-permute-start.1 = (f32[32,2048]{1,0:T(8,128)}, f32[32,2048]{1,0:T(8,128)S(1)}, u32[]{:S(2)}, u32[]{:S(2)}) collective-permute-start(f32[32,2048]{1,0:T(8,128)} %dir_ref.5), channel_id=1, source_target_pairs={{0,2},{1,3},{2,0},{3,1},{4,6},{5,7},{6,4},{7,5},{8,10},{9,11},{10,... | collective-permute-start | bytes 786440 | tf_op jit(solution)/shard_map/ppermute | solution.py:184
  1.2 9.8 %collective-permute-start.2 = (f32[32,2048]{1,0:T(8,128)}, f32[32,2048]{1,0:T(8,128)S(1)}, u32[]{:S(2)}, u32[]{:S(2)}) collective-permute-start(f32[32,2048]{1,0:T(8,128)} %pts_ref.1), channel_id=1, source_target_pairs={{0,64},{1,189},{2,194},{3,67},{4,68},{5,193},{6,198},{7,71},{8,72}... | collective-permute-start | bytes 786440 | tf_op jit(solution)/shard_map/ppermute | solution.py:184
  2.8 9.0 %collective-permute-start.3 = (f32[32,2048]{1,0:T(8,128)}, f32[32,2048]{1,0:T(8,128)S(1)}, u32[]{:S(2)}, u32[]{:S(2)}) collective-permute-start(f32[32,2048]{1,0:T(8,128)} %dir_ref.5), channel_id=1, source_target_pairs={{0,64},{1,189},{2,194},{3,67},{4,68},{5,193},{6,198},{7,71},{8,72}... | collective-permute-start | bytes 786440 | tf_op jit(solution)/shard_map/ppermute | solution.py:184
  4.5 1.0 %copy-start = (f32[32,2048]{1,0:T(8,128)S(1)}, f32[32,2048]{1,0:T(8,128)}, u32[]{:S(2)}) copy-start(f32[32,2048]{1,0:T(8,128)} %dir_ref.5) | copy-start | bytes 786436
  5.4 0.9 %copy-start.3 = (f32[32,2048]{1,0:T(8,128)S(1)}, f32[32,2048]{1,0:T(8,128)}, u32[]{:S(2)}) copy-start(f32[32,2048]{1,0:T(8,128)} %pts_ref.1) | copy-start | bytes 786436
  27.0 6.4 %collective-permute-start.4 = (f32[32,2048]{1,0:T(8,128)S(1)}, f32[32,2048]{1,0:T(8,128)S(1)}, u32[]{:S(2)}, u32[]{:S(2)}) collective-permute-start(f32[32,2048]{1,0:T(8,128)S(1)} %get-tuple-element.14), channel_id=1, source_target_pairs={{0,192},{1,70},{2,65},{3,195},{4,196},{5,74},{6,69},{7,199},{8,200... | collective-permute-start | bytes 786440 | tf_op jit(solution)/shard_map/ppermute | solution.py:184
  33.5 8.7 %copy-start.1 = (f32[32,2048]{1,0:T(8,128)S(1)}, f32[32,2048]{1,0:T(8,128)}, u32[]{:S(2)}) copy-start(f32[32,2048]{1,0:T(8,128)} %dir_ref.5) | copy-start | bytes 786436
  33.5 8.7 %copy-start.2 = (f32[32,2048]{1,0:T(8,128)S(1)}, f32[32,2048]{1,0:T(8,128)}, u32[]{:S(2)}) copy-start(f32[32,2048]{1,0:T(8,128)} %res_ref.3) | copy-start | bytes 786436
  33.5 8.7 %collective-permute-start.5 = (f32[32,2048]{1,0:T(8,128)S(1)}, f32[32,2048]{1,0:T(8,128)S(1)}, u32[]{:S(2)}, u32[]{:S(2)}) collective-permute-start(f32[32,2048]{1,0:T(8,128)S(1)} %add.12.own_ref), channel_id=1, source_target_pairs={{0,2},{1,3},{2,0},{3,1},{4,6},{5,7},{6,4},{7,5},{8,10},{9,11},{10,... | collective-permute-start | bytes 786440 | tf_op jit(solution)/shard_map/ppermute | solution.py:184
  42.4 30.1 %copy-start.4 = (f32[32,2048]{1,0:T(8,128)S(1)}, f32[32,2048]{1,0:T(8,128)}, u32[]{:S(2)}) copy-start(f32[32,2048]{1,0:T(8,128)} %sol_ref.1) | copy-start | bytes 786436
  42.4 1.2 %collective-permute-start.6 = (f32[8,128]{1,0:T(8,128)S(1)}, f32[8,128]{1,0:T(8,128)S(1)}, u32[]{:S(2)}, u32[]{:S(2)}) collective-permute-start(f32[8,128]{1,0:T(8,128)S(1)} %get-tuple-element.15), channel_id=1, source_target_pairs={{0,2},{1,3},{2,0},{3,1},{4,6},{5,7},{6,4},{7,5},{8,10},{9,11},{10,... | collective-permute-start | bytes 12296 | tf_op jit(solution)/shard_map/ppermute | solution.py:184
  43.7 3.9 %collective-permute-start.7 = (f32[8,128]{1,0:T(8,128)S(1)}, f32[8,128]{1,0:T(8,128)S(1)}, u32[]{:S(2)}, u32[]{:S(2)}) collective-permute-start(f32[8,128]{1,0:T(8,128)S(1)} %add.13), channel_id=1, source_target_pairs={{0,1},{1,0},{2,3},{3,2},{4,5},{5,4},{6,7},{7,6},{8,9},{9,8},{10,11... | collective-permute-start | bytes 12296 | tf_op jit(solution)/shard_map/ppermute | solution.py:184
  43.7 19.8 %collective-permute-start.9 = (f32[32,2048]{1,0:T(8,128)S(1)}, f32[32,2048]{1,0:T(8,128)S(1)}, u32[]{:S(2)}, u32[]{:S(2)}) collective-permute-start(f32[32,2048]{1,0:T(8,128)S(1)} %get-tuple-element.16.image_ref), channel_id=1, source_target_pairs={{0,1},{3,2},{4,5},{7,6},{8,9},{11,10},{12,13},{15,14},{16,17},{19,... | collective-permute-start | bytes 786440 | tf_op jit(solution)/shard_map/ppermute | solution.py:184
  47.7 4.9 %collective-permute-start.8 = (f32[8,128]{1,0:T(8,128)S(1)}, f32[8,128]{1,0:T(8,128)S(1)}, u32[]{:S(2)}, u32[]{:S(2)}) collective-permute-start(f32[8,128]{1,0:T(8,128)S(1)} %add.14), channel_id=1, source_target_pairs={{0,5},{1,4},{2,7},{3,6},{4,1},{5,0},{6,3},{7,2},{8,13},{9,12},{10,... | collective-permute-start | bytes 12296 | tf_op jit(solution)/shard_map/ppermute | solution.py:184
  53.2 19.3 %all-to-all-start = ((f32[32,8,128]{2,1,0:T(8,128)}), f32[32,8,128]{2,1,0:T(8,128)S(1)}, u32[]{:S(2)}, u32[]{:S(2)}) async-start(f32[32,8,128]{2,1,0:T(8,128)} %broadcast_in_dim.2), calls=%async_computation | async-start | bytes 262144 | tf_op jit(solution)/shard_map/all_to_all | solution.py:220
  62.7 0.7 copy-start.6

commit v3 on v2

--- a/solution.py
+++ b/solution.py
@@ -116,50 +116,65 @@
     out_ref[...] = folded(total[...], 4.0 / 3.0)
 
 
-def cross_kernel(
-    left, vecs, far_pts_ref, far_dir_ref, len_ref, diag_ref, own_ref, back_ref,
-    right, far_vecs, own_total, back_total,
-):
+def kernel_kernel(left, vecs, far_pts_ref, len_ref, back_ref, head_ref, rest_ref, right, back_total):
     right[...] = right_side(far_pts_ref[...] * len_ref[...] * ROOT_FIVE)
-    far_vecs[...] = both_pieces(far_dir_ref[...])
     back_total[...] = jnp.zeros_like(back_total)
 
     def some_rows(position, carry):
         rows = pl.ds(pl.multiple_of(position * TILE, TILE), TILE)
-        part = jnp.zeros((2 * RHS, TILE), F32)
         for c in range(STEPS):
             cols = slice(c * TILE, (c + 1) * TILE)
-            kernel = matern_tile(left[rows, :], right[:, cols])
-            part = part + to_rows(far_vecs[:, cols], kernel)
-            back_total[:, cols] += to_columns(vecs[:, rows], kernel)
-        own_total[:, rows] = part
+            head, rest = matern_tile(left[rows, :], right[:, cols])
+            head_ref[rows, cols] = head
+            rest_ref[rows, cols] = rest
+            back_total[:, cols] += jnp.dot(vecs[:, rows], head, preferred_element_type=F32)
+            back_total[:RHS, cols] += jnp.dot(vecs[:RHS, rows], rest, preferred_element_type=F32)
         return carry
 
     lax.fori_loop(0, STEPS, some_rows, 0)
-    own_ref[...] = folded(own_total[...], 1.0 / 3.0) + diag_ref[...]
     back_ref[...] = folded(back_total[...], 1.0 / 3.0)
 
 
-def sums_kernel(own_ref, other_ref, dir_ref, res_ref, image_ref, sums_ref):
-    vecs, res = dir_ref[...], res_ref[...]
-    product = own_ref[...] + other_ref[...]
-    image_ref[...] = product
+def product_kernel(head_ref, rest_ref, far_dir_ref, diag_ref, own_ref, far_vecs, total):
+    blank = jnp.zeros((128 - 2 * RHS, BLOCK), BF16)
+    far_vecs[...] = jnp.concatenate([both_pieces(far_dir_ref[...]), blank], 0).T
+
+    def some_rows(position, carry):
+        rows = pl.ds(pl.multiple_of(position * TILE, TILE), TILE)
+        total[rows, :] = jnp.dot(head_ref[rows, :], far_vecs[...], preferred_element_type=F32) + jnp.dot(
+            rest_ref[rows, :], far_vecs[...], preferred_element_type=F32
+        )
+        return carry
+
+    lax.fori_loop(0, STEPS, some_rows, 0)
+    own_ref[...] = folded(total[...].T[: 2 * RHS], 1.0 / 3.0) + diag_ref[...]
+
+
+def sums_kernel(
+    own_ref, back_ref, other_ref, dir_ref, swap_dir_ref, res_ref, swap_res_ref, product_ref, sums_ref
+):
+    mine = handles_own_block()
+    vecs = jnp.where(mine, dir_ref[...], swap_dir_ref[...])
+    res = jnp.where(mine, res_ref[...], swap_res_ref[...])
+    product = (own_ref[...] + back_ref[...]) + other_ref[...]
+    product_ref[...] = product
     image = product + NOISE * vecs
     lane = lax.broadcasted_iota(jnp.int32, (RHS, 128), 1)
     table = jnp.zeros((RHS, 128), F32)
     for i, (a, b) in enumerate(((res, res), (vecs, image), (res, image), (image, image))):
         table = jnp.where(lane == i, jnp.sum(a * b, 1, keepdims=True), table)
-    table = jnp.where(handles_own_block(), table, 0.0)
-    table = jnp.concatenate([table, jnp.zeros((128 - RHS, 128), F32)], 0)
-    sums_ref[...] = table.T[:8]
+    table = jnp.concatenate([table, jnp.zeros((128 - RHS, 128), F32)], 0).T
+    row = jnp.concatenate([table[i : i + 1, :RHS] for i in range(4)], 1)
+    sums_ref[...] = jnp.broadcast_to(row[None], sums_ref.shape)
 
 
 def update_kernel(
     sums_ref, active_ref, image_ref, other_ref, dir_ref, res_ref, sol_ref, sol_out, res_out, dir_out
 ):
-    table = sums_ref[0]
-    for i in range(1, sums_ref.shape[0]):
-        table = table + sums_ref[i]
+    row = jnp.sum(sums_ref[...], 0)
+    table = jnp.concatenate([row[:, i * RHS : (i + 1) * RHS] for i in range(4)], 0)
+    table = jnp.concatenate([table, jnp.zeros((4, RHS), F32)], 0)
+    table = jnp.concatenate([table, jnp.zeros((8, 128 - RHS), F32)], 1)
     table = jnp.concatenate([table, jnp.zeros((120, 128), F32)], 0).T
     norm_old, curvature = table[:RHS, 0:1], table[:RHS, 1:2]
     res_image, image_image = table[:RHS, 2:3], table[:RHS, 3:4]
@@ -185,9 +200,9 @@
 
 
 def to_partner(block, core, rep):
-    if core == rep:
-        return block + 32, rep
-    return block - 32 - 2 * rep, rep
+    if core == 0:
+        return (block + 32, 0) if rep == 1 else (block - 34, 1)
+    return (block + 32, 1) if rep == 1 else (block - 32, 0)
 
 
 def to_home(block, core, rep):
@@ -200,24 +215,13 @@
     return block ^ 1, rep
 
 
-def swap_rep(block, core, rep):
-    return block, 1 - rep
-
-
-def swap_near(block, core, rep):
-    return block ^ 2, 1 - rep
-
-
 def to_twin(block, core, rep):
     return (block, 1 - rep) if core == rep else None
 
 
-def over_y_and_z(value):
-    groups = []
-    for low in range(8):
-        groups.append([high * 8 + low for high in range(32)])
-    copies = jnp.broadcast_to(value[None], (32,) + value.shape)
-    return lax.all_to_all(copies, AXES, 0, 0, axis_index_groups=groups)
+def over_chips(value):
+    groups = [[block * 2 + rep for block in range(core, 128, 2) for rep in range(2)] for core in range(2)]
+    return lax.all_to_all(value, AXES, 0, 0, axis_index_groups=groups)
 
 
 def call(kernel, outs, scratch=(), name=None):
@@ -227,7 +231,7 @@
         out_shape=tuple(jax.ShapeDtypeStruct(*(out if isinstance(out[0], tuple) else (out, F32))) for out in outs),
         out_specs=(vmem,) * len(outs),
         scratch_shapes=scratch,
-        compiler_params=pltpu.CompilerParams(vmem_limit_bytes=40 * 2**20),
+        compiler_params=pltpu.CompilerParams(vmem_limit_bytes=28 * 2**20),
         name=name,
     )
 
@@ -238,24 +242,30 @@
     far_dir = permuted(direction, to_partner)
     swap_pts = permuted(points, swap_core)
     swap_dir = permuted(direction, swap_core)
+    swap_res = permuted(residual, swap_core)
     whole = (RHS, BLOCK)
+    square = ((BLOCK, BLOCK), BF16)
     side = pltpu.VMEM((DEPTH, BLOCK), BF16)
-    two = pltpu.VMEM((2 * RHS, BLOCK), BF16)
     acc = pltpu.VMEM((2 * RHS, BLOCK), F32)
+    tall = (BLOCK, 128)
     diag, left, vecs = call(
         own_kernel, [whole, ((BLOCK, DEPTH), BF16), ((2 * RHS, BLOCK), BF16)], [side, acc], "own_tile"
     )(points, swap_pts, lengths, direction, swap_dir)
-    own, back = call(cross_kernel, [whole, whole], [side, two, acc, acc], "cross_tile")(
-        left, vecs, far_pts, far_dir, lengths, diag
-    )
-    own = own + permuted(back, to_home)
-    other = permuted(own, swap_core)
-    product, sums = call(sums_kernel, [whole, (8, 128)], name="sums")(own, other, direction, residual)
-    for change in (swap_core, swap_rep, swap_near):
-        sums = sums + permuted(sums, change)
+    back, head, rest = call(kernel_kernel, [whole, square, square], [side, acc], "cross_kernel")(
+        left, vecs, far_pts, lengths
+    )
+    back = permuted(back, to_home)
+    (own,) = call(product_kernel, [whole], [pltpu.VMEM(tall, BF16), pltpu.VMEM(tall, F32)], "cross_product")(
+        head, rest, far_dir, diag
+    )
+    part = own + back
+    other = permuted(part, swap_core)
+    product, sums = call(sums_kernel, [whole, (128, 1, 128)], name="sums")(
+        own, back, other, direction, swap_dir, residual, swap_res
+    )
     twin = permuted(product, to_twin)
     return call(update_kernel, [whole] * 3, name="update")(
-        over_y_and_z(sums), active.reshape(RHS, 1), product, twin, direction, residual, solution
+        over_chips(sums), active.reshape(RHS, 1), product, twin, direction, residual, solution
     )
 
 

time: 73.9 us -> 67.2 us (0.909)
  the two profiles are of different devices: /device:TPU:32 before, /device:TPU:1 now
where the time goes in v3:
time: 67.2 us; the launch traced here: 66.9 us
  starting transfers between devices  26.7 us (40%)
  Pallas kernels  24.6 us (37%)
  waiting for transfers between devices  12.1 us (18%)
  local copies, waits for them, and re-layouts  2.74 us (4%)
  between operations  0.72 us (1%)
    ppermute x8, starting transfers between devices, permuted(): return lax.ppermute(value, AXES, pairs)  19 us
    pallas_call x1, Pallas kernels, on_device(): call(kernel_kernel, [whole, square, square], [side, acc], 'cross_kernel')  12.1 us
    all_to_all x1, waiting for transfers between devices, over_chips(): return lax.all_to_all(value, AXES, 0, 0, axis_index_groups=groups)  10.8 us
    all_to_all x1, starting transfers between devices, over_chips(): return lax.all_to_all(value, AXES, 0, 0, axis_index_groups=groups)  7.72 us
    pallas_call x1, Pallas kernels, on_device(): call(product_kernel, [whole], [pltpu.VMEM(tall, BF16), pltpu.VMEM(tall, F...  5.52 us
    pallas_call x1, Pallas kernels, on_device(): call(own_kernel, [whole, ((BLOCK, DEPTH), BF16), ((2 * RHS, BLOCK), BF16)...  4.68 us
    unnamed x12, local copies, waits for them, and re-layouts  1.91 us
    ppermute x8, waiting for transfers between devices, permuted(): return lax.ppermute(value, AXES, pairs)  1.36 us
  transfers between devices with their start and end apart: 9, of which 3 were waited for; matrix products, arithmetic and copies ran while one was open for 1% of the time, Pallas kernels for 33%

profile of v3, /device:TPU:1, one launch (start us, length us, event | category | flops | bytes accessed | tf_op | source)
XLA Modules:
  0.0 66.9 jit_solution(17450203708938289181)
XLA Ops:
  0.6 3.3 %collective-permute-start.1 = (f32[32,2048]{1,0:T(8,128)}, f32[32,2048]{1,0:T(8,128)S(1)}, u32[]{:S(2)}, u32[]{:S(2)}) collective-permute-start(f32[32,2048]{1,0:T(8,128)} %dir_ref.5), channel_id=1, source_target_pairs={{0,2},{1,3},{2,0},{3,1},{4,6},{5,7},{6,4},{7,5},{8,10},{9,11},{10,... | collective-permute-start | bytes 786440 | tf_op jit(solution)/shard_map/ppermute | solution.py:199
  4.0 0.1 collective-permute-start
  4.1 1.0 %collective-permute-start.2 = (f32[32,2048]{1,0:T(8,128)}, f32[32,2048]{1,0:T(8,128)S(1)}, u32[]{:S(2)}, u32[]{:S(2)}) collective-permute-start(f32[32,2048]{1,0:T(8,128)} %pts_ref.1), channel_id=1, source_target_pairs={{0,189},{1,64},{2,194},{3,67},{4,193},{5,68},{6,198},{7,71},{8,197... | collective-permute-start | bytes 786440 | tf_op jit(solution)/shard_map/ppermute | solution.py:199
  5.1 0.5 collective-permute-start.3
  5.5 0.7 %copy.9.len_ref = f32[32,1]{1,0:T(8,128)S(1)} copy(f32[32,1]{0,1:T(1,128)} %bitcast.2) | data formatting | bytes 256 | tf_op jit(solution)/shard_map/reshape | solution.py:240
  6.3 0.0 collective-permute-done.1.swap_dir_ref
  6.3 0.0 copy-start
  6.3 0.9 %copy-done = f32[32,2048]{1,0:T(8,128)S(1)} copy-done((f32[32,2048]{1,0:T(8,128)S(1)}, f32[32,2048]{1,0:T(8,128)}, u32[]{:S(2)}) %copy-start) | copy-done | bytes 262168
  7.2 0.9 %copy-done.3 = f32[32,2048]{1,0:T(8,128)S(1)} copy-done((f32[32,2048]{1,0:T(8,128)S(1)}, f32[32,2048]{1,0:T(8,128)}, u32[]{:S(2)}) %copy-start.3) | copy-done | bytes 262168
  8.2 4.7 %own_tile.1 = (f32[32,2048]{1,0:T(8,128)S(1)}, bf16[2048,256]{1,0:T(8,128)(2,1)S(1)}, bf16[64,2048]{1,0:T(8,128)(2,1)S(1)}) custom-call(f32[32,2048]{1,0:T(8,128)S(1)} %copy-done.3, f32[32,2048]{1,0:T(8,128)S(1)} %collective-permute-done.swap_pts_ref, f32[32,1]{1,0:T(8,128)S(1)} %copy.9.len_ref, f32[32,2048]{1,0:T(8,128)S(1)} %copy-done, ...), custom_call_target="tpu_custom_call" | custom-call | tf_op jit(solution)/shard_map/own_tile/pallas_call | solution.py:251
  12.9 12.1 %cross_kernel.1 = (f32[32,2048]{1,0:T(8,128)S(1)}, bf16[2048,2048]{1,0:T(8,128)(2,1)S(1)}, bf16[2048,2048]{1,0:T(8,128)(2,1)S(1)}) custom-call(bf16[2048,256]{1,0:T(8,128)(2,1)S(1)} %get-tuple-element.11.left, bf16[64,2048]{1,0:T(8,128)(2,1)S(1)} %get-tuple-element.12.vecs, f32[32,2048]{1,0:T(8,128)S(1)} %collective-permute-done.2.far_pts_ref, ...), custom_call_target="tpu_custom_call" | custom-call | tf_op jit(solution)/shard_map/cross_kernel/pallas_call | solution.py:254
  24.9 8.7 %collective-permute-start.4 = (f32[32,2048]{1,0:T(8,128)S(1)}, f32[32,2048]{1,0:T(8,128)S(1)}, u32[]{:S(2)}, u32[]{:S(2)}) collective-permute-start(f32[32,2048]{1,0:T(8,128)S(1)} %get-tuple-element.16), channel_id=1, source_target_pairs={{0,192},{1,70},{2,65},{3,195},{4,196},{5,74},{6,69},{7,199},{8,200... | collective-permute-start | bytes 786440 | tf_op jit(solution)/shard_map/ppermute | solution.py:199
  33.7 2.1 %collective-permute-start.6 = (f32[32,2048]{1,0:T(8,128)}, f32[32,2048]{1,0:T(8,128)S(1)}, u32[]{:S(2)}, u32[]{:S(2)}) collective-permute-start(f32[32,2048]{1,0:T(8,128)} %res_ref.3), channel_id=1, source_target_pairs={{0,2},{1,3},{2,0},{3,1},{4,6},{5,7},{6,4},{7,5},{8,10},{9,11},{10,... | collective-permute-start | bytes 786440 | tf_op jit(solution)/shard_map/ppermute | solution.py:199
  35.8 0.0 copy-start.4
  35.8 5.5 %cross_product.1.own_ref = f32[32,2048]{1,0:T(8,128)S(1)} custom-call(bf16[2048,2048]{1,0:T(8,128)(2,1)S(1)} %get-tuple-element.13.head_ref, bf16[2048,2048]{1,0:T(8,128)(2,1)S(1)} %get-tuple-element.14.rest_ref, f32[32,2048]{1,0:T(8,128)S(1)} %collective-permute-done.3.far_dir_ref, f32[32,2048]{1,0:T(8,128)S(1)} %get-tuple-element.15.diag_ref), custom_call_target="tpu_custom_call" | custom-call | tf_op jit(solution)/shard_map/cross_product/pallas_call | solution.py:258
  41.3 0.2 collective-permute-done.4.back_ref
  41.6 2.0 %collective-permute-start.5 = (f32[32,2048]{1,0:T(8,128)S(1)}, f32[32,2048]{1,0:T(8,128)S(1)}, u32[]{:S(2)}, u32[]{:S(2)}) collective-permute-start(f32[32,2048]{1,0:T(8,128)S(1)} %add.3), channel_id=1, source_target_pairs={{0,2},{1,3},{2,0},{3,1},{4,6},{5,7},{6,4},{7,5},{8,10},{9,11},{10,... | collective-permute-start | bytes 786440 | tf_op jit(solution)/shard_map/ppermute | solution.py:199
  43.5 1.2 %collective-permute-done.5.other_ref = f32[32,2048]{1,0:T(8,128)S(1)} collective-permute-done((f32[32,2048]{1,0:T(8,128)S(1)}, f32[32,2048]{1,0:T(8,128)S(1)}, u32[]{:S(2)}, u32[]{:S(2)}) %collective-permute-start.5) | collective-permute-done | bytes 262176 | tf_op jit(solution)/shard_map/ppermute | solution.py:199
  44.7 1.0 %sums.1 = (f32[32,2048]{1,0:T(8,128)S(1)}, f32[128,1,128]{2,1,0:T(1,128)}) custom-call(f32[32,2048]{1,0:T(8,128)S(1)} %cross_product.1.own_ref, f32[32,2048]{1,0:T(8,128)S(1)} %collective-permute-done.4.back_ref, f32[32,2048]{1,0:T(8,128)S(1)} %collective-permute-done.5.other_ref, f32[32,2048]{1,0:T(8,128)S(1)} %copy-done.1, ...), custom_call_target="tpu_custom_call" | custom-call | tf_op jit(solution)/shard_map/sums/pallas_call | solution.py:263
  45.7 1.3 %collective-permute-start.7 = (f32[32,2048]{1,0:T(8,128)S(1)}, f32[32,2048]{1,0:T(8,128)S(1)}, u32[]{:S(2)}, u32[]{:S(2)}) collective-permute-start(f32[32,2048]{1,0:T(8,128)S(1)} %get-tuple-element.18.image_ref), channel_id=1, source_target_pairs={{0,1},{3,2},{4,5},{7,6},{8,9},{11,10},{12,13},{15,14},{16,17},{19,... | collective-permute-start | bytes 786440 | tf_op jit(solution)/shard_map/ppermute | solution.py:199
  47.0 7.7 %all-to-all-start = ((f32[128,1,128]{2,1,0:T(1,128)}), f32[128,1,128]{2,1,0:T(1,128)S(1)}, u32[]{:S(2)}, u32[]{:S(2)}) async-start(f32[128,1,128]{2,1,0:T(1,128)} %get-tuple-element.17), calls=%async_computation | async-start | bytes 131072 | tf_op jit(solution)/shard_map/all_to_all | solution.py:224
  54.7 0.1 copy.11.active_ref
  54.8 10.8 %all-to-all-done.sums_ref = f32[128,1,128]{2,1,0:T(1,128)S(1)} async-done(((f32[128,1,128]{2,1,0:T(1,128)}), f32[128,1,128]{2,1,0:T(1,128)S(1)}, u32[]{:S(2)}, u32[]{:S(2)}) %all-to-all-start) | async-done | bytes 65568 | tf_op jit(solution)/shard_map/all_to_all | solution.py:224
  65.6 1.4 %update.1 = (f32[32,2048]{1,0:T(8,128)}, f32[32,2048]{1,0:T(8,128)}, f32[32,2048]{1,0:T(8,128)}) custom-call(f32[128,1,128]{2,1,0:T(1,128)S(1)} %all-to-all-done.sums_ref, s32[32,1]{1,0:T(8,128)S(1)} %copy.11.active_ref, f32[32,2048]{1,0:T(8,128)S(1)} %get-tuple-element.18.image_ref, f32[32,2048]{1,0:T(8,128)S(1)} %collective-permute-done.7.other_ref, ...), custom_call_target="tpu_custom_call" | custom-call | tf_op jit(solution)/shard_map/update/pallas_call | solution.py:267
  (14 shorter events, 0.1 us)
Async XLA Ops:
  0.6 5.6 %collective-permute-start.1 = (f32[32,2048]{1,0:T(8,128)}, f32[32,2048]{1,0:T(8,128)S(1)}, u32[]{:S(2)}, u32[]{:S(2)}) collective-permute-start(f32[32,2048]{1,0:T(8,128)} %dir_ref.5), channel_id=1, source_target_pairs={{0,2},{1,3},{2,0},{3,1},{4,6},{5,7},{6,4},{7,5},{8,10},{9,11},{10,... | collective-permute-start | bytes 786440 | tf_op jit(solution)/shard_map/ppermute | solution.py:199
  4.0 2.3 %collective-permute-start = (f32[32,2048]{1,0:T(8,128)}, f32[32,2048]{1,0:T(8,128)S(1)}, u32[]{:S(2)}, u32[]{:S(2)}) collective-permute-start(f32[32,2048]{1,0:T(8,128)} %pts_ref.1), channel_id=1, source_target_pairs={{0,2},{1,3},{2,0},{3,1},{4,6},{5,7},{6,4},{7,5},{8,10},{9,11},{10,... | collective-permute-start | bytes 786440 | tf_op jit(solution)/shard_map/ppermute | solution.py:199
  4.1 8.8 %collective-permute-start.2 = (f32[32,2048]{1,0:T(8,128)}, f32[32,2048]{1,0:T(8,128)S(1)}, u32[]{:S(2)}, u32[]{:S(2)}) collective-permute-start(f32[32,2048]{1,0:T(8,128)} %pts_ref.1), channel_id=1, source_target_pairs={{0,189},{1,64},{2,194},{3,67},{4,193},{5,68},{6,198},{7,71},{8,197... | collective-permute-start | bytes 786440 | tf_op jit(solution)/shard_map/ppermute | solution.py:199
  5.1 30.7 %collective-permute-start.3 = (f32[32,2048]{1,0:T(8,128)}, f32[32,2048]{1,0:T(8,128)S(1)}, u32[]{:S(2)}, u32[]{:S(2)}) collective-permute-start(f32[32,2048]{1,0:T(8,128)} %dir_ref.5), channel_id=1, source_target_pairs={{0,189},{1,64},{2,194},{3,67},{4,193},{5,68},{6,198},{7,71},{8,197... | collective-permute-start | bytes 786440 | tf_op jit(solution)/shard_map/ppermute | solution.py:199
  6.3 1.0 %copy-start = (f32[32,2048]{1,0:T(8,128)S(1)}, f32[32,2048]{1,0:T(8,128)}, u32[]{:S(2)}) copy-start(f32[32,2048]{1,0:T(8,128)} %dir_ref.5) | copy-start | bytes 786436
  7.2 0.9 %copy-start.3 = (f32[32,2048]{1,0:T(8,128)S(1)}, f32[32,2048]{1,0:T(8,128)}, u32[]{:S(2)}) copy-start(f32[32,2048]{1,0:T(8,128)} %pts_ref.1) | copy-start | bytes 786436
  24.9 16.6 %collective-permute-start.4 = (f32[32,2048]{1,0:T(8,128)S(1)}, f32[32,2048]{1,0:T(8,128)S(1)}, u32[]{:S(2)}, u32[]{:S(2)}) collective-permute-start(f32[32,2048]{1,0:T(8,128)S(1)} %get-tuple-element.16), channel_id=1, source_target_pairs={{0,192},{1,70},{2,65},{3,195},{4,196},{5,74},{6,69},{7,199},{8,200... | collective-permute-start | bytes 786440 | tf_op jit(solution)/shard_map/ppermute | solution.py:199
  33.7 9.8 %collective-permute-start.6 = (f32[32,2048]{1,0:T(8,128)}, f32[32,2048]{1,0:T(8,128)S(1)}, u32[]{:S(2)}, u32[]{:S(2)}) collective-permute-start(f32[32,2048]{1,0:T(8,128)} %res_ref.3), channel_id=1, source_target_pairs={{0,2},{1,3},{2,0},{3,1},{4,6},{5,7},{6,4},{7,5},{8,10},{9,11},{10,... | collective-permute-start | bytes 786440 | tf_op jit(solution)/shard_map/ppermute | solution.py:199
  35.8 8.9 %copy-start.1 = (f32[32,2048]{1,0:T(8,128)S(1)}, f32[32,2048]{1,0:T(8,128)}, u32[]{:S(2)}) copy-start(f32[32,2048]{1,0:T(8,128)} %dir_ref.5) | copy-start | bytes 786436
  35.8 8.9 %copy-start.2 = (f32[32,2048]{1,0:T(8,128)S(1)}, f32[32,2048]{1,0:T(8,128)}, u32[]{:S(2)}) copy-start(f32[32,2048]{1,0:T(8,128)} %res_ref.3) | copy-start | bytes 786436
  35.8 18.9 %copy-start.5 = (s32[32]{0:T(128)S(1)}, s32[32]{0:T(128)}, u32[]{:S(2)}) copy-start(s32[32]{0:T(128)} %param.11) | copy-start | bytes 388
  35.8 29.8 %copy-start.4 = (f32[32,2048]{1,0:T(8,128)S(1)}, f32[32,2048]{1,0:T(8,128)}, u32[]{:S(2)}) copy-start(f32[32,2048]{1,0:T(8,128)} %sol_ref.1) | copy-start | bytes 786436
  41.6 3.1 %collective-permute-start.5 = (f32[32,2048]{1,0:T(8,128)S(1)}, f32[32,2048]{1,0:T(8,128)S(1)}, u32[]{:S(2)}, u32[]{:S(2)}) collective-permute-start(f32[32,2048]{1,0:T(8,128)S(1)} %add.3), channel_id=1, source_target_pairs={{0,2},{1,3},{2,0},{3,1},{4,6},{5,7},{6,4},{7,5},{8,10},{9,11},{10,... | collective-permute-start | bytes 786440 | tf_op jit(solution)/shard_map/ppermute | solution.py:199
  45.7 19.9 %collective-permute-start.7 = (f32[32,2048]{1,0:T(8,128)S(1)}, f32[32,2048]{1,0:T(8,128)S(1)}, u32[]{:S(2)}, u32[]{:S(2)}) collective-permute-start(f32[32,2048]{1,0:T(8,128)S(1)} %get-tuple-element.18.image_ref), channel_id=1, source_target_pairs={{0,1},{3,2},{4,5},{7,6},{8,9},{11,10},{12,13},{15,14},{16,17},{19,... | collective-permute-start | bytes 786440 | tf_op jit(solution)/shard_map/ppermute | solution.py:199
  47.0 18.6 %all-to-all-start = ((f32[128,1,128]{2,1,0:T(1,128)}), f32[128,1,128]{2,1,0:T(1,128)S(1)}, u32[]{:S(2)}, u32[]{:S(2)}) async-start(f32[128,1,128]{2,1,0:T(1,128)} %get-tuple-element.17), calls=%async_computation | async-start | bytes 131072 | tf_op jit(solution)/shard_map/all_to_all | solution.py:224

commit v4 on v3

--- a/solution.py
+++ b/solution.py
@@ -11,6 +11,8 @@
 F32, BF16 = jnp.float32, jnp.bfloat16
 ROOT_FIVE = math.sqrt(5.0)
 LOG2_E = 1.4426950408889634
+SCALE = ROOT_FIVE * LOG2_E
+SHARE = 1.0 / (3.0 * LOG2_E * LOG2_E)
 NOISE = 0.5
 BLOCK = 2048
 DIM = 32
@@ -63,21 +65,40 @@
     return jnp.concatenate(pieces(vectors, 2), 0)
 
 
-def matern_tile(left, right):
-    sq = jnp.dot(left, right, preferred_element_type=F32)
-    sq = jnp.maximum(sq, 1e-30)
+def squares(left, right):
+    return jnp.maximum(jnp.dot(left, right, preferred_element_type=F32), 1e-30)
+
+
+def matern(sq):
     dist = sq * lax.rsqrt(sq)
-    kernel = (dist * (dist + 3.0) + 3.0) * jnp.exp2(dist * -LOG2_E)
+    return (dist * (dist + 3.0 * LOG2_E) + 3.0 * LOG2_E * LOG2_E) * jnp.exp2(-dist)
+
+
+def halves(kernel):
     head = kernel.astype(BF16)
     return head, (kernel - head.astype(F32)).astype(BF16)
 
 
-def to_rows(vectors, kernel):
-    return sum(lax.dot_general(vectors, k, NT, preferred_element_type=F32) for k in kernel)
-
-
-def to_columns(vectors, kernel):
-    return sum(jnp.dot(vectors, k, preferred_element_type=F32) for k in kernel)
+def add_rows(total, rows, vecs, cols, kernel):
+    head, rest = kernel
+    total[:, rows] += lax.dot_general(vecs[:, cols], head, NT, preferred_element_type=F32)
+    total[:RHS, rows] += lax.dot_general(vecs[:RHS, cols], rest, NT, preferred_element_type=F32)
+
+
+def add_columns(total, cols, vecs, rows, kernel):
+    head, rest = kernel
+    total[:, cols] += jnp.dot(vecs[:, rows], head, preferred_element_type=F32)
+    total[:RHS, cols] += jnp.dot(vecs[:RHS, rows], rest, preferred_element_type=F32)
+
+
+def span(index):
+    return pl.ds(pl.multiple_of(index * TILE, TILE), TILE)
+
+
+def as_column(row):
+    n = row.shape[1]
+    square = lax.broadcasted_iota(jnp.int32, (n, n), 0) == lax.broadcasted_iota(jnp.int32, (n, n), 1)
+    return jnp.sum(jnp.where(square, row, jnp.zeros_like(row)), 1, keepdims=True)
 
 
 def folded(total, scale):
@@ -88,66 +109,99 @@
     return lax.rem(lax.axis_index("blk"), 2) == lax.axis_index("rep")
 
 
-def own_kernel(pts_ref, swap_pts_ref, len_ref, dir_ref, swap_dir_ref, out_ref, left, vecs, right, total):
+def own_tiles(left, right, vecs, total, first):
+    half = lax.rem(lax.axis_index("blk"), 2)
+
+    def diagonal(i):
+        rows = span(i)
+        add_columns(total, rows, vecs, rows, halves(matern(squares(left[rows, :], right[:, rows]))))
+
+    def pair(i, j):
+        rows, cols = span(i), span(j)
+        kernel = halves(matern(squares(left[rows, :], right[:, cols])))
+        add_rows(total, rows, vecs, cols, kernel)
+        add_columns(total, cols, vecs, rows, kernel)
+
+    i = half * (STEPS // 2)
+    if first:
+        diagonal(i)
+        pair(i, i + 1)
+    else:
+        diagonal(i + 1)
+        pair(i + 1, lax.rem(i + 2, STEPS))
+        pair(half, half + STEPS // 2)
+
+
+def start_kernel(
+    pts_ref, swap_pts_ref, len_ref, dir_ref, swap_dir_ref,
+    left, right, vecs, total, scale_ref, pts, dirs, lengths, arrived,
+):
+    copies = [pltpu.make_async_copy(len_ref, lengths, arrived.at[8])]
+    for n, (source, target) in enumerate(((pts_ref, pts), (dir_ref, dirs))):
+        for k in range(4):
+            rows = slice(k * 8, k * 8 + 8)
+            copies.append(pltpu.make_async_copy(source.at[rows], target.at[rows], arrived.at[4 * n + k]))
+    for copy in copies:
+        copy.start()
     mine = handles_own_block()
-    points = jnp.where(mine, pts_ref[...], swap_pts_ref[...]) * len_ref[...] * ROOT_FIVE
+    total[...] = jnp.zeros_like(total)
+    for copy in copies:
+        copy.wait()
+    scale = as_column(lengths[...]) * SCALE
+    scale_ref[...] = jnp.broadcast_to(scale, scale_ref.shape)
+    points = jnp.where(mine, pts[...], swap_pts_ref[...]) * scale
     left[...] = left_side(points).T
     right[...] = right_side(points)
-    vecs[...] = both_pieces(jnp.where(mine, dir_ref[...], swap_dir_ref[...]))
+    vecs[...] = both_pieces(jnp.where(mine, dirs[...], swap_dir_ref[...]))
+    own_tiles(left, right, vecs, total, True)
+
+
+def kernel_kernel(left, vecs, far_pts_ref, scale_ref, back_ref, kernel_ref, right, total, sq, parts):
+    right[...] = right_side(far_pts_ref[...] * scale_ref[:, 0:1])
     total[...] = jnp.zeros_like(total)
-    half = lax.rem(lax.axis_index("blk"), 2)
-
-    def span(index):
-        return pl.ds(pl.multiple_of(index * TILE, TILE), TILE)
-
-    def pair(i, j):
-        rows, cols = span(i), span(j)
-        kernel = matern_tile(left[rows, :], right[:, cols])
-        total[:, rows] += to_rows(vecs[:, cols], kernel)
-        total[:, cols] += to_columns(vecs[:, rows], kernel)
-
-    for k in range(STEPS // 2):
-        i = half * (STEPS // 2) + k
-        rows = span(i)
-        kernel = matern_tile(left[rows, :], right[:, rows])
-        total[:, rows] += to_columns(vecs[:, rows], kernel)
-        pair(i, lax.rem(i + 1, STEPS))
-    pair(half, half + STEPS // 2)
-    out_ref[...] = folded(total[...], 4.0 / 3.0)
-
-
-def kernel_kernel(left, vecs, far_pts_ref, len_ref, back_ref, head_ref, rest_ref, right, back_total):
-    right[...] = right_side(far_pts_ref[...] * len_ref[...] * ROOT_FIVE)
-    back_total[...] = jnp.zeros_like(back_total)
-
-    def some_rows(position, carry):
-        rows = pl.ds(pl.multiple_of(position * TILE, TILE), TILE)
+    cols = [slice(c * TILE, (c + 1) * TILE) for c in range(STEPS)]
+
+    def distances(r, c):
+        sq[c % 2] = squares(left[span(r), :], right[:, cols[c]])
+
+    def product(r, c):
+        add_columns(total, cols[c], vecs, span(r), (parts[c % 2, 0], parts[c % 2, 1]))
+
+    distances(0, 0)
+
+    def some_rows(r, carry):
         for c in range(STEPS):
-            cols = slice(c * TILE, (c + 1) * TILE)
-            head, rest = matern_tile(left[rows, :], right[:, cols])
-            head_ref[rows, cols] = head
-            rest_ref[rows, cols] = rest
-            back_total[:, cols] += jnp.dot(vecs[:, rows], head, preferred_element_type=F32)
-            back_total[:RHS, cols] += jnp.dot(vecs[:RHS, rows], rest, preferred_element_type=F32)
+            if c + 1 < STEPS:
+                distances(r, c + 1)
+            else:
+                distances(jnp.minimum(r + 1, STEPS - 1), 0)
+            kernel = matern(sq[c % 2])
+            kernel_ref[span(r), cols[c]] = kernel
+            parts[c % 2, 0], parts[c % 2, 1] = halves(kernel)
+            if c > 0:
+                product(r, c - 1)
+        product(r, STEPS - 1)
         return carry
 
     lax.fori_loop(0, STEPS, some_rows, 0)
-    back_ref[...] = folded(back_total[...], 1.0 / 3.0)
-
-
-def product_kernel(head_ref, rest_ref, far_dir_ref, diag_ref, own_ref, far_vecs, total):
+    back_ref[...] = folded(total[...], SHARE)
+
+
+def product_kernel(kernel_ref, far_dir_ref, left, right, vecs, total_ref, own_ref, far_vecs, tall, total):
+    total[...] = total_ref[...]
+    own_tiles(left, right, vecs, total, False)
     blank = jnp.zeros((128 - 2 * RHS, BLOCK), BF16)
     far_vecs[...] = jnp.concatenate([both_pieces(far_dir_ref[...]), blank], 0).T
 
-    def some_rows(position, carry):
-        rows = pl.ds(pl.multiple_of(position * TILE, TILE), TILE)
-        total[rows, :] = jnp.dot(head_ref[rows, :], far_vecs[...], preferred_element_type=F32) + jnp.dot(
-            rest_ref[rows, :], far_vecs[...], preferred_element_type=F32
+    def some_rows(r, carry):
+        head, rest = halves(kernel_ref[span(r), :])
+        tall[span(r), :] = jnp.dot(head, far_vecs[...], preferred_element_type=F32) + jnp.dot(
+            rest, far_vecs[...], preferred_element_type=F32
         )
         return carry
 
     lax.fori_loop(0, STEPS, some_rows, 0)
-    own_ref[...] = folded(total[...].T[: 2 * RHS], 1.0 / 3.0) + diag_ref[...]
+    own_ref[...] = folded(tall[...].T[: 2 * RHS], SHARE) + folded(total[...], 4.0 * SHARE)
 
 
 def sums_kernel(
@@ -178,7 +232,7 @@
     table = jnp.concatenate([table, jnp.zeros((120, 128), F32)], 0).T
     norm_old, curvature = table[:RHS, 0:1], table[:RHS, 1:2]
     res_image, image_image = table[:RHS, 2:3], table[:RHS, 3:4]
-    active = active_ref[...]
+    active = as_column(active_ref[...])
     alpha = active.astype(F32) * norm_old / curvature
     norm_new = norm_old - 2.0 * alpha * res_image + alpha * alpha * image_image
     vecs = dir_ref[...]
@@ -224,11 +278,13 @@
     return lax.all_to_all(value, AXES, 0, 0, axis_index_groups=groups)
 
 
-def call(kernel, outs, scratch=(), name=None):
+def call(kernel, outs, ins, scratch=(), name=None):
     vmem = pl.BlockSpec(memory_space=pltpu.VMEM)
+    hbm = pl.BlockSpec(memory_space=pltpu.HBM)
     return pl.pallas_call(
         kernel,
         out_shape=tuple(jax.ShapeDtypeStruct(*(out if isinstance(out[0], tuple) else (out, F32))) for out in outs),
+        in_specs=[hbm if i == "h" else vmem for i in ins],
         out_specs=(vmem,) * len(outs),
         scratch_shapes=scratch,
         compiler_params=pltpu.CompilerParams(vmem_limit_bytes=28 * 2**20),
@@ -237,35 +293,56 @@
 
 
 def on_device(points, inv_length, direction, residual, solution, active):
-    lengths = inv_length.reshape(DIM, 1)
+    lengths = inv_length.reshape(1, DIM)
     far_pts = permuted(points, to_partner)
     far_dir = permuted(direction, to_partner)
     swap_pts = permuted(points, swap_core)
     swap_dir = permuted(direction, swap_core)
     swap_res = permuted(residual, swap_core)
     whole = (RHS, BLOCK)
-    square = ((BLOCK, BLOCK), BF16)
-    side = pltpu.VMEM((DEPTH, BLOCK), BF16)
-    acc = pltpu.VMEM((2 * RHS, BLOCK), F32)
+    left_shape, right_shape = ((BLOCK, DEPTH), BF16), ((DEPTH, BLOCK), BF16)
+    vecs_shape, total_shape = ((2 * RHS, BLOCK), BF16), ((2 * RHS, BLOCK), F32)
+    left, right, vecs, total, scale = call(
+        start_kernel,
+        [left_shape, right_shape, vecs_shape, total_shape, (DIM, 128)],
+        "hvhhv",
+        [
+            pltpu.VMEM(whole, F32),
+            pltpu.VMEM(whole, F32),
+            pltpu.VMEM((1, DIM), F32),
+            pltpu.SemaphoreType.DMA((9,)),
+        ],
+        "own_start",
+    )(points, swap_pts, lengths, direction, swap_dir)
+    back, kernel = call(
+        kernel_kernel,
+        [whole, (BLOCK, BLOCK)],
+        "vvvv",
+        [
+            pltpu.VMEM(*right_shape),
+            pltpu.VMEM(*total_shape),
+            pltpu.VMEM((2, TILE, TILE), F32),
+            pltpu.VMEM((2, 2, TILE, TILE), BF16),
+        ],
+        "cross_kernel",
+    )(left, vecs, far_pts, scale)
+    back = permuted(back, to_home)
     tall = (BLOCK, 128)
-    diag, left, vecs = call(
-        own_kernel, [whole, ((BLOCK, DEPTH), BF16), ((2 * RHS, BLOCK), BF16)], [side, acc], "own_tile"
-    )(points, swap_pts, lengths, direction, swap_dir)
-    back, head, rest = call(kernel_kernel, [whole, square, square], [side, acc], "cross_kernel")(
-        left, vecs, far_pts, lengths
-    )
-    back = permuted(back, to_home)
-    (own,) = call(product_kernel, [whole], [pltpu.VMEM(tall, BF16), pltpu.VMEM(tall, F32)], "cross_product")(
-        head, rest, far_dir, diag
-    )
+    (own,) = call(
+        product_kernel,
+        [whole],
+        "vvvvvv",
+        [pltpu.VMEM(tall, BF16), pltpu.VMEM(tall, F32), pltpu.VMEM(*total_shape)],
+        "cross_product",
+    )(kernel, far_dir, left, right, vecs, total)
     part = own + back
     other = permuted(part, swap_core)
-    product, sums = call(sums_kernel, [whole, (128, 1, 128)], name="sums")(
+    product, sums = call(sums_kernel, [whole, (128, 1, 128)], "vvvvvvv", name="sums")(
         own, back, other, direction, swap_dir, residual, swap_res
     )
     twin = permuted(product, to_twin)
-    return call(update_kernel, [whole] * 3, name="update")(
-        over_chips(sums), active.reshape(RHS, 1), product, twin, direction, residual, solution
+    return call(update_kernel, [whole] * 3, "vvvvvvv", name="update")(
+        over_chips(sums), active.reshape(1, RHS), product, twin, direction, residual, solution
     )
 
 

time: 67.2 us -> 64.7 us (0.963)
  blocking collectives: 0 us -> 20.4 us
  waiting for transfers between devices: 12.1 us -> 1.71 us
  starting transfers between devices: 26.7 us -> 17 us
  Pallas kernels: 24.6 us -> 22.1 us
    all_to_all x0 -> x1, blocking collectives: none -> 20.4 us  [over_chips(): return lax.all_to_all(value, AXES, 0, 0, axis_index_groups=groups)]
    all_to_all x1 -> x0, waiting for transfers between devices: 10.8 us -> none  [over_chips(): return lax.all_to_all(value, AXES, 0, 0, axis_index_groups=groups)]
    all_to_all x1 -> x0, starting transfers between devices: 7.72 us -> none  [over_chips(): return lax.all_to_all(value, AXES, 0, 0, axis_index_groups=groups)]
    pallas_call x5, Pallas kernels: 24.6 us -> 22.1 us  [the longest x1 9.57 us: on_device(): call(kernel_kernel, [whole, (BLOCK, BLOCK)], 'vvvv', [pltpu.VMEM(*right_s...]
    ppermute x8, starting transfers between devices: 19 us -> 17 us  [permuted(): return lax.ppermute(value, AXES, pairs)]
    reshape x2 -> x0, local copies, waits for them, and re-layouts: 0.82 us -> none  [the longest x1 0.74 us: on_device(): lengths = inv_length.reshape(DIM, 1)]
    unnamed x12 -> x14, local copies, waits for them, and re-layouts: 1.91 us -> 2.57 us
  transfers between devices with their start and end apart: 9 -> 8, of which waited for: 3 -> 2; matrix products, arithmetic and copies ran while one was open for 1% -> 0% of each run, Pallas kernels for 33% -> 32%
where the time goes in v4:
time: 64.7 us; the launch traced here: 64.5 us
  Pallas kernels  22.1 us (34%)
  blocking collectives  20.4 us (32%)
  starting transfers between devices  17 us (26%)
  local copies, waits for them, and re-layouts  2.57 us (4%)
  waiting for transfers between devices  1.71 us (3%)
  between operations  0.73 us (1%)
    all_to_all x1, blocking collectives, over_chips(): return lax.all_to_all(value, AXES, 0, 0, axis_index_groups=groups)  20.4 us
    ppermute x8, starting transfers between devices, permuted(): return lax.ppermute(value, AXES, pairs)  17 us
    pallas_call x1, Pallas kernels, on_device(): call(kernel_kernel, [whole, (BLOCK, BLOCK)], 'vvvv', [pltpu.VMEM(*right_s...  9.57 us
    pallas_call x1, Pallas kernels, on_device(): call(product_kernel, [whole], 'vvvvvv', [pltpu.VMEM(tall, BF16), pltpu.VM...  7.91 us
    pallas_call x1, Pallas kernels, on_device(): call(start_kernel, [left_shape, right_shape, vecs_shape, total_shape, (DI...  2.91 us
    unnamed x14, local copies, waits for them, and re-layouts  2.57 us
    ppermute x8, waiting for transfers between devices, permuted(): return lax.ppermute(value, AXES, pairs)  1.71 us
    pallas_call x1, Pallas kernels, on_device(): call(update_kernel, [whole] * 3, 'vvvvvvv', name='update')  1.35 us
  transfers between devices with their start and end apart: 8, of which 2 were waited for; matrix products, arithmetic and copies ran while one was open for 0% of the time, Pallas kernels for 32%

profile of v4, /device:TPU:1, one launch (start us, length us, event | category | flops | bytes accessed | tf_op | source)
XLA Modules:
  0.0 64.5 jit_solution(16338836579267048320)
XLA Ops:
  0.6 3.3 %collective-permute-start.1 = (f32[32,2048]{1,0:T(8,128)}, f32[32,2048]{1,0:T(8,128)S(1)}, u32[]{:S(2)}, u32[]{:S(2)}) collective-permute-start(f32[32,2048]{1,0:T(8,128)} %dir_ref.5), channel_id=1, source_target_pairs={{0,2},{1,3},{2,0},{3,1},{4,6},{5,7},{6,4},{7,5},{8,10},{9,11},{10,... | collective-permute-start | bytes 786440 | tf_op jit(solution)/shard_map/ppermute | solution.py:253
  4.0 0.1 collective-permute-start
  4.1 1.0 %collective-permute-start.2 = (f32[32,2048]{1,0:T(8,128)}, f32[32,2048]{1,0:T(8,128)S(1)}, u32[]{:S(2)}, u32[]{:S(2)}) collective-permute-start(f32[32,2048]{1,0:T(8,128)} %pts_ref.1), channel_id=1, source_target_pairs={{0,189},{1,64},{2,194},{3,67},{4,193},{5,68},{6,198},{7,71},{8,197... | collective-permute-start | bytes 786440 | tf_op jit(solution)/shard_map/ppermute | solution.py:253
  5.1 0.5 collective-permute-start.3
  5.5 0.0 collective-permute-done.1.swap_dir_ref
  5.5 0.2 collective-permute-done.swap_pts_ref
  5.7 0.9 %copy-done = f32[32,2048]{1,0:T(8,128)S(1)} copy-done((f32[32,2048]{1,0:T(8,128)S(1)}, f32[32,2048]{1,0:T(8,128)}, u32[]{:S(2)}) %copy-start) | copy-done | bytes 262168
  6.7 0.9 %copy-done.4 = f32[32,2048]{1,0:T(8,128)S(1)} copy-done((f32[32,2048]{1,0:T(8,128)S(1)}, f32[32,2048]{1,0:T(8,128)}, u32[]{:S(2)}) %copy-start.4) | copy-done | bytes 262168
  7.6 0.7 %copy-done.6 = f32[32]{0:T(128)S(1)} copy-done((f32[32]{0:T(128)S(1)}, f32[32]{0:T(128)}, u32[]{:S(2)}) %copy-start.6) | copy-done | bytes 152
  8.3 2.9 %own_start.1 = (bf16[2048,256]{1,0:T(8,128)(2,1)S(1)}, bf16[256,2048]{1,0:T(8,128)(2,1)S(1)}, bf16[64,2048]{1,0:T(8,128)(2,1)S(1)}, f32[64,2048]{1,0:T(8,128)S(1)}, f32[32,128]{1,0:T(8,128)S(1)}) custom-call(f32[32,2048]{1,0:T(8,128)S(1)} %copy-done.4, f32[32,2048]{1,0:T(8,128)S(1)} %collective-permute-done.swap_pts_ref, f32[1,32]{1,0:T(1,128)S(1)} %bitcast.3, ...), custom_call_target="tpu_custom_call" | custom-call | tf_op jit(solution)/shard_map/own_start/pallas_call | solution.py:305
  11.2 0.0 collective-permute-done.2.far_pts_ref
  11.2 9.6 %cross_kernel.1 = (f32[32,2048]{1,0:T(8,128)S(1)}, f32[2048,2048]{1,0:T(8,128)S(1)}) custom-call(bf16[2048,256]{1,0:T(8,128)(2,1)S(1)} %get-tuple-element.12.left, bf16[64,2048]{1,0:T(8,128)(2,1)S(1)} %get-tuple-element.13.vecs, f32[32,2048]{1,0:T(8,128)S(1)} %collective-permute-done.2.far_pts_ref, f32[32,128]{1,0:T(8,128)S(1)} %get-tuple-element.14.scale_ref), custom_call_target="tpu_custom_call" | custom-call | tf_op jit(solution)/shard_map/cross_kernel/pallas_call | solution.py:317
  20.8 8.6 %collective-permute-start.4 = (f32[32,2048]{1,0:T(8,128)S(1)}, f32[32,2048]{1,0:T(8,128)S(1)}, u32[]{:S(2)}, u32[]{:S(2)}) collective-permute-start(f32[32,2048]{1,0:T(8,128)S(1)} %get-tuple-element.18), channel_id=1, source_target_pairs={{0,192},{1,70},{2,65},{3,195},{4,196},{5,74},{6,69},{7,199},{8,200... | collective-permute-start | bytes 786440 | tf_op jit(solution)/shard_map/ppermute | solution.py:253
  29.4 2.1 %collective-permute-start.6 = (f32[32,2048]{1,0:T(8,128)}, f32[32,2048]{1,0:T(8,128)S(1)}, u32[]{:S(2)}, u32[]{:S(2)}) collective-permute-start(f32[32,2048]{1,0:T(8,128)} %res_ref.3), channel_id=1, source_target_pairs={{0,2},{1,3},{2,0},{3,1},{4,6},{5,7},{6,4},{7,5},{8,10},{9,11},{10,... | collective-permute-start | bytes 786440 | tf_op jit(solution)/shard_map/ppermute | solution.py:253
  31.5 0.0 collective-permute-done.3.far_dir_ref
  31.5 7.9 %cross_product.1.own_ref = f32[32,2048]{1,0:T(8,128)S(1)} custom-call(f32[2048,2048]{1,0:T(8,128)S(1)} %get-tuple-element.15.kernel_ref, f32[32,2048]{1,0:T(8,128)S(1)} %collective-permute-done.3.far_dir_ref, bf16[2048,256]{1,0:T(8,128)(2,1)S(1)} %get-tuple-element.12.left, bf16[256,2048]{1,0:T(8,128)(2,1)S(1)} %get-tuple-element.16.right, ...), custom_call_target="tpu_custom_call" | custom-call | tf_op jit(solution)/shard_map/cross_product/pallas_call | solution.py:331
  39.4 0.0 collective-permute-done.4.back_ref
  39.5 0.1 collective-permute-start.5
  39.6 0.0 collective-permute-done.6.swap_res_ref
  39.6 1.5 %collective-permute-done.5.other_ref = f32[32,2048]{1,0:T(8,128)S(1)} collective-permute-done((f32[32,2048]{1,0:T(8,128)S(1)}, f32[32,2048]{1,0:T(8,128)S(1)}, u32[]{:S(2)}, u32[]{:S(2)}) %collective-permute-start.5) | collective-permute-done | bytes 262176 | tf_op jit(solution)/shard_map/ppermute | solution.py:253
  41.1 0.4 sums.1
  41.5 1.3 %collective-permute-start.7 = (f32[32,2048]{1,0:T(8,128)S(1)}, f32[32,2048]{1,0:T(8,128)S(1)}, u32[]{:S(2)}, u32[]{:S(2)}) collective-permute-start(f32[32,2048]{1,0:T(8,128)S(1)} %get-tuple-element.20.image_ref), channel_id=1, source_target_pairs={{0,1},{3,2},{4,5},{7,6},{8,9},{11,10},{12,13},{15,14},{16,17},{19,... | collective-permute-start | bytes 786440 | tf_op jit(solution)/shard_map/ppermute | solution.py:253
  42.8 20.4 %all_to_all.5.sums_ref = f32[128,1,128]{2,1,0:T(1,128)S(1)} all-to-all(f32[128,1,128]{2,1,0:T(1,128)S(1)} %get-tuple-element.19), channel_id=1, replica_groups={{0,1,4,5,8,9,12,13,16,17,20,21,24,25,28,29,32,33,36,37,40,41,44,45,48,4..., dimensions={0} | all-to-all | bytes 131072 | tf_op jit(solution)/shard_map/all_to_all | solution.py:278
  63.1 1.4 %update.1 = (f32[32,2048]{1,0:T(8,128)}, f32[32,2048]{1,0:T(8,128)}, f32[32,2048]{1,0:T(8,128)}) custom-call(f32[128,1,128]{2,1,0:T(1,128)S(1)} %all_to_all.5.sums_ref, s32[1,32]{1,0:T(1,128)S(1)} %bitcast.2, f32[32,2048]{1,0:T(8,128)S(1)} %get-tuple-element.20.image_ref, f32[32,2048]{1,0:T(8,128)S(1)} %collective-permute-done.7.other_ref, ...), custom_call_target="tpu_custom_call" | custom-call | tf_op jit(solution)/shard_map/update/pallas_call | solution.py:344
  (13 shorter events, 0.1 us)
Async XLA Ops:
  0.6 62.5 %copy-start.5 = (s32[32]{0:T(128)S(1)}, s32[32]{0:T(128)}, u32[]{:S(2)}) copy-start(s32[32]{0:T(128)} %param.11) | copy-start | bytes 388
  0.6 4.9 %collective-permute-start.1 = (f32[32,2048]{1,0:T(8,128)}, f32[32,2048]{1,0:T(8,128)S(1)}, u32[]{:S(2)}, u32[]{:S(2)}) collective-permute-start(f32[32,2048]{1,0:T(8,128)} %dir_ref.5), channel_id=1, source_target_pairs={{0,2},{1,3},{2,0},{3,1},{4,6},{5,7},{6,4},{7,5},{8,10},{9,11},{10,... | collective-permute-start | bytes 786440 | tf_op jit(solution)/shard_map/ppermute | solution.py:253
  4.0 1.7 %collective-permute-start = (f32[32,2048]{1,0:T(8,128)}, f32[32,2048]{1,0:T(8,128)S(1)}, u32[]{:S(2)}, u32[]{:S(2)}) collective-permute-start(f32[32,2048]{1,0:T(8,128)} %pts_ref.1), channel_id=1, source_target_pairs={{0,2},{1,3},{2,0},{3,1},{4,6},{5,7},{6,4},{7,5},{8,10},{9,11},{10,... | collective-permute-start | bytes 786440 | tf_op jit(solution)/shard_map/ppermute | solution.py:253
  4.1 7.1 %collective-permute-start.2 = (f32[32,2048]{1,0:T(8,128)}, f32[32,2048]{1,0:T(8,128)S(1)}, u32[]{:S(2)}, u32[]{:S(2)}) collective-permute-start(f32[32,2048]{1,0:T(8,128)} %pts_ref.1), channel_id=1, source_target_pairs={{0,189},{1,64},{2,194},{3,67},{4,193},{5,68},{6,198},{7,71},{8,197... | collective-permute-start | bytes 786440 | tf_op jit(solution)/shard_map/ppermute | solution.py:253
  5.1 26.4 %collective-permute-start.3 = (f32[32,2048]{1,0:T(8,128)}, f32[32,2048]{1,0:T(8,128)S(1)}, u32[]{:S(2)}, u32[]{:S(2)}) collective-permute-start(f32[32,2048]{1,0:T(8,128)} %dir_ref.5), channel_id=1, source_target_pairs={{0,189},{1,64},{2,194},{3,67},{4,193},{5,68},{6,198},{7,71},{8,197... | collective-permute-start | bytes 786440 | tf_op jit(solution)/shard_map/ppermute | solution.py:253
  5.7 0.9 %copy-start = (f32[32,2048]{1,0:T(8,128)S(1)}, f32[32,2048]{1,0:T(8,128)}, u32[]{:S(2)}) copy-start(f32[32,2048]{1,0:T(8,128)} %dir_ref.5) | copy-start | bytes 786436
  6.7 0.9 %copy-start.4 = (f32[32,2048]{1,0:T(8,128)S(1)}, f32[32,2048]{1,0:T(8,128)}, u32[]{:S(2)}) copy-start(f32[32,2048]{1,0:T(8,128)} %pts_ref.1) | copy-start | bytes 786436
  7.6 0.7 %copy-start.6 = (f32[32]{0:T(128)S(1)}, f32[32]{0:T(128)}, u32[]{:S(2)}) copy-start(f32[32]{0:T(128)} %param.7) | copy-start | bytes 388
  8.3 32.8 %copy-start.1 = (f32[32,2048]{1,0:T(8,128)S(1)}, f32[32,2048]{1,0:T(8,128)}, u32[]{:S(2)}) copy-start(f32[32,2048]{1,0:T(8,128)} %dir_ref.5) | copy-start | bytes 786436
  8.3 32.8 %copy-start.2 = (f32[32,2048]{1,0:T(8,128)S(1)}, f32[32,2048]{1,0:T(8,128)}, u32[]{:S(2)}) copy-start(f32[32,2048]{1,0:T(8,128)} %res_ref.3) | copy-start | bytes 786436
  8.3 54.9 %copy-start.3 = (f32[32,2048]{1,0:T(8,128)S(1)}, f32[32,2048]{1,0:T(8,128)}, u32[]{:S(2)}) copy-start(f32[32,2048]{1,0:T(8,128)} %sol_ref.1) | copy-start | bytes 786436
  20.8 18.6 %collective-permute-start.4 = (f32[32,2048]{1,0:T(8,128)S(1)}, f32[32,2048]{1,0:T(8,128)S(1)}, u32[]{:S(2)}, u32[]{:S(2)}) collective-permute-start(f32[32,2048]{1,0:T(8,128)S(1)} %get-tuple-element.18), channel_id=1, source_target_pairs={{0,192},{1,70},{2,65},{3,195},{4,196},{5,74},{6,69},{7,199},{8,200... | collective-permute-start | bytes 786440 | tf_op jit(solution)/shard_map/ppermute | solution.py:253
  29.4 10.2 %collective-permute-start.6 = (f32[32,2048]{1,0:T(8,128)}, f32[32,2048]{1,0:T(8,128)S(1)}, u32[]{:S(2)}, u32[]{:S(2)}) collective-permute-start(f32[32,2048]{1,0:T(8,128)} %res_ref.3), channel_id=1, source_target_pairs={{0,2},{1,3},{2,0},{3,1},{4,6},{5,7},{6,4},{7,5},{8,10},{9,11},{10,... | collective-permute-start | bytes 786440 | tf_op jit(solution)/shard_map/ppermute | solution.py:253
  39.5 1.6 %collective-permute-start.5 = (f32[32,2048]{1,0:T(8,128)S(1)}, f32[32,2048]{1,0:T(8,128)S(1)}, u32[]{:S(2)}, u32[]{:S(2)}) collective-permute-start(f32[32,2048]{1,0:T(8,128)S(1)} %add.3), channel_id=1, source_target_pairs={{0,2},{1,3},{2,0},{3,1},{4,6},{5,7},{6,4},{7,5},{8,10},{9,11},{10,... | collective-permute-start | bytes 786440 | tf_op jit(solution)/shard_map/ppermute | solution.py:253
  41.5 21.7 %collective-permute-start.7 = (f32[32,2048]{1,0:T(8,128)S(1)}, f32[32,2048]{1,0:T(8,128)S(1)}, u32[]{:S(2)}, u32[]{:S(2)}) collective-permute-start(f32[32,2048]{1,0:T(8,128)S(1)} %get-tuple-element.20.image_ref), channel_id=1, source_target_pairs={{0,1},{3,2},{4,5},{7,6},{8,9},{11,10},{12,13},{15,14},{16,17},{19,... | collective-permute-start | bytes 786440 | tf_op jit(solution)/shard_map/ppermute | solution.py:253

commit v5 on v4

--- a/solution.py
+++ b/solution.py
@@ -107,6 +107,10 @@
 
 def handles_own_block():
     return lax.rem(lax.axis_index("blk"), 2) == lax.axis_index("rep")
+
+
+def waits_longest():
+    return jnp.logical_and(lax.rem(lax.axis_index("blk"), 32) == 30, lax.axis_index("rep") == 1)
 
 
 def own_tiles(left, right, vecs, total, first):
@@ -155,6 +159,10 @@
     vecs[...] = both_pieces(jnp.where(mine, dirs[...], swap_dir_ref[...]))
     own_tiles(left, right, vecs, total, True)
 
+    @pl.when(waits_longest())
+    def _():
+        own_tiles(left, right, vecs, total, False)
+
 
 def kernel_kernel(left, vecs, far_pts_ref, scale_ref, back_ref, kernel_ref, right, total, sq, parts):
     right[...] = right_side(far_pts_ref[...] * scale_ref[:, 0:1])
@@ -189,7 +197,11 @@
 
 def product_kernel(kernel_ref, far_dir_ref, left, right, vecs, total_ref, own_ref, far_vecs, tall, total):
     total[...] = total_ref[...]
-    own_tiles(left, right, vecs, total, False)
+
+    @pl.when(jnp.logical_not(waits_longest()))
+    def _():
+        own_tiles(left, right, vecs, total, False)
+
     blank = jnp.zeros((128 - 2 * RHS, BLOCK), BF16)
     far_vecs[...] = jnp.concatenate([both_pieces(far_dir_ref[...]), blank], 0).T
 
@@ -223,7 +235,8 @@
 
 
 def update_kernel(
-    sums_ref, active_ref, image_ref, other_ref, dir_ref, res_ref, sol_ref, sol_out, res_out, dir_out
+    sums_ref, active_ref, image_ref, other_ref, dir_ref, res_ref, sol_ref,
+    sol_out, res_out, dir_out, sol_next, res_next, dir_next, sent,
 ):
     row = jnp.sum(sums_ref[...], 0)
     table = jnp.concatenate([row[:, i * RHS : (i + 1) * RHS] for i in range(4)], 0)
@@ -235,12 +248,22 @@
     active = as_column(active_ref[...])
     alpha = active.astype(F32) * norm_old / curvature
     norm_new = norm_old - 2.0 * alpha * res_image + alpha * alpha * image_image
-    vecs = dir_ref[...]
-    image = jnp.where(handles_own_block(), image_ref[...], other_ref[...]) + NOISE * vecs
-    sol_out[...] = sol_ref[...] + alpha * vecs
-    res_next = res_ref[...] - alpha * image
-    res_out[...] = res_next
-    dir_out[...] = jnp.where(active == 1, res_next + (norm_new / norm_old) * vecs, vecs)
+    ratio = norm_new / norm_old
+    mine = handles_own_block()
+    copies = []
+    for k in range(4):
+        rows = slice(k * 8, k * 8 + 8)
+        vecs = dir_ref[rows]
+        image = jnp.where(mine, image_ref[rows], other_ref[rows]) + NOISE * vecs
+        sol_next[rows] = sol_ref[rows] + alpha[rows] * vecs
+        after = res_ref[rows] - alpha[rows] * image
+        res_next[rows] = after
+        dir_next[rows] = jnp.where(active[rows] == 1, after + ratio[rows] * vecs, vecs)
+        for n, (source, target) in enumerate(((sol_next, sol_out), (res_next, res_out), (dir_next, dir_out))):
+            copies.append(pltpu.make_async_copy(source.at[rows], target.at[rows], sent.at[3 * k + n]))
+            copies[-1].start()
+    for copy in copies:
+        copy.wait()
 
 
 def permuted(value, change):
@@ -278,18 +301,23 @@
     return lax.all_to_all(value, AXES, 0, 0, axis_index_groups=groups)
 
 
-def call(kernel, outs, ins, scratch=(), name=None):
+def call(kernel, outs, ins, scratch=(), name=None, out_space=pltpu.VMEM):
     vmem = pl.BlockSpec(memory_space=pltpu.VMEM)
     hbm = pl.BlockSpec(memory_space=pltpu.HBM)
-    return pl.pallas_call(
+    run = pl.pallas_call(
         kernel,
         out_shape=tuple(jax.ShapeDtypeStruct(*(out if isinstance(out[0], tuple) else (out, F32))) for out in outs),
         in_specs=[hbm if i == "h" else vmem for i in ins],
-        out_specs=(vmem,) * len(outs),
+        out_specs=(pl.BlockSpec(memory_space=out_space),) * len(outs),
         scratch_shapes=scratch,
         compiler_params=pltpu.CompilerParams(vmem_limit_bytes=28 * 2**20),
         name=name,
     )
+
+    def placed(*args):
+        return run(*(pltpu.with_memory_space_constraint(a, pltpu.HBM) if i == "h" else a for i, a in zip(ins, args)))
+
+    return placed
 
 
 def on_device(points, inv_length, direction, residual, solution, active):
@@ -341,7 +369,14 @@
         own, back, other, direction, swap_dir, residual, swap_res
     )
     twin = permuted(product, to_twin)
-    return call(update_kernel, [whole] * 3, "vvvvvvv", name="update")(
+    return call(
+        update_kernel,
+        [whole] * 3,
+        "vvvvvvv",
+        [pltpu.VMEM(whole, F32)] * 3 + [pltpu.SemaphoreType.DMA((12,))],
+        "update",
+        pltpu.HBM,
+    )(
         over_chips(sums), active.reshape(1, RHS), product, twin, direction, residual, solution
     )
 

time: 64.7 us -> 65.4 us (1.011)
  local copies, waits for them, and re-layouts: 2.57 us -> 0.02 us
  waiting for transfers between devices: 1.71 us -> 3.71 us
  blocking collectives: 20.4 us -> 21.2 us
  Pallas kernels: 22.1 us -> 22.9 us
    unnamed x14 -> x8, local copies, waits for them, and re-layouts: 2.57 us -> 0.02 us
    ppermute x8, waiting for transfers between devices: 1.71 us -> 3.71 us  [permuted(): return lax.ppermute(value, AXES, pairs)]
    all_to_all x1, blocking collectives: 20.4 us -> 21.2 us  [over_chips(): return lax.all_to_all(value, AXES, 0, 0, axis_index_groups=groups)]
    pallas_call x5, Pallas kernels: 22.1 us -> 22.9 us  [placed(): run(*(pltpu.with_memory_space_constraint(a, pltpu.HBM) if i == 'h' else a...]
  transfers between devices with their start and end apart: 8 -> 8, of which waited for: 2 -> 4; matrix products, arithmetic and copies ran while one was open for 0% -> 0% of each run, Pallas kernels for 32% -> 32%
where the time goes in v5:
time: 65.4 us; the launch traced here: 65.2 us
  Pallas kernels  22.9 us (35%)
  blocking collectives  21.2 us (32%)
  starting transfers between devices  16.4 us (25%)
  waiting for transfers between devices  3.71 us (6%)
  between operations  0.89 us (1%)
    pallas_call x5, Pallas kernels, placed(): run(*(pltpu.with_memory_space_constraint(a, pltpu.HBM) if i == 'h' else a...  22.9 us
    all_to_all x1, blocking collectives, over_chips(): return lax.all_to_all(value, AXES, 0, 0, axis_index_groups=groups)  21.2 us
    ppermute x8, starting transfers between devices, permuted(): return lax.ppermute(value, AXES, pairs)  16.4 us
    ppermute x8, waiting for transfers between devices, permuted(): return lax.ppermute(value, AXES, pairs)  3.71 us
  transfers between devices with their start and end apart: 8, of which 4 were waited for; matrix products, arithmetic and copies ran while one was open for 0% of the time, Pallas kernels for 32%

profile of v5, /device:TPU:1, one launch (start us, length us, event | category | flops | bytes accessed | tf_op | source)
XLA Modules:
  0.0 65.2 jit_solution(5447930895545457678)
XLA Ops:
  0.6 0.0 copy-start
  0.6 0.0 copy-start.1
  0.7 3.3 %collective-permute-start.1 = (f32[32,2048]{1,0:T(8,128)}, f32[32,2048]{1,0:T(8,128)S(1)}, u32[]{:S(2)}, u32[]{:S(2)}) collective-permute-start(f32[32,2048]{1,0:T(8,128)} %dir_ref.5), channel_id=1, source_target_pairs={{0,2},{1,3},{2,0},{3,1},{4,6},{5,7},{6,4},{7,5},{8,10},{9,11},{10,... | collective-permute-start | bytes 786440 | tf_op jit(solution)/shard_map/ppermute | solution.py:276
  4.0 0.1 collective-permute-start
  4.1 1.0 %collective-permute-start.2 = (f32[32,2048]{1,0:T(8,128)}, f32[32,2048]{1,0:T(8,128)S(1)}, u32[]{:S(2)}, u32[]{:S(2)}) collective-permute-start(f32[32,2048]{1,0:T(8,128)} %pts_ref.1), channel_id=1, source_target_pairs={{0,189},{1,64},{2,194},{3,67},{4,193},{5,68},{6,198},{7,71},{8,197... | collective-permute-start | bytes 786440 | tf_op jit(solution)/shard_map/ppermute | solution.py:276
  5.1 0.5 collective-permute-start.3
  5.6 0.0 collective-permute-done.1.swap_dir_ref
  5.6 0.2 collective-permute-done.swap_pts_ref
  5.7 3.3 %own_start.1 = (bf16[2048,256]{1,0:T(8,128)(2,1)S(1)}, bf16[256,2048]{1,0:T(8,128)(2,1)S(1)}, bf16[64,2048]{1,0:T(8,128)(2,1)S(1)}, f32[64,2048]{1,0:T(8,128)S(1)}, f32[32,128]{1,0:T(8,128)S(1)}) custom-call(f32[32,2048]{1,0:T(8,128)} %pts_ref.1, f32[32,2048]{1,0:T(8,128)S(1)} %collective-permute-done.swap_pts_ref, f32[1,32]{1,0:T(1,128)} %bitcast.3, ...), custom_call_target="tpu_custom_call" | custom-call | tf_op jit(solution)/shard_map/own_start/pallas_call | solution.py:318
  9.0 0.5 collective-permute-done.2.far_pts_ref
  9.5 9.6 %cross_kernel.1 = (f32[32,2048]{1,0:T(8,128)S(1)}, f32[2048,2048]{1,0:T(8,128)S(1)}) custom-call(bf16[2048,256]{1,0:T(8,128)(2,1)S(1)} %get-tuple-element.12.left, bf16[64,2048]{1,0:T(8,128)(2,1)S(1)} %get-tuple-element.13.vecs, f32[32,2048]{1,0:T(8,128)S(1)} %collective-permute-done.2.far_pts_ref, f32[32,128]{1,0:T(8,128)S(1)} %get-tuple-element.14.scale_ref), custom_call_target="tpu_custom_call" | custom-call | tf_op jit(solution)/shard_map/cross_kernel/pallas_call | solution.py:318
  19.1 8.1 %collective-permute-start.4 = (f32[32,2048]{1,0:T(8,128)S(1)}, f32[32,2048]{1,0:T(8,128)S(1)}, u32[]{:S(2)}, u32[]{:S(2)}) collective-permute-start(f32[32,2048]{1,0:T(8,128)S(1)} %get-tuple-element.18), channel_id=1, source_target_pairs={{0,192},{1,70},{2,65},{3,195},{4,196},{5,74},{6,69},{7,199},{8,200... | collective-permute-start | bytes 786440 | tf_op jit(solution)/shard_map/ppermute | solution.py:276
  27.2 2.1 %collective-permute-start.6 = (f32[32,2048]{1,0:T(8,128)}, f32[32,2048]{1,0:T(8,128)S(1)}, u32[]{:S(2)}, u32[]{:S(2)}) collective-permute-start(f32[32,2048]{1,0:T(8,128)} %res_ref.3), channel_id=1, source_target_pairs={{0,2},{1,3},{2,0},{3,1},{4,6},{5,7},{6,4},{7,5},{8,10},{9,11},{10,... | collective-permute-start | bytes 786440 | tf_op jit(solution)/shard_map/ppermute | solution.py:276
  29.3 0.0 collective-permute-done.3.far_dir_ref
  29.3 8.3 %cross_product.1.own_ref = f32[32,2048]{1,0:T(8,128)S(1)} custom-call(f32[2048,2048]{1,0:T(8,128)S(1)} %get-tuple-element.15.kernel_ref, f32[32,2048]{1,0:T(8,128)S(1)} %collective-permute-done.3.far_dir_ref, bf16[2048,256]{1,0:T(8,128)(2,1)S(1)} %get-tuple-element.12.left, bf16[256,2048]{1,0:T(8,128)(2,1)S(1)} %get-tuple-element.16.right, ...), custom_call_target="tpu_custom_call" | custom-call | tf_op jit(solution)/shard_map/cross_product/pallas_call | solution.py:318
  37.6 1.5 %collective-permute-done.4.back_ref = f32[32,2048]{1,0:T(8,128)S(1)} collective-permute-done((f32[32,2048]{1,0:T(8,128)S(1)}, f32[32,2048]{1,0:T(8,128)S(1)}, u32[]{:S(2)}, u32[]{:S(2)}) %collective-permute-start.4) | collective-permute-done | bytes 262176 | tf_op jit(solution)/shard_map/ppermute | solution.py:276
  39.1 0.1 collective-permute-start.5
  39.2 0.0 collective-permute-done.6.swap_res_ref
  39.2 1.5 %collective-permute-done.5.other_ref = f32[32,2048]{1,0:T(8,128)S(1)} collective-permute-done((f32[32,2048]{1,0:T(8,128)S(1)}, f32[32,2048]{1,0:T(8,128)S(1)}, u32[]{:S(2)}, u32[]{:S(2)}) %collective-permute-start.5) | collective-permute-done | bytes 262176 | tf_op jit(solution)/shard_map/ppermute | solution.py:276
  40.7 0.4 sums.1
  41.1 1.3 %collective-permute-start.7 = (f32[32,2048]{1,0:T(8,128)S(1)}, f32[32,2048]{1,0:T(8,128)S(1)}, u32[]{:S(2)}, u32[]{:S(2)}) collective-permute-start(f32[32,2048]{1,0:T(8,128)S(1)} %get-tuple-element.20.image_ref), channel_id=1, source_target_pairs={{0,1},{3,2},{4,5},{7,6},{8,9},{11,10},{12,13},{15,14},{16,17},{19,... | collective-permute-start | bytes 786440 | tf_op jit(solution)/shard_map/ppermute | solution.py:276
  42.4 21.2 %all_to_all.5.sums_ref = f32[128,1,128]{2,1,0:T(1,128)S(1)} all-to-all(f32[128,1,128]{2,1,0:T(1,128)S(1)} %get-tuple-element.19), channel_id=1, replica_groups={{0,1,4,5,8,9,12,13,16,17,20,21,24,25,28,29,32,33,36,37,40,41,44,45,48,4..., dimensions={0} | all-to-all | bytes 131072 | tf_op jit(solution)/shard_map/all_to_all | solution.py:301
  63.6 0.0 collective-permute-done.7.other_ref
  63.7 1.4 %update.1 = (f32[32,2048]{1,0:T(8,128)}, f32[32,2048]{1,0:T(8,128)}, f32[32,2048]{1,0:T(8,128)}) custom-call(f32[128,1,128]{2,1,0:T(1,128)S(1)} %all_to_all.5.sums_ref, s32[1,32]{1,0:T(1,128)S(1)} %bitcast.2, f32[32,2048]{1,0:T(8,128)S(1)} %get-tuple-element.20.image_ref, f32[32,2048]{1,0:T(8,128)S(1)} %collective-permute-done.7.other_ref, ...), custom_call_target="tpu_custom_call" | custom-call | tf_op jit(solution)/shard_map/update/pallas_call | solution.py:318
  (7 shorter events, 0.0 us)
Async XLA Ops:
  0.6 40.1 %copy-start = (f32[32,2048]{1,0:T(8,128)S(1)}, f32[32,2048]{1,0:T(8,128)}, u32[]{:S(2)}) copy-start(f32[32,2048]{1,0:T(8,128)} %dir_ref.5) | copy-start | bytes 786436
  0.6 40.1 %copy-start.1 = (f32[32,2048]{1,0:T(8,128)S(1)}, f32[32,2048]{1,0:T(8,128)}, u32[]{:S(2)}) copy-start(f32[32,2048]{1,0:T(8,128)} %res_ref.3) | copy-start | bytes 786436
  0.7 63.0 %copy-start.3 = (s32[32]{0:T(128)S(1)}, s32[32]{0:T(128)}, u32[]{:S(2)}) copy-start(s32[32]{0:T(128)} %param.11) | copy-start | bytes 388
  0.7 63.0 %copy-start.2 = (f32[32,2048]{1,0:T(8,128)S(1)}, f32[32,2048]{1,0:T(8,128)}, u32[]{:S(2)}) copy-start(f32[32,2048]{1,0:T(8,128)} %sol_ref.1) | copy-start | bytes 786436
  0.7 4.9 %collective-permute-start.1 = (f32[32,2048]{1,0:T(8,128)}, f32[32,2048]{1,0:T(8,128)S(1)}, u32[]{:S(2)}, u32[]{:S(2)}) collective-permute-start(f32[32,2048]{1,0:T(8,128)} %dir_ref.5), channel_id=1, source_target_pairs={{0,2},{1,3},{2,0},{3,1},{4,6},{5,7},{6,4},{7,5},{8,10},{9,11},{10,... | collective-permute-start | bytes 786440 | tf_op jit(solution)/shard_map/ppermute | solution.py:276
  4.0 1.7 %collective-permute-start = (f32[32,2048]{1,0:T(8,128)}, f32[32,2048]{1,0:T(8,128)S(1)}, u32[]{:S(2)}, u32[]{:S(2)}) collective-permute-start(f32[32,2048]{1,0:T(8,128)} %pts_ref.1), channel_id=1, source_target_pairs={{0,2},{1,3},{2,0},{3,1},{4,6},{5,7},{6,4},{7,5},{8,10},{9,11},{10,... | collective-permute-start | bytes 786440 | tf_op jit(solution)/shard_map/ppermute | solution.py:276
  4.1 5.4 %collective-permute-start.2 = (f32[32,2048]{1,0:T(8,128)}, f32[32,2048]{1,0:T(8,128)S(1)}, u32[]{:S(2)}, u32[]{:S(2)}) collective-permute-start(f32[32,2048]{1,0:T(8,128)} %pts_ref.1), channel_id=1, source_target_pairs={{0,189},{1,64},{2,194},{3,67},{4,193},{5,68},{6,198},{7,71},{8,197... | collective-permute-start | bytes 786440 | tf_op jit(solution)/shard_map/ppermute | solution.py:276
  5.1 24.2 %collective-permute-start.3 = (f32[32,2048]{1,0:T(8,128)}, f32[32,2048]{1,0:T(8,128)S(1)}, u32[]{:S(2)}, u32[]{:S(2)}) collective-permute-start(f32[32,2048]{1,0:T(8,128)} %dir_ref.5), channel_id=1, source_target_pairs={{0,189},{1,64},{2,194},{3,67},{4,193},{5,68},{6,198},{7,71},{8,197... | collective-permute-start | bytes 786440 | tf_op jit(solution)/shard_map/ppermute | solution.py:276
  19.1 20.0 %collective-permute-start.4 = (f32[32,2048]{1,0:T(8,128)S(1)}, f32[32,2048]{1,0:T(8,128)S(1)}, u32[]{:S(2)}, u32[]{:S(2)}) collective-permute-start(f32[32,2048]{1,0:T(8,128)S(1)} %get-tuple-element.18), channel_id=1, source_target_pairs={{0,192},{1,70},{2,65},{3,195},{4,196},{5,74},{6,69},{7,199},{8,200... | collective-permute-start | bytes 786440 | tf_op jit(solution)/shard_map/ppermute | solution.py:276
  27.2 12.0 %collective-permute-start.6 = (f32[32,2048]{1,0:T(8,128)}, f32[32,2048]{1,0:T(8,128)S(1)}, u32[]{:S(2)}, u32[]{:S(2)}) collective-permute-start(f32[32,2048]{1,0:T(8,128)} %res_ref.3), channel_id=1, source_target_pairs={{0,2},{1,3},{2,0},{3,1},{4,6},{5,7},{6,4},{7,5},{8,10},{9,11},{10,... | collective-permute-start | bytes 786440 | tf_op jit(solution)/shard_map/ppermute | solution.py:276
  39.1 1.6 %collective-permute-start.5 = (f32[32,2048]{1,0:T(8,128)S(1)}, f32[32,2048]{1,0:T(8,128)S(1)}, u32[]{:S(2)}, u32[]{:S(2)}) collective-permute-start(f32[32,2048]{1,0:T(8,128)S(1)} %add.3), channel_id=1, source_target_pairs={{0,2},{1,3},{2,0},{3,1},{4,6},{5,7},{6,4},{7,5},{8,10},{9,11},{10,... | collective-permute-start | bytes 786440 | tf_op jit(solution)/shard_map/ppermute | solution.py:276
  41.1 22.5 %collective-permute-start.7 = (f32[32,2048]{1,0:T(8,128)S(1)}, f32[32,2048]{1,0:T(8,128)S(1)}, u32[]{:S(2)}, u32[]{:S(2)}) collective-permute-start(f32[32,2048]{1,0:T(8,128)S(1)} %get-tuple-element.20.image_ref), channel_id=1, source_target_pairs={{0,1},{3,2},{4,5},{7,6},{8,9},{11,10},{12,13},{15,14},{16,17},{19,... | collective-permute-start | bytes 786440 | tf_op jit(solution)/shard_map/ppermute | solution.py:276

commit v6 on v5

--- a/solution.py
+++ b/solution.py
@@ -110,7 +110,7 @@
 
 
 def waits_longest():
-    return jnp.logical_and(lax.rem(lax.axis_index("blk"), 32) == 30, lax.axis_index("rep") == 1)
+    return jnp.logical_and(lax.rem(lax.axis_index("blk"), 4) == 2, lax.axis_index("rep") == 1)
 
 
 def own_tiles(left, right, vecs, total, first):
@@ -159,7 +159,21 @@
     vecs[...] = both_pieces(jnp.where(mine, dirs[...], swap_dir_ref[...]))
     own_tiles(left, right, vecs, total, True)
 
+
+def early_kernel(left, right, vecs, total_in, scale_in, total, scale):
+    total[...] = total_in[...]
+    scale[...] = scale_in[...]
+
     @pl.when(waits_longest())
+    def _():
+        own_tiles(left, right, vecs, total, False)
+
+
+def late_kernel(left, right, vecs, total_in, back_in, total, back):
+    total[...] = total_in[...]
+    back[...] = back_in[...]
+
+    @pl.when(jnp.logical_not(waits_longest()))
     def _():
         own_tiles(left, right, vecs, total, False)
 
@@ -195,13 +209,7 @@
     back_ref[...] = folded(total[...], SHARE)
 
 
-def product_kernel(kernel_ref, far_dir_ref, left, right, vecs, total_ref, own_ref, far_vecs, tall, total):
-    total[...] = total_ref[...]
-
-    @pl.when(jnp.logical_not(waits_longest()))
-    def _():
-        own_tiles(left, right, vecs, total, False)
-
+def product_kernel(kernel_ref, far_dir_ref, total_ref, own_ref, far_vecs, tall):
     blank = jnp.zeros((128 - 2 * RHS, BLOCK), BF16)
     far_vecs[...] = jnp.concatenate([both_pieces(far_dir_ref[...]), blank], 0).T
 
@@ -213,7 +221,7 @@
         return carry
 
     lax.fori_loop(0, STEPS, some_rows, 0)
-    own_ref[...] = folded(tall[...].T[: 2 * RHS], SHARE) + folded(total[...], 4.0 * SHARE)
+    own_ref[...] = folded(tall[...].T[: 2 * RHS], SHARE) + folded(total_ref[...], 4.0 * SHARE)
 
 
 def sums_kernel(
@@ -323,7 +331,6 @@
 def on_device(points, inv_length, direction, residual, solution, active):
     lengths = inv_length.reshape(1, DIM)
     far_pts = permuted(points, to_partner)
-    far_dir = permuted(direction, to_partner)
     swap_pts = permuted(points, swap_core)
     swap_dir = permuted(direction, swap_core)
     swap_res = permuted(residual, swap_core)
@@ -342,6 +349,11 @@
         ],
         "own_start",
     )(points, swap_pts, lengths, direction, swap_dir)
+    later, scale = lax.optimization_barrier((direction, scale))
+    far_dir = permuted(later, to_partner)
+    total, scale = call(
+        early_kernel, [total_shape, (DIM, 128)], "vvvvv", name="own_early"
+    )(left, right, vecs, total, scale)
     back, kernel = call(
         kernel_kernel,
         [whole, (BLOCK, BLOCK)],
@@ -354,15 +366,18 @@
         ],
         "cross_kernel",
     )(left, vecs, far_pts, scale)
+    total, back = call(late_kernel, [total_shape, whole], "vvvvv", name="own_late")(
+        left, right, vecs, total, back
+    )
     back = permuted(back, to_home)
     tall = (BLOCK, 128)
     (own,) = call(
         product_kernel,
         [whole],
-        "vvvvvv",
-        [pltpu.VMEM(tall, BF16), pltpu.VMEM(tall, F32), pltpu.VMEM(*total_shape)],
+        "vvv",
+        [pltpu.VMEM(tall, BF16), pltpu.VMEM(tall, F32)],
         "cross_product",
-    )(kernel, far_dir, left, right, vecs, total)
+    )(kernel, far_dir, total)
     part = own + back
     other = permuted(part, swap_core)
     product, sums = call(sums_kernel, [whole, (128, 1, 128)], "vvvvvvv", name="sums")(

time: 65.4 us -> 62.8 us (0.960)
  blocking collectives: 21.2 us -> 18 us
  starting transfers between devices: 16.4 us -> 17.2 us
    all_to_all x1, blocking collectives: 21.2 us -> 18 us  [over_chips(): return lax.all_to_all(value, AXES, 0, 0, axis_index_groups=groups)]
    ppermute x8, starting transfers between devices: 16.4 us -> 17.2 us  [permuted(): return lax.ppermute(value, AXES, pairs)]
    pallas_call x5 -> x7, Pallas kernels: 22.9 us -> 22.8 us  [placed(): run(*(pltpu.with_memory_space_constraint(a, pltpu.HBM) if i == 'h' else a...]
  transfers between devices with their start and end apart: 8 -> 8, of which waited for: 4 -> 4; matrix products, arithmetic and copies ran while one was open for 0% -> 0% of each run, Pallas kernels for 32% -> 34%
where the time goes in v6:
time: 62.8 us; the launch traced here: 62.6 us
  Pallas kernels  22.8 us (36%)
  blocking collectives  18 us (29%)
  starting transfers between devices  17.2 us (27%)
  waiting for transfers between devices  3.63 us (6%)
  between operations  0.89 us (1%)
    pallas_call x7, Pallas kernels, placed(): run(*(pltpu.with_memory_space_constraint(a, pltpu.HBM) if i == 'h' else a...  22.8 us
    all_to_all x1, blocking collectives, over_chips(): return lax.all_to_all(value, AXES, 0, 0, axis_index_groups=groups)  18 us
    ppermute x8, starting transfers between devices, permuted(): return lax.ppermute(value, AXES, pairs)  17.2 us
    ppermute x8, waiting for transfers between devices, permuted(): return lax.ppermute(value, AXES, pairs)  3.63 us
  transfers between devices with their start and end apart: 8, of which 4 were waited for; matrix products, arithmetic and copies ran while one was open for 0% of the time, Pallas kernels for 34%

profile of v6, /device:TPU:1, one launch (start us, length us, event | category | flops | bytes accessed | tf_op | source)
XLA Modules:
  0.0 62.6 jit_solution(16884161720850786177)
XLA Ops:
  0.6 0.0 copy-start
  0.6 0.0 copy-start.1
  0.7 3.3 %collective-permute-start.1 = (f32[32,2048]{1,0:T(8,128)}, f32[32,2048]{1,0:T(8,128)S(1)}, u32[]{:S(2)}, u32[]{:S(2)}) collective-permute-start(f32[32,2048]{1,0:T(8,128)} %dir_ref.5), channel_id=1, source_target_pairs={{0,2},{1,3},{2,0},{3,1},{4,6},{5,7},{6,4},{7,5},{8,10},{9,11},{10,... | collective-permute-start | bytes 786440 | tf_op jit(solution)/shard_map/ppermute | solution.py:284
  4.0 0.1 collective-permute-start
  4.1 1.0 %collective-permute-start.2 = (f32[32,2048]{1,0:T(8,128)}, f32[32,2048]{1,0:T(8,128)S(1)}, u32[]{:S(2)}, u32[]{:S(2)}) collective-permute-start(f32[32,2048]{1,0:T(8,128)} %pts_ref.1), channel_id=1, source_target_pairs={{0,189},{1,64},{2,194},{3,67},{4,193},{5,68},{6,198},{7,71},{8,197... | collective-permute-start | bytes 786440 | tf_op jit(solution)/shard_map/ppermute | solution.py:284
  5.1 0.3 collective-permute-done.1.swap_dir_ref
  5.4 0.4 collective-permute-done.swap_pts_ref
  5.8 3.2 %own_start.1 = (bf16[2048,256]{1,0:T(8,128)(2,1)S(1)}, bf16[256,2048]{1,0:T(8,128)(2,1)S(1)}, bf16[64,2048]{1,0:T(8,128)(2,1)S(1)}, f32[64,2048]{1,0:T(8,128)S(1)}, f32[32,128]{1,0:T(8,128)S(1)}) custom-call(f32[32,2048]{1,0:T(8,128)} %pts_ref.1, f32[32,2048]{1,0:T(8,128)S(1)} %collective-permute-done.swap_pts_ref, f32[1,32]{1,0:T(1,128)} %bitcast.3, ...), custom_call_target="tpu_custom_call" | custom-call | tf_op jit(solution)/shard_map/own_start/pallas_call | solution.py:326
  9.0 1.1 %collective-permute-start.3 = (f32[32,2048]{1,0:T(8,128)}, f32[32,2048]{1,0:T(8,128)S(1)}, u32[]{:S(2)}, u32[]{:S(2)}) collective-permute-start(f32[32,2048]{1,0:T(8,128)} %dir_ref.5), channel_id=1, source_target_pairs={{0,189},{1,64},{2,194},{3,67},{4,193},{5,68},{6,198},{7,71},{8,197... | collective-permute-start | bytes 786440 | tf_op jit(solution)/shard_map/ppermute | solution.py:284
  10.1 0.0 collective-permute-done.2.far_pts_ref
  10.1 9.6 %cross_kernel.1 = (f32[32,2048]{1,0:T(8,128)S(1)}, f32[2048,2048]{1,0:T(8,128)S(1)}) custom-call(bf16[2048,256]{1,0:T(8,128)(2,1)S(1)} %get-tuple-element.18.left, bf16[64,2048]{1,0:T(8,128)(2,1)S(1)} %get-tuple-element.19.vecs, f32[32,2048]{1,0:T(8,128)S(1)} %collective-permute-done.2.far_pts_ref, f32[32,128]{1,0:T(8,128)S(1)} %get-tuple-element.24.scale_ref), custom_call_target="tpu_custom_call" | custom-call | tf_op jit(solution)/shard_map/cross_kernel/pallas_call | solution.py:326
  19.7 2.6 %own_late.1 = (f32[64,2048]{1,0:T(8,128)S(1)}, f32[32,2048]{1,0:T(8,128)S(1)}) custom-call(bf16[2048,256]{1,0:T(8,128)(2,1)S(1)} %get-tuple-element.18.left, bf16[256,2048]{1,0:T(8,128)(2,1)S(1)} %get-tuple-element.20.right, bf16[64,2048]{1,0:T(8,128)(2,1)S(1)} %get-tuple-element.19.vecs, f32[64,2048]{1,0:T(8,128)S(1)} %get-tuple-element.27.total_in, ...), custom_call_target="tpu_custom_call" | custom-call | tf_op jit(solution)/shard_map/own_late/pallas_call | solution.py:326
  22.3 7.7 %collective-permute-start.4 = (f32[32,2048]{1,0:T(8,128)S(1)}, f32[32,2048]{1,0:T(8,128)S(1)}, u32[]{:S(2)}, u32[]{:S(2)}) collective-permute-start(f32[32,2048]{1,0:T(8,128)S(1)} %get-tuple-element.30), channel_id=1, source_target_pairs={{0,192},{1,70},{2,65},{3,195},{4,196},{5,74},{6,69},{7,199},{8,200... | collective-permute-start | bytes 786440 | tf_op jit(solution)/shard_map/ppermute | solution.py:284
  30.0 2.1 %collective-permute-start.6 = (f32[32,2048]{1,0:T(8,128)}, f32[32,2048]{1,0:T(8,128)S(1)}, u32[]{:S(2)}, u32[]{:S(2)}) collective-permute-start(f32[32,2048]{1,0:T(8,128)} %res_ref.3), channel_id=1, source_target_pairs={{0,2},{1,3},{2,0},{3,1},{4,6},{5,7},{6,4},{7,5},{8,10},{9,11},{10,... | collective-permute-start | bytes 786440 | tf_op jit(solution)/shard_map/ppermute | solution.py:284
  32.1 0.0 collective-permute-done.3.far_dir_ref
  32.1 5.5 %cross_product.1.own_ref = f32[32,2048]{1,0:T(8,128)S(1)} custom-call(f32[2048,2048]{1,0:T(8,128)S(1)} %get-tuple-element.25.kernel_ref, f32[32,2048]{1,0:T(8,128)S(1)} %collective-permute-done.3.far_dir_ref, f32[64,2048]{1,0:T(8,128)S(1)} %get-tuple-element.29.total_ref), custom_call_target="tpu_custom_call" | custom-call | tf_op jit(solution)/shard_map/cross_product/pallas_call | solution.py:326
  37.7 1.8 %collective-permute-done.4.back_ref = f32[32,2048]{1,0:T(8,128)S(1)} collective-permute-done((f32[32,2048]{1,0:T(8,128)S(1)}, f32[32,2048]{1,0:T(8,128)S(1)}, u32[]{:S(2)}, u32[]{:S(2)}) %collective-permute-start.4) | collective-permute-done | bytes 262176 | tf_op jit(solution)/shard_map/ppermute | solution.py:284
  39.5 0.6 collective-permute-start.5
  40.1 0.0 collective-permute-done.6.swap_res_ref
  40.1 1.2 %collective-permute-done.5.other_ref = f32[32,2048]{1,0:T(8,128)S(1)} collective-permute-done((f32[32,2048]{1,0:T(8,128)S(1)}, f32[32,2048]{1,0:T(8,128)S(1)}, u32[]{:S(2)}, u32[]{:S(2)}) %collective-permute-start.5) | collective-permute-done | bytes 262176 | tf_op jit(solution)/shard_map/ppermute | solution.py:284
  41.3 0.4 sums.1
  41.7 1.3 %collective-permute-start.7 = (f32[32,2048]{1,0:T(8,128)S(1)}, f32[32,2048]{1,0:T(8,128)S(1)}, u32[]{:S(2)}, u32[]{:S(2)}) collective-permute-start(f32[32,2048]{1,0:T(8,128)S(1)} %get-tuple-element.32.image_ref), channel_id=1, source_target_pairs={{0,1},{3,2},{4,5},{7,6},{8,9},{11,10},{12,13},{15,14},{16,17},{19,... | collective-permute-start | bytes 786440 | tf_op jit(solution)/shard_map/ppermute | solution.py:284
  43.0 18.0 %all_to_all.5.sums_ref = f32[128,1,128]{2,1,0:T(1,128)S(1)} all-to-all(f32[128,1,128]{2,1,0:T(1,128)S(1)} %get-tuple-element.31), channel_id=1, replica_groups={{0,1,4,5,8,9,12,13,16,17,20,21,24,25,28,29,32,33,36,37,40,41,44,45,48,4..., dimensions={0} | all-to-all | bytes 131072 | tf_op jit(solution)/shard_map/all_to_all | solution.py:309
  61.0 1.4 %update.1 = (f32[32,2048]{1,0:T(8,128)}, f32[32,2048]{1,0:T(8,128)}, f32[32,2048]{1,0:T(8,128)}) custom-call(f32[128,1,128]{2,1,0:T(1,128)S(1)} %all_to_all.5.sums_ref, s32[1,32]{1,0:T(1,128)S(1)} %bitcast.2, f32[32,2048]{1,0:T(8,128)S(1)} %get-tuple-element.32.image_ref, f32[32,2048]{1,0:T(8,128)S(1)} %collective-permute-done.7.other_ref, ...), custom_call_target="tpu_custom_call" | custom-call | tf_op jit(solution)/shard_map/update/pallas_call | solution.py:326
  (9 shorter events, 0.1 us)
Async XLA Ops:
  0.6 40.7 %copy-start = (f32[32,2048]{1,0:T(8,128)S(1)}, f32[32,2048]{1,0:T(8,128)}, u32[]{:S(2)}) copy-start(f32[32,2048]{1,0:T(8,128)} %dir_ref.5) | copy-start | bytes 786436
  0.6 40.6 %copy-start.1 = (f32[32,2048]{1,0:T(8,128)S(1)}, f32[32,2048]{1,0:T(8,128)}, u32[]{:S(2)}) copy-start(f32[32,2048]{1,0:T(8,128)} %res_ref.3) | copy-start | bytes 786436
  0.7 60.4 %copy-start.3 = (s32[32]{0:T(128)S(1)}, s32[32]{0:T(128)}, u32[]{:S(2)}) copy-start(s32[32]{0:T(128)} %param.11) | copy-start | bytes 388
  0.7 60.4 %copy-start.2 = (f32[32,2048]{1,0:T(8,128)S(1)}, f32[32,2048]{1,0:T(8,128)}, u32[]{:S(2)}) copy-start(f32[32,2048]{1,0:T(8,128)} %sol_ref.1) | copy-start | bytes 786436
  0.7 4.7 %collective-permute-start.1 = (f32[32,2048]{1,0:T(8,128)}, f32[32,2048]{1,0:T(8,128)S(1)}, u32[]{:S(2)}, u32[]{:S(2)}) collective-permute-start(f32[32,2048]{1,0:T(8,128)} %dir_ref.5), channel_id=1, source_target_pairs={{0,2},{1,3},{2,0},{3,1},{4,6},{5,7},{6,4},{7,5},{8,10},{9,11},{10,... | collective-permute-start | bytes 786440 | tf_op jit(solution)/shard_map/ppermute | solution.py:284
  4.0 1.7 %collective-permute-start = (f32[32,2048]{1,0:T(8,128)}, f32[32,2048]{1,0:T(8,128)S(1)}, u32[]{:S(2)}, u32[]{:S(2)}) collective-permute-start(f32[32,2048]{1,0:T(8,128)} %pts_ref.1), channel_id=1, source_target_pairs={{0,2},{1,3},{2,0},{3,1},{4,6},{5,7},{6,4},{7,5},{8,10},{9,11},{10,... | collective-permute-start | bytes 786440 | tf_op jit(solution)/shard_map/ppermute | solution.py:284
  4.1 6.0 %collective-permute-start.2 = (f32[32,2048]{1,0:T(8,128)}, f32[32,2048]{1,0:T(8,128)S(1)}, u32[]{:S(2)}, u32[]{:S(2)}) collective-permute-start(f32[32,2048]{1,0:T(8,128)} %pts_ref.1), channel_id=1, source_target_pairs={{0,189},{1,64},{2,194},{3,67},{4,193},{5,68},{6,198},{7,71},{8,197... | collective-permute-start | bytes 786440 | tf_op jit(solution)/shard_map/ppermute | solution.py:284
  9.0 23.1 %collective-permute-start.3 = (f32[32,2048]{1,0:T(8,128)}, f32[32,2048]{1,0:T(8,128)S(1)}, u32[]{:S(2)}, u32[]{:S(2)}) collective-permute-start(f32[32,2048]{1,0:T(8,128)} %dir_ref.5), channel_id=1, source_target_pairs={{0,189},{1,64},{2,194},{3,67},{4,193},{5,68},{6,198},{7,71},{8,197... | collective-permute-start | bytes 786440 | tf_op jit(solution)/shard_map/ppermute | solution.py:284
  22.3 17.2 %collective-permute-start.4 = (f32[32,2048]{1,0:T(8,128)S(1)}, f32[32,2048]{1,0:T(8,128)S(1)}, u32[]{:S(2)}, u32[]{:S(2)}) collective-permute-start(f32[32,2048]{1,0:T(8,128)S(1)} %get-tuple-element.30), channel_id=1, source_target_pairs={{0,192},{1,70},{2,65},{3,195},{4,196},{5,74},{6,69},{7,199},{8,200... | collective-permute-start | bytes 786440 | tf_op jit(solution)/shard_map/ppermute | solution.py:284
  30.0 10.1 %collective-permute-start.6 = (f32[32,2048]{1,0:T(8,128)}, f32[32,2048]{1,0:T(8,128)S(1)}, u32[]{:S(2)}, u32[]{:S(2)}) collective-permute-start(f32[32,2048]{1,0:T(8,128)} %res_ref.3), channel_id=1, source_target_pairs={{0,2},{1,3},{2,0},{3,1},{4,6},{5,7},{6,4},{7,5},{8,10},{9,11},{10,... | collective-permute-start | bytes 786440 | tf_op jit(solution)/shard_map/ppermute | solution.py:284
  39.5 1.8 %collective-permute-start.5 = (f32[32,2048]{1,0:T(8,128)S(1)}, f32[32,2048]{1,0:T(8,128)S(1)}, u32[]{:S(2)}, u32[]{:S(2)}) collective-permute-start(f32[32,2048]{1,0:T(8,128)S(1)} %add.3), channel_id=1, source_target_pairs={{0,2},{1,3},{2,0},{3,1},{4,6},{5,7},{6,4},{7,5},{8,10},{9,11},{10,... | collective-permute-start | bytes 786440 | tf_op jit(solution)/shard_map/ppermute | solution.py:284
  41.7 19.3 %collective-permute-start.7 = (f32[32,2048]{1,0:T(8,128)S(1)}, f32[32,2048]{1,0:T(8,128)S(1)}, u32[]{:S(2)}, u32[]{:S(2)}) collective-permute-start(f32[32,2048]{1,0:T(8,128)S(1)} %get-tuple-element.32.image_ref), channel_id=1, source_target_pairs={{0,1},{3,2},{4,5},{7,6},{8,9},{11,10},{12,13},{15,14},{16,17},{19,... | collective-permute-start | bytes 786440 | tf_op jit(solution)/shard_map/ppermute | solution.py:284

commit v7 on v6

--- a/solution.py
+++ b/solution.py
@@ -8,7 +8,7 @@
 from jax.experimental.pallas import tpu as pltpu
 from jax.sharding import PartitionSpec as P
 
-F32, BF16 = jnp.float32, jnp.bfloat16
+F32, BF16, F8 = jnp.float32, jnp.bfloat16, jnp.float8_e4m3fn
 ROOT_FIVE = math.sqrt(5.0)
 LOG2_E = 1.4426950408889634
 SCALE = ROOT_FIVE * LOG2_E
@@ -19,6 +19,10 @@
 RHS = 32
 TILE = 512
 STEPS = BLOCK // TILE
+WIDTH = 256
+ACROSS = BLOCK // WIDTH
+REST_SCALE = 2.0**14
+LOW_SCALE = 2.0**4
 DEPTH = 256
 AXES = ("blk", "rep")
 NT = (((1,), (1,)), ((), ()))
@@ -110,7 +114,7 @@
 
 
 def waits_longest():
-    return jnp.logical_and(lax.rem(lax.axis_index("blk"), 4) == 2, lax.axis_index("rep") == 1)
+    return jnp.logical_and(lax.rem(lax.axis_index("blk"), 2) == 0, lax.axis_index("rep") == 1)
 
 
 def own_tiles(left, right, vecs, total, first):
@@ -181,7 +185,7 @@
 def kernel_kernel(left, vecs, far_pts_ref, scale_ref, back_ref, kernel_ref, right, total, sq, parts):
     right[...] = right_side(far_pts_ref[...] * scale_ref[:, 0:1])
     total[...] = jnp.zeros_like(total)
-    cols = [slice(c * TILE, (c + 1) * TILE) for c in range(STEPS)]
+    cols = [slice(c * WIDTH, (c + 1) * WIDTH) for c in range(ACROSS)]
 
     def distances(r, c):
         sq[c % 2] = squares(left[span(r), :], right[:, cols[c]])
@@ -192,8 +196,8 @@
     distances(0, 0)
 
     def some_rows(r, carry):
-        for c in range(STEPS):
-            if c + 1 < STEPS:
+        for c in range(ACROSS):
+            if c + 1 < ACROSS:
                 distances(r, c + 1)
             else:
                 distances(jnp.minimum(r + 1, STEPS - 1), 0)
@@ -202,26 +206,38 @@
             parts[c % 2, 0], parts[c % 2, 1] = halves(kernel)
             if c > 0:
                 product(r, c - 1)
-        product(r, STEPS - 1)
+        product(r, ACROSS - 1)
         return carry
 
     lax.fori_loop(0, STEPS, some_rows, 0)
     back_ref[...] = folded(total[...], SHARE)
 
 
-def product_kernel(kernel_ref, far_dir_ref, total_ref, own_ref, far_vecs, tall):
-    blank = jnp.zeros((128 - 2 * RHS, BLOCK), BF16)
-    far_vecs[...] = jnp.concatenate([both_pieces(far_dir_ref[...]), blank], 0).T
+def product_kernel(kernel_ref, far_dir_ref, total_ref, own_ref, far_vecs, far_coarse, tall):
+    vecs = far_dir_ref[...]
+    coarse = vecs.astype(F8).astype(F32)
+    fine = ((vecs - coarse) * LOW_SCALE).astype(F8).astype(F32)
+    columns = jnp.concatenate([part.astype(F32) for part in pieces(vecs, 2)] + [coarse, fine], 0).T
+    far_vecs[...] = columns.astype(BF16)
+    far_coarse[...] = columns.astype(F8)
+    from_head = lax.broadcasted_iota(jnp.int32, (TILE, 128), 1) < 2 * RHS
 
     def some_rows(r, carry):
-        head, rest = halves(kernel_ref[span(r), :])
-        tall[span(r), :] = jnp.dot(head, far_vecs[...], preferred_element_type=F32) + jnp.dot(
-            rest, far_vecs[...], preferred_element_type=F32
+        kernel = kernel_ref[span(r), :]
+        head = kernel.astype(BF16)
+        rest = ((kernel - head.astype(F32)) * REST_SCALE).astype(F8)
+        tall[span(r), :] = jnp.where(
+            from_head,
+            jnp.dot(head, far_vecs[...], preferred_element_type=F32),
+            jnp.dot(rest, far_coarse[...], preferred_element_type=F32),
         )
         return carry
 
     lax.fori_loop(0, STEPS, some_rows, 0)
-    own_ref[...] = folded(tall[...].T[: 2 * RHS], SHARE) + folded(total_ref[...], 4.0 * SHARE)
+    wide = tall[...].T
+    product = folded(wide[: 2 * RHS], SHARE)
+    low = (wide[2 * RHS : 3 * RHS] + wide[3 * RHS :] * (1.0 / LOW_SCALE)) * (SHARE / REST_SCALE)
+    own_ref[...] = (product + low) + folded(total_ref[...], 4.0 * SHARE)
 
 
 def sums_kernel(
@@ -285,9 +301,9 @@
 
 
 def to_partner(block, core, rep):
-    if core == 0:
-        return (block + 32, 0) if rep == 1 else (block - 34, 1)
-    return (block + 32, 1) if rep == 1 else (block - 32, 0)
+    if core == rep:
+        return block + 32, rep
+    return block - 32 - 2 * rep, rep
 
 
 def to_home(block, core, rep):
@@ -361,8 +377,8 @@
         [
             pltpu.VMEM(*right_shape),
             pltpu.VMEM(*total_shape),
-            pltpu.VMEM((2, TILE, TILE), F32),
-            pltpu.VMEM((2, 2, TILE, TILE), BF16),
+            pltpu.VMEM((2, TILE, WIDTH), F32),
+            pltpu.VMEM((2, 2, TILE, WIDTH), BF16),
         ],
         "cross_kernel",
     )(left, vecs, far_pts, scale)
@@ -375,7 +391,7 @@
         product_kernel,
         [whole],
         "vvv",
-        [pltpu.VMEM(tall, BF16), pltpu.VMEM(tall, F32)],
+        [pltpu.VMEM(tall, BF16), pltpu.VMEM(tall, F8), pltpu.VMEM(tall, F32)],
         "cross_product",
     )(kernel, far_dir, total)
     part = own + back

time: 62.8 us -> 61.8 us (0.984)
  waiting for transfers between devices: 3.63 us -> 5.76 us
  Pallas kernels: 22.8 us -> 21.1 us
  starting transfers between devices: 17.2 us -> 16 us
    ppermute x8, waiting for transfers between devices: 3.63 us -> 5.76 us  [permuted(): return lax.ppermute(value, AXES, pairs)]
    pallas_call x7, Pallas kernels: 22.8 us -> 21.1 us  [placed(): run(*(pltpu.with_memory_space_constraint(a, pltpu.HBM) if i == 'h' else a...]
    ppermute x8, starting transfers between devices: 17.2 us -> 16 us  [permuted(): return lax.ppermute(value, AXES, pairs)]
    all_to_all x1, blocking collectives: 18 us -> 17.4 us  [over_chips(): return lax.all_to_all(value, AXES, 0, 0, axis_index_groups=groups)]
  transfers between devices with their start and end apart: 8 -> 8, of which waited for: 4 -> 4; matrix products, arithmetic and copies ran while one was open for 0% -> 0% of each run, Pallas kernels for 34% -> 32%
where the time goes in v7:
time: 61.8 us; the launch traced here: 61.3 us
  Pallas kernels  21.1 us (34%)
  blocking collectives  17.4 us (28%)
  starting transfers between devices  16 us (26%)
  waiting for transfers between devices  5.76 us (9%)
  between operations  0.91 us (1%)
    pallas_call x7, Pallas kernels, placed(): run(*(pltpu.with_memory_space_constraint(a, pltpu.HBM) if i == 'h' else a...  21.1 us
    all_to_all x1, blocking collectives, over_chips(): return lax.all_to_all(value, AXES, 0, 0, axis_index_groups=groups)  17.4 us
    ppermute x8, starting transfers between devices, permuted(): return lax.ppermute(value, AXES, pairs)  16 us
    ppermute x8, waiting for transfers between devices, permuted(): return lax.ppermute(value, AXES, pairs)  5.76 us
  transfers between devices with their start and end apart: 8, of which 4 were waited for; matrix products, arithmetic and copies ran while one was open for 0% of the time, Pallas kernels for 32%

profile of v7, /device:TPU:1, one launch (start us, length us, event | category | flops | bytes accessed | tf_op | source)
XLA Modules:
  0.0 61.3 jit_solution(3982245305362726238)
XLA Ops:
  0.6 0.0 copy-start
  0.6 0.0 copy-start.1
  0.7 3.3 %collective-permute-start.1 = (f32[32,2048]{1,0:T(8,128)}, f32[32,2048]{1,0:T(8,128)S(1)}, u32[]{:S(2)}, u32[]{:S(2)}) collective-permute-start(f32[32,2048]{1,0:T(8,128)} %dir_ref.5), channel_id=1, source_target_pairs={{0,2},{1,3},{2,0},{3,1},{4,6},{5,7},{6,4},{7,5},{8,10},{9,11},{10,... | collective-permute-start | bytes 786440 | tf_op jit(solution)/shard_map/ppermute | solution.py:300
  4.0 0.1 collective-permute-start
  4.1 1.0 %collective-permute-start.2 = (f32[32,2048]{1,0:T(8,128)}, f32[32,2048]{1,0:T(8,128)S(1)}, u32[]{:S(2)}, u32[]{:S(2)}) collective-permute-start(f32[32,2048]{1,0:T(8,128)} %pts_ref.1), channel_id=1, source_target_pairs={{0,64},{1,189},{2,194},{3,67},{4,68},{5,193},{6,198},{7,71},{8,72}... | collective-permute-start | bytes 786440 | tf_op jit(solution)/shard_map/ppermute | solution.py:300
  5.1 0.3 collective-permute-done.1.swap_dir_ref
  5.4 0.4 collective-permute-done.swap_pts_ref
  5.8 3.2 %own_start.1 = (bf16[2048,256]{1,0:T(8,128)(2,1)S(1)}, bf16[256,2048]{1,0:T(8,128)(2,1)S(1)}, bf16[64,2048]{1,0:T(8,128)(2,1)S(1)}, f32[64,2048]{1,0:T(8,128)S(1)}, f32[32,128]{1,0:T(8,128)S(1)}) custom-call(f32[32,2048]{1,0:T(8,128)} %pts_ref.1, f32[32,2048]{1,0:T(8,128)S(1)} %collective-permute-done.swap_pts_ref, f32[1,32]{1,0:T(1,128)} %bitcast.3, ...), custom_call_target="tpu_custom_call" | custom-call | tf_op jit(solution)/shard_map/own_start/pallas_call | solution.py:342
  9.0 1.1 %collective-permute-start.3 = (f32[32,2048]{1,0:T(8,128)}, f32[32,2048]{1,0:T(8,128)S(1)}, u32[]{:S(2)}, u32[]{:S(2)}) collective-permute-start(f32[32,2048]{1,0:T(8,128)} %dir_ref.5), channel_id=1, source_target_pairs={{0,64},{1,189},{2,194},{3,67},{4,68},{5,193},{6,198},{7,71},{8,72}... | collective-permute-start | bytes 786440 | tf_op jit(solution)/shard_map/ppermute | solution.py:300
  10.1 8.8 %cross_kernel.1 = (f32[32,2048]{1,0:T(8,128)S(1)}, f32[2048,2048]{1,0:T(8,128)S(1)}) custom-call(bf16[2048,256]{1,0:T(8,128)(2,1)S(1)} %get-tuple-element.18.left, bf16[64,2048]{1,0:T(8,128)(2,1)S(1)} %get-tuple-element.19.vecs, f32[32,2048]{1,0:T(8,128)S(1)} %collective-permute-done.2.far_pts_ref, f32[32,128]{1,0:T(8,128)S(1)} %get-tuple-element.24.scale_ref), custom_call_target="tpu_custom_call" | custom-call | tf_op jit(solution)/shard_map/cross_kernel/pallas_call | solution.py:342
  18.9 2.6 %own_late.1 = (f32[64,2048]{1,0:T(8,128)S(1)}, f32[32,2048]{1,0:T(8,128)S(1)}) custom-call(bf16[2048,256]{1,0:T(8,128)(2,1)S(1)} %get-tuple-element.18.left, bf16[256,2048]{1,0:T(8,128)(2,1)S(1)} %get-tuple-element.20.right, bf16[64,2048]{1,0:T(8,128)(2,1)S(1)} %get-tuple-element.19.vecs, f32[64,2048]{1,0:T(8,128)S(1)} %get-tuple-element.27.total_in, ...), custom_call_target="tpu_custom_call" | custom-call | tf_op jit(solution)/shard_map/own_late/pallas_call | solution.py:342
  21.5 9.1 %collective-permute-start.4 = (f32[32,2048]{1,0:T(8,128)S(1)}, f32[32,2048]{1,0:T(8,128)S(1)}, u32[]{:S(2)}, u32[]{:S(2)}) collective-permute-start(f32[32,2048]{1,0:T(8,128)S(1)} %get-tuple-element.30), channel_id=1, source_target_pairs={{0,192},{1,70},{2,65},{3,195},{4,196},{5,74},{6,69},{7,199},{8,200... | collective-permute-start | bytes 786440 | tf_op jit(solution)/shard_map/ppermute | solution.py:300
  30.6 0.0 collective-permute-start.6
  30.6 0.0 collective-permute-done.3.far_dir_ref
  30.6 4.7 %cross_product.1.own_ref = f32[32,2048]{1,0:T(8,128)S(1)} custom-call(f32[2048,2048]{1,0:T(8,128)S(1)} %get-tuple-element.25.kernel_ref, f32[32,2048]{1,0:T(8,128)S(1)} %collective-permute-done.3.far_dir_ref, f32[64,2048]{1,0:T(8,128)S(1)} %get-tuple-element.29.total_ref), custom_call_target="tpu_custom_call" | custom-call | tf_op jit(solution)/shard_map/cross_product/pallas_call | solution.py:342
  35.4 3.6 %collective-permute-done.4.back_ref = f32[32,2048]{1,0:T(8,128)S(1)} collective-permute-done((f32[32,2048]{1,0:T(8,128)S(1)}, f32[32,2048]{1,0:T(8,128)S(1)}, u32[]{:S(2)}, u32[]{:S(2)}) %collective-permute-start.4) | collective-permute-done | bytes 262176 | tf_op jit(solution)/shard_map/ppermute | solution.py:300
  39.0 0.1 collective-permute-start.5
  39.1 0.0 collective-permute-done.6.swap_res_ref
  39.1 1.5 %collective-permute-done.5.other_ref = f32[32,2048]{1,0:T(8,128)S(1)} collective-permute-done((f32[32,2048]{1,0:T(8,128)S(1)}, f32[32,2048]{1,0:T(8,128)S(1)}, u32[]{:S(2)}, u32[]{:S(2)}) %collective-permute-start.5) | collective-permute-done | bytes 262176 | tf_op jit(solution)/shard_map/ppermute | solution.py:300
  40.6 0.4 sums.1
  41.0 1.3 %collective-permute-start.7 = (f32[32,2048]{1,0:T(8,128)S(1)}, f32[32,2048]{1,0:T(8,128)S(1)}, u32[]{:S(2)}, u32[]{:S(2)}) collective-permute-start(f32[32,2048]{1,0:T(8,128)S(1)} %get-tuple-element.32.image_ref), channel_id=1, source_target_pairs={{0,1},{3,2},{4,5},{7,6},{8,9},{11,10},{12,13},{15,14},{16,17},{19,... | collective-permute-start | bytes 786440 | tf_op jit(solution)/shard_map/ppermute | solution.py:300
  42.3 17.4 %all_to_all.5.sums_ref = f32[128,1,128]{2,1,0:T(1,128)S(1)} all-to-all(f32[128,1,128]{2,1,0:T(1,128)S(1)} %get-tuple-element.31), channel_id=1, replica_groups={{0,1,4,5,8,9,12,13,16,17,20,21,24,25,28,29,32,33,36,37,40,41,44,45,48,4..., dimensions={0} | all-to-all | bytes 131072 | tf_op jit(solution)/shard_map/all_to_all | solution.py:325
  59.7 0.0 collective-permute-done.7.other_ref
  59.7 1.4 %update.1 = (f32[32,2048]{1,0:T(8,128)}, f32[32,2048]{1,0:T(8,128)}, f32[32,2048]{1,0:T(8,128)}) custom-call(f32[128,1,128]{2,1,0:T(1,128)S(1)} %all_to_all.5.sums_ref, s32[1,32]{1,0:T(1,128)S(1)} %bitcast.2, f32[32,2048]{1,0:T(8,128)S(1)} %get-tuple-element.32.image_ref, f32[32,2048]{1,0:T(8,128)S(1)} %collective-permute-done.7.other_ref, ...), custom_call_target="tpu_custom_call" | custom-call | tf_op jit(solution)/shard_map/update/pallas_call | solution.py:342
  (9 shorter events, 0.1 us)
Async XLA Ops:
  0.6 40.0 %copy-start = (f32[32,2048]{1,0:T(8,128)S(1)}, f32[32,2048]{1,0:T(8,128)}, u32[]{:S(2)}) copy-start(f32[32,2048]{1,0:T(8,128)} %dir_ref.5) | copy-start | bytes 786436
  0.6 40.0 %copy-start.1 = (f32[32,2048]{1,0:T(8,128)S(1)}, f32[32,2048]{1,0:T(8,128)}, u32[]{:S(2)}) copy-start(f32[32,2048]{1,0:T(8,128)} %res_ref.3) | copy-start | bytes 786436
  0.7 59.0 %copy-start.3 = (s32[32]{0:T(128)S(1)}, s32[32]{0:T(128)}, u32[]{:S(2)}) copy-start(s32[32]{0:T(128)} %param.11) | copy-start | bytes 388
  0.7 59.0 %copy-start.2 = (f32[32,2048]{1,0:T(8,128)S(1)}, f32[32,2048]{1,0:T(8,128)}, u32[]{:S(2)}) copy-start(f32[32,2048]{1,0:T(8,128)} %sol_ref.1) | copy-start | bytes 786436
  0.7 4.7 %collective-permute-start.1 = (f32[32,2048]{1,0:T(8,128)}, f32[32,2048]{1,0:T(8,128)S(1)}, u32[]{:S(2)}, u32[]{:S(2)}) collective-permute-start(f32[32,2048]{1,0:T(8,128)} %dir_ref.5), channel_id=1, source_target_pairs={{0,2},{1,3},{2,0},{3,1},{4,6},{5,7},{6,4},{7,5},{8,10},{9,11},{10,... | collective-permute-start | bytes 786440 | tf_op jit(solution)/shard_map/ppermute | solution.py:300
  4.0 1.7 %collective-permute-start = (f32[32,2048]{1,0:T(8,128)}, f32[32,2048]{1,0:T(8,128)S(1)}, u32[]{:S(2)}, u32[]{:S(2)}) collective-permute-start(f32[32,2048]{1,0:T(8,128)} %pts_ref.1), channel_id=1, source_target_pairs={{0,2},{1,3},{2,0},{3,1},{4,6},{5,7},{6,4},{7,5},{8,10},{9,11},{10,... | collective-permute-start | bytes 786440 | tf_op jit(solution)/shard_map/ppermute | solution.py:300
  4.1 6.0 %collective-permute-start.2 = (f32[32,2048]{1,0:T(8,128)}, f32[32,2048]{1,0:T(8,128)S(1)}, u32[]{:S(2)}, u32[]{:S(2)}) collective-permute-start(f32[32,2048]{1,0:T(8,128)} %pts_ref.1), channel_id=1, source_target_pairs={{0,64},{1,189},{2,194},{3,67},{4,68},{5,193},{6,198},{7,71},{8,72}... | collective-permute-start | bytes 786440 | tf_op jit(solution)/shard_map/ppermute | solution.py:300
  9.0 21.6 %collective-permute-start.3 = (f32[32,2048]{1,0:T(8,128)}, f32[32,2048]{1,0:T(8,128)S(1)}, u32[]{:S(2)}, u32[]{:S(2)}) collective-permute-start(f32[32,2048]{1,0:T(8,128)} %dir_ref.5), channel_id=1, source_target_pairs={{0,64},{1,189},{2,194},{3,67},{4,68},{5,193},{6,198},{7,71},{8,72}... | collective-permute-start | bytes 786440 | tf_op jit(solution)/shard_map/ppermute | solution.py:300
  21.5 17.5 %collective-permute-start.4 = (f32[32,2048]{1,0:T(8,128)S(1)}, f32[32,2048]{1,0:T(8,128)S(1)}, u32[]{:S(2)}, u32[]{:S(2)}) collective-permute-start(f32[32,2048]{1,0:T(8,128)S(1)} %get-tuple-element.30), channel_id=1, source_target_pairs={{0,192},{1,70},{2,65},{3,195},{4,196},{5,74},{6,69},{7,199},{8,200... | collective-permute-start | bytes 786440 | tf_op jit(solution)/shard_map/ppermute | solution.py:300
  30.6 8.5 %collective-permute-start.6 = (f32[32,2048]{1,0:T(8,128)}, f32[32,2048]{1,0:T(8,128)S(1)}, u32[]{:S(2)}, u32[]{:S(2)}) collective-permute-start(f32[32,2048]{1,0:T(8,128)} %res_ref.3), channel_id=1, source_target_pairs={{0,2},{1,3},{2,0},{3,1},{4,6},{5,7},{6,4},{7,5},{8,10},{9,11},{10,... | collective-permute-start | bytes 786440 | tf_op jit(solution)/shard_map/ppermute | solution.py:300
  39.0 1.6 %collective-permute-start.5 = (f32[32,2048]{1,0:T(8,128)S(1)}, f32[32,2048]{1,0:T(8,128)S(1)}, u32[]{:S(2)}, u32[]{:S(2)}) collective-permute-start(f32[32,2048]{1,0:T(8,128)S(1)} %add.3), channel_id=1, source_target_pairs={{0,2},{1,3},{2,0},{3,1},{4,6},{5,7},{6,4},{7,5},{8,10},{9,11},{10,... | collective-permute-start | bytes 786440 | tf_op jit(solution)/shard_map/ppermute | solution.py:300
  41.0 18.7 %collective-permute-start.7 = (f32[32,2048]{1,0:T(8,128)S(1)}, f32[32,2048]{1,0:T(8,128)S(1)}, u32[]{:S(2)}, u32[]{:S(2)}) collective-permute-start(f32[32,2048]{1,0:T(8,128)S(1)} %get-tuple-element.32.image_ref), channel_id=1, source_target_pairs={{0,1},{3,2},{4,5},{7,6},{8,9},{11,10},{12,13},{15,14},{16,17},{19,... | collective-permute-start | bytes 786440 | tf_op jit(solution)/shard_map/ppermute | solution.py:300

commit v8 on v7

--- a/solution.py
+++ b/solution.py
@@ -114,7 +114,7 @@
 
 
 def waits_longest():
-    return jnp.logical_and(lax.rem(lax.axis_index("blk"), 2) == 0, lax.axis_index("rep") == 1)
+    return jnp.logical_and(lax.rem(lax.axis_index("blk"), 4) == 2, lax.axis_index("rep") == 1)
 
 
 def own_tiles(left, right, vecs, total, first):
@@ -241,12 +241,12 @@
 
 
 def sums_kernel(
-    own_ref, back_ref, other_ref, dir_ref, swap_dir_ref, res_ref, swap_res_ref, product_ref, sums_ref
+    part_ref, other_ref, dir_ref, swap_dir_ref, res_ref, swap_res_ref, product_ref, sums_ref
 ):
     mine = handles_own_block()
     vecs = jnp.where(mine, dir_ref[...], swap_dir_ref[...])
     res = jnp.where(mine, res_ref[...], swap_res_ref[...])
-    product = (own_ref[...] + back_ref[...]) + other_ref[...]
+    product = part_ref[...] + other_ref[...]
     product_ref[...] = product
     image = product + NOISE * vecs
     lane = lax.broadcasted_iota(jnp.int32, (RHS, 128), 1)
@@ -295,15 +295,18 @@
     for index in range(256):
         block, rep = index // 2, index % 2
         to = change(block, block % 2, rep)
-        if to is not None:
-            pairs.append((index, to[0] % 128 * 2 + to[1]))
+        pairs.append((index, to[0] % 128 * 2 + to[1]))
     return lax.ppermute(value, AXES, pairs)
 
 
 def to_partner(block, core, rep):
     if core == rep:
-        return block + 32, rep
-    return block - 32 - 2 * rep, rep
+        to = (block + 32, rep)
+    else:
+        to = (block - 32 - 2 * rep, rep)
+    if block % 32 == 0:
+        to = (block - 34, 1) if rep == 0 else (block + 32, 0)
+    return to
 
 
 def to_home(block, core, rep):
@@ -316,8 +319,8 @@
     return block ^ 1, rep
 
 
-def to_twin(block, core, rep):
-    return (block, 1 - rep) if core == rep else None
+def swap_rep(block, core, rep):
+    return block, 1 - rep
 
 
 def over_chips(value):
@@ -396,10 +399,10 @@
     )(kernel, far_dir, total)
     part = own + back
     other = permuted(part, swap_core)
-    product, sums = call(sums_kernel, [whole, (128, 1, 128)], "vvvvvvv", name="sums")(
-        own, back, other, direction, swap_dir, residual, swap_res
+    product, sums = call(sums_kernel, [whole, (128, 1, 128)], "vvvvvv", name="sums")(
+        part, other, direction, swap_dir, residual, swap_res
     )
-    twin = permuted(product, to_twin)
+    twin = permuted(product, swap_rep)
     return call(
         update_kernel,
         [whole] * 3,

time: 61.8 us -> 60.1 us (0.972)
  waiting for transfers between devices: 5.76 us -> 4.69 us
    ppermute x8, waiting for transfers between devices: 5.76 us -> 4.69 us  [permuted(): return lax.ppermute(value, AXES, pairs)]
where the time goes in v8:
time: 60.1 us; the launch traced here: 59.9 us
  Pallas kernels  21.1 us (35%)
  blocking collectives  17.3 us (29%)
  starting transfers between devices  15.8 us (26%)
  waiting for transfers between devices  4.69 us (8%)
  between operations  0.89 us (1%)
    pallas_call x7, Pallas kernels, placed(): run(*(pltpu.with_memory_space_constraint(a, pltpu.HBM) if i == 'h' else a...  21.1 us
    all_to_all x1, blocking collectives, over_chips(): return lax.all_to_all(value, AXES, 0, 0, axis_index_groups=groups)  17.3 us
    ppermute x8, starting transfers between devices, permuted(): return lax.ppermute(value, AXES, pairs)  15.8 us
    ppermute x8, waiting for transfers between devices, permuted(): return lax.ppermute(value, AXES, pairs)  4.69 us
  transfers between devices with their start and end apart: 8, of which 4 were waited for; matrix products, arithmetic and copies ran while one was open for 0% of the time, Pallas kernels for 32%

profile of v8, /device:TPU:1, one launch (start us, length us, event | category | flops | bytes accessed | tf_op | source)
XLA Modules:
  0.0 59.9 jit_solution(5789442448770638362)
XLA Ops:
  0.6 0.0 copy-start
  0.6 0.0 copy-start.1
  0.7 3.3 %collective-permute-start.1 = (f32[32,2048]{1,0:T(8,128)}, f32[32,2048]{1,0:T(8,128)S(1)}, u32[]{:S(2)}, u32[]{:S(2)}) collective-permute-start(f32[32,2048]{1,0:T(8,128)} %dir_ref.5), channel_id=1, source_target_pairs={{0,2},{1,3},{2,0},{3,1},{4,6},{5,7},{6,4},{7,5},{8,10},{9,11},{10,... | collective-permute-start | bytes 786440 | tf_op jit(solution)/shard_map/ppermute | solution.py:299
  4.0 0.1 collective-permute-start
  4.1 1.0 %collective-permute-start.2 = (f32[32,2048]{1,0:T(8,128)}, f32[32,2048]{1,0:T(8,128)S(1)}, u32[]{:S(2)}, u32[]{:S(2)}) collective-permute-start(f32[32,2048]{1,0:T(8,128)} %pts_ref.1), channel_id=1, source_target_pairs={{0,189},{1,64},{2,194},{3,67},{4,68},{5,193},{6,198},{7,71},{8,72}... | collective-permute-start | bytes 786440 | tf_op jit(solution)/shard_map/ppermute | solution.py:299
  5.1 0.3 collective-permute-done.1.swap_dir_ref
  5.4 0.4 collective-permute-done.swap_pts_ref
  5.8 3.2 %own_start.1 = (bf16[2048,256]{1,0:T(8,128)(2,1)S(1)}, bf16[256,2048]{1,0:T(8,128)(2,1)S(1)}, bf16[64,2048]{1,0:T(8,128)(2,1)S(1)}, f32[64,2048]{1,0:T(8,128)S(1)}, f32[32,128]{1,0:T(8,128)S(1)}) custom-call(f32[32,2048]{1,0:T(8,128)} %pts_ref.1, f32[32,2048]{1,0:T(8,128)S(1)} %collective-permute-done.swap_pts_ref, f32[1,32]{1,0:T(1,128)} %bitcast.3, ...), custom_call_target="tpu_custom_call" | custom-call | tf_op jit(solution)/shard_map/own_start/pallas_call | solution.py:345
  9.0 1.1 %collective-permute-start.3 = (f32[32,2048]{1,0:T(8,128)}, f32[32,2048]{1,0:T(8,128)S(1)}, u32[]{:S(2)}, u32[]{:S(2)}) collective-permute-start(f32[32,2048]{1,0:T(8,128)} %dir_ref.5), channel_id=1, source_target_pairs={{0,189},{1,64},{2,194},{3,67},{4,68},{5,193},{6,198},{7,71},{8,72}... | collective-permute-start | bytes 786440 | tf_op jit(solution)/shard_map/ppermute | solution.py:299
  10.1 0.0 collective-permute-done.2.far_pts_ref
  10.1 8.8 %cross_kernel.1 = (f32[32,2048]{1,0:T(8,128)S(1)}, f32[2048,2048]{1,0:T(8,128)S(1)}) custom-call(bf16[2048,256]{1,0:T(8,128)(2,1)S(1)} %get-tuple-element.18.left, bf16[64,2048]{1,0:T(8,128)(2,1)S(1)} %get-tuple-element.19.vecs, f32[32,2048]{1,0:T(8,128)S(1)} %collective-permute-done.2.far_pts_ref, f32[32,128]{1,0:T(8,128)S(1)} %get-tuple-element.24.scale_ref), custom_call_target="tpu_custom_call" | custom-call | tf_op jit(solution)/shard_map/cross_kernel/pallas_call | solution.py:345
  18.9 2.6 %own_late.1 = (f32[64,2048]{1,0:T(8,128)S(1)}, f32[32,2048]{1,0:T(8,128)S(1)}) custom-call(bf16[2048,256]{1,0:T(8,128)(2,1)S(1)} %get-tuple-element.18.left, bf16[256,2048]{1,0:T(8,128)(2,1)S(1)} %get-tuple-element.20.right, bf16[64,2048]{1,0:T(8,128)(2,1)S(1)} %get-tuple-element.19.vecs, f32[64,2048]{1,0:T(8,128)S(1)} %get-tuple-element.27.total_in, ...), custom_call_target="tpu_custom_call" | custom-call | tf_op jit(solution)/shard_map/own_late/pallas_call | solution.py:345
  21.5 7.7 %collective-permute-start.4 = (f32[32,2048]{1,0:T(8,128)S(1)}, f32[32,2048]{1,0:T(8,128)S(1)}, u32[]{:S(2)}, u32[]{:S(2)}) collective-permute-start(f32[32,2048]{1,0:T(8,128)S(1)} %get-tuple-element.30), channel_id=1, source_target_pairs={{0,192},{1,70},{2,65},{3,195},{4,196},{5,74},{6,69},{7,199},{8,200... | collective-permute-start | bytes 786440 | tf_op jit(solution)/shard_map/ppermute | solution.py:299
  29.2 1.9 %collective-permute-start.6 = (f32[32,2048]{1,0:T(8,128)}, f32[32,2048]{1,0:T(8,128)S(1)}, u32[]{:S(2)}, u32[]{:S(2)}) collective-permute-start(f32[32,2048]{1,0:T(8,128)} %res_ref.3), channel_id=1, source_target_pairs={{0,2},{1,3},{2,0},{3,1},{4,6},{5,7},{6,4},{7,5},{8,10},{9,11},{10,... | collective-permute-start | bytes 786440 | tf_op jit(solution)/shard_map/ppermute | solution.py:299
  31.1 0.0 collective-permute-done.3.far_dir_ref
  31.1 4.7 %cross_product.1 = f32[32,2048]{1,0:T(8,128)S(1)} custom-call(f32[2048,2048]{1,0:T(8,128)S(1)} %get-tuple-element.25.kernel_ref, f32[32,2048]{1,0:T(8,128)S(1)} %collective-permute-done.3.far_dir_ref, f32[64,2048]{1,0:T(8,128)S(1)} %get-tuple-element.29.total_ref), custom_call_target="tpu_custom_call" | custom-call | tf_op jit(solution)/shard_map/cross_product/pallas_call | solution.py:345
  35.8 2.9 %collective-permute-done.4 = f32[32,2048]{1,0:T(8,128)S(1)} collective-permute-done((f32[32,2048]{1,0:T(8,128)S(1)}, f32[32,2048]{1,0:T(8,128)S(1)}, u32[]{:S(2)}, u32[]{:S(2)}) %collective-permute-start.4) | collective-permute-done | bytes 262176 | tf_op jit(solution)/shard_map/ppermute | solution.py:299
  38.7 0.6 %collective-permute-start.5 = (f32[32,2048]{1,0:T(8,128)S(1)}, f32[32,2048]{1,0:T(8,128)S(1)}, u32[]{:S(2)}, u32[]{:S(2)}) collective-permute-start(f32[32,2048]{1,0:T(8,128)S(1)} %add.3.part_ref), channel_id=1, source_target_pairs={{0,2},{1,3},{2,0},{3,1},{4,6},{5,7},{6,4},{7,5},{8,10},{9,11},{10,... | collective-permute-start | bytes 786440 | tf_op jit(solution)/shard_map/ppermute | solution.py:299
  39.3 0.0 collective-permute-done.6.swap_res_ref
  39.3 1.2 %collective-permute-done.5.other_ref = f32[32,2048]{1,0:T(8,128)S(1)} collective-permute-done((f32[32,2048]{1,0:T(8,128)S(1)}, f32[32,2048]{1,0:T(8,128)S(1)}, u32[]{:S(2)}, u32[]{:S(2)}) %collective-permute-start.5) | collective-permute-done | bytes 262176 | tf_op jit(solution)/shard_map/ppermute | solution.py:299
  40.5 0.4 sums.1
  40.9 0.1 collective-permute-start.7
  41.0 17.3 %all_to_all.5.sums_ref = f32[128,1,128]{2,1,0:T(1,128)S(1)} all-to-all(f32[128,1,128]{2,1,0:T(1,128)S(1)} %get-tuple-element.31), channel_id=1, replica_groups={{0,1,4,5,8,9,12,13,16,17,20,21,24,25,28,29,32,33,36,37,40,41,44,45,48,4..., dimensions={0} | all-to-all | bytes 131072 | tf_op jit(solution)/shard_map/all_to_all | solution.py:328
  58.3 1.4 %update.1 = (f32[32,2048]{1,0:T(8,128)}, f32[32,2048]{1,0:T(8,128)}, f32[32,2048]{1,0:T(8,128)}) custom-call(f32[128,1,128]{2,1,0:T(1,128)S(1)} %all_to_all.5.sums_ref, s32[1,32]{1,0:T(1,128)S(1)} %bitcast.2, f32[32,2048]{1,0:T(8,128)S(1)} %get-tuple-element.32.image_ref, f32[32,2048]{1,0:T(8,128)S(1)} %collective-permute-done.7.other_ref, ...), custom_call_target="tpu_custom_call" | custom-call | tf_op jit(solution)/shard_map/update/pallas_call | solution.py:345
  (9 shorter events, 0.1 us)
Async XLA Ops:
  0.6 39.9 %copy-start = (f32[32,2048]{1,0:T(8,128)S(1)}, f32[32,2048]{1,0:T(8,128)}, u32[]{:S(2)}) copy-start(f32[32,2048]{1,0:T(8,128)} %dir_ref.5) | copy-start | bytes 786436
  0.6 39.9 %copy-start.1 = (f32[32,2048]{1,0:T(8,128)S(1)}, f32[32,2048]{1,0:T(8,128)}, u32[]{:S(2)}) copy-start(f32[32,2048]{1,0:T(8,128)} %res_ref.3) | copy-start | bytes 786436
  0.7 57.7 %copy-start.3 = (s32[32]{0:T(128)S(1)}, s32[32]{0:T(128)}, u32[]{:S(2)}) copy-start(s32[32]{0:T(128)} %param.11) | copy-start | bytes 388
  0.7 57.7 %copy-start.2 = (f32[32,2048]{1,0:T(8,128)S(1)}, f32[32,2048]{1,0:T(8,128)}, u32[]{:S(2)}) copy-start(f32[32,2048]{1,0:T(8,128)} %sol_ref.1) | copy-start | bytes 786436
  0.7 4.7 %collective-permute-start.1 = (f32[32,2048]{1,0:T(8,128)}, f32[32,2048]{1,0:T(8,128)S(1)}, u32[]{:S(2)}, u32[]{:S(2)}) collective-permute-start(f32[32,2048]{1,0:T(8,128)} %dir_ref.5), channel_id=1, source_target_pairs={{0,2},{1,3},{2,0},{3,1},{4,6},{5,7},{6,4},{7,5},{8,10},{9,11},{10,... | collective-permute-start | bytes 786440 | tf_op jit(solution)/shard_map/ppermute | solution.py:299
  4.0 1.7 %collective-permute-start = (f32[32,2048]{1,0:T(8,128)}, f32[32,2048]{1,0:T(8,128)S(1)}, u32[]{:S(2)}, u32[]{:S(2)}) collective-permute-start(f32[32,2048]{1,0:T(8,128)} %pts_ref.1), channel_id=1, source_target_pairs={{0,2},{1,3},{2,0},{3,1},{4,6},{5,7},{6,4},{7,5},{8,10},{9,11},{10,... | collective-permute-start | bytes 786440 | tf_op jit(solution)/shard_map/ppermute | solution.py:299
  4.1 6.0 %collective-permute-start.2 = (f32[32,2048]{1,0:T(8,128)}, f32[32,2048]{1,0:T(8,128)S(1)}, u32[]{:S(2)}, u32[]{:S(2)}) collective-permute-start(f32[32,2048]{1,0:T(8,128)} %pts_ref.1), channel_id=1, source_target_pairs={{0,189},{1,64},{2,194},{3,67},{4,68},{5,193},{6,198},{7,71},{8,72}... | collective-permute-start | bytes 786440 | tf_op jit(solution)/shard_map/ppermute | solution.py:299
  9.0 22.1 %collective-permute-start.3 = (f32[32,2048]{1,0:T(8,128)}, f32[32,2048]{1,0:T(8,128)S(1)}, u32[]{:S(2)}, u32[]{:S(2)}) collective-permute-start(f32[32,2048]{1,0:T(8,128)} %dir_ref.5), channel_id=1, source_target_pairs={{0,189},{1,64},{2,194},{3,67},{4,68},{5,193},{6,198},{7,71},{8,72}... | collective-permute-start | bytes 786440 | tf_op jit(solution)/shard_map/ppermute | solution.py:299
  21.5 17.2 %collective-permute-start.4 = (f32[32,2048]{1,0:T(8,128)S(1)}, f32[32,2048]{1,0:T(8,128)S(1)}, u32[]{:S(2)}, u32[]{:S(2)}) collective-permute-start(f32[32,2048]{1,0:T(8,128)S(1)} %get-tuple-element.30), channel_id=1, source_target_pairs={{0,192},{1,70},{2,65},{3,195},{4,196},{5,74},{6,69},{7,199},{8,200... | collective-permute-start | bytes 786440 | tf_op jit(solution)/shard_map/ppermute | solution.py:299
  29.2 10.1 %collective-permute-start.6 = (f32[32,2048]{1,0:T(8,128)}, f32[32,2048]{1,0:T(8,128)S(1)}, u32[]{:S(2)}, u32[]{:S(2)}) collective-permute-start(f32[32,2048]{1,0:T(8,128)} %res_ref.3), channel_id=1, source_target_pairs={{0,2},{1,3},{2,0},{3,1},{4,6},{5,7},{6,4},{7,5},{8,10},{9,11},{10,... | collective-permute-start | bytes 786440 | tf_op jit(solution)/shard_map/ppermute | solution.py:299
  38.7 1.8 %collective-permute-start.5 = (f32[32,2048]{1,0:T(8,128)S(1)}, f32[32,2048]{1,0:T(8,128)S(1)}, u32[]{:S(2)}, u32[]{:S(2)}) collective-permute-start(f32[32,2048]{1,0:T(8,128)S(1)} %add.3.part_ref), channel_id=1, source_target_pairs={{0,2},{1,3},{2,0},{3,1},{4,6},{5,7},{6,4},{7,5},{8,10},{9,11},{10,... | collective-permute-start | bytes 786440 | tf_op jit(solution)/shard_map/ppermute | solution.py:299
  40.9 17.4 %collective-permute-start.7 = (f32[32,2048]{1,0:T(8,128)S(1)}, f32[32,2048]{1,0:T(8,128)S(1)}, u32[]{:S(2)}, u32[]{:S(2)}) collective-permute-start(f32[32,2048]{1,0:T(8,128)S(1)} %get-tuple-element.32.image_ref), channel_id=1, source_target_pairs={{0,1},{1,0},{2,3},{3,2},{4,5},{5,4},{6,7},{7,6},{8,9},{9,8},{10,11... | collective-permute-start | bytes 786440 | tf_op jit(solution)/shard_map/ppermute | solution.py:299

commit v9 on v8

--- a/solution.py
+++ b/solution.py
@@ -324,7 +324,11 @@
 
 
 def over_chips(value):
-    groups = [[block * 2 + rep for block in range(core, 128, 2) for rep in range(2)] for core in range(2)]
+    def hops(k):
+        x, z, y = k % 4, k // 4 % 8, k // 32
+        return -(min(x, 4 - x) + min(y, 4 - y) + min(z, 8 - z)), -k
+
+    groups = [[k // 2 * 4 + core * 2 + k % 2 for k in sorted(range(128), key=hops)] for core in range(2)]
     return lax.all_to_all(value, AXES, 0, 0, axis_index_groups=groups)
 
 

time: 60.1 us -> 58.4 us (0.972)
  blocking collectives: 17.3 us -> 15.2 us
    all_to_all x1, blocking collectives: 17.3 us -> 15.2 us  [over_chips(): return lax.all_to_all(value, AXES, 0, 0, axis_index_groups=groups)]
  transfers between devices with their start and end apart: 8 -> 8, of which waited for: 4 -> 4; matrix products, arithmetic and copies ran while one was open for 0% -> 0% of each run, Pallas kernels for 32% -> 34%
where the time goes in v9:
time: 58.4 us; the launch traced here: 57.7 us
  Pallas kernels  21.1 us (36%)
  starting transfers between devices  15.8 us (27%)
  blocking collectives  15.2 us (26%)
  waiting for transfers between devices  4.69 us (8%)
  between operations  0.89 us (2%)
    pallas_call x7, Pallas kernels, placed(): run(*(pltpu.with_memory_space_constraint(a, pltpu.HBM) if i == 'h' else a...  21.1 us
    ppermute x8, starting transfers between devices, permuted(): return lax.ppermute(value, AXES, pairs)  15.8 us
    all_to_all x1, blocking collectives, over_chips(): return lax.all_to_all(value, AXES, 0, 0, axis_index_groups=groups)  15.2 us
    ppermute x8, waiting for transfers between devices, permuted(): return lax.ppermute(value, AXES, pairs)  4.69 us
  transfers between devices with their start and end apart: 8, of which 4 were waited for; matrix products, arithmetic and copies ran while one was open for 0% of the time, Pallas kernels for 34%

profile of v9, /device:TPU:1, one launch (start us, length us, event | category | flops | bytes accessed | tf_op | source)
XLA Modules:
  0.0 57.7 jit_solution(14620369464911685131)
XLA Ops:
  0.6 0.0 copy-start
  0.6 0.0 copy-start.1
  0.7 3.3 %collective-permute-start.1 = (f32[32,2048]{1,0:T(8,128)}, f32[32,2048]{1,0:T(8,128)S(1)}, u32[]{:S(2)}, u32[]{:S(2)}) collective-permute-start(f32[32,2048]{1,0:T(8,128)} %dir_ref.5), channel_id=1, source_target_pairs={{0,2},{1,3},{2,0},{3,1},{4,6},{5,7},{6,4},{7,5},{8,10},{9,11},{10,... | collective-permute-start | bytes 786440 | tf_op jit(solution)/shard_map/ppermute | solution.py:299
  4.0 0.1 collective-permute-start
  4.1 1.0 %collective-permute-start.2 = (f32[32,2048]{1,0:T(8,128)}, f32[32,2048]{1,0:T(8,128)S(1)}, u32[]{:S(2)}, u32[]{:S(2)}) collective-permute-start(f32[32,2048]{1,0:T(8,128)} %pts_ref.1), channel_id=1, source_target_pairs={{0,189},{1,64},{2,194},{3,67},{4,68},{5,193},{6,198},{7,71},{8,72}... | collective-permute-start | bytes 786440 | tf_op jit(solution)/shard_map/ppermute | solution.py:299
  5.1 0.3 collective-permute-done.1.swap_dir_ref
  5.4 0.4 collective-permute-done.swap_pts_ref
  5.8 3.2 %own_start.1 = (bf16[2048,256]{1,0:T(8,128)(2,1)S(1)}, bf16[256,2048]{1,0:T(8,128)(2,1)S(1)}, bf16[64,2048]{1,0:T(8,128)(2,1)S(1)}, f32[64,2048]{1,0:T(8,128)S(1)}, f32[32,128]{1,0:T(8,128)S(1)}) custom-call(f32[32,2048]{1,0:T(8,128)} %pts_ref.1, f32[32,2048]{1,0:T(8,128)S(1)} %collective-permute-done.swap_pts_ref, f32[1,32]{1,0:T(1,128)} %bitcast.3, ...), custom_call_target="tpu_custom_call" | custom-call | tf_op jit(solution)/shard_map/own_start/pallas_call | solution.py:349
  9.0 1.1 %collective-permute-start.3 = (f32[32,2048]{1,0:T(8,128)}, f32[32,2048]{1,0:T(8,128)S(1)}, u32[]{:S(2)}, u32[]{:S(2)}) collective-permute-start(f32[32,2048]{1,0:T(8,128)} %dir_ref.5), channel_id=1, source_target_pairs={{0,189},{1,64},{2,194},{3,67},{4,68},{5,193},{6,198},{7,71},{8,72}... | collective-permute-start | bytes 786440 | tf_op jit(solution)/shard_map/ppermute | solution.py:299
  10.1 0.0 collective-permute-done.2.far_pts_ref
  10.1 8.8 %cross_kernel.1 = (f32[32,2048]{1,0:T(8,128)S(1)}, f32[2048,2048]{1,0:T(8,128)S(1)}) custom-call(bf16[2048,256]{1,0:T(8,128)(2,1)S(1)} %get-tuple-element.18.left, bf16[64,2048]{1,0:T(8,128)(2,1)S(1)} %get-tuple-element.19.vecs, f32[32,2048]{1,0:T(8,128)S(1)} %collective-permute-done.2.far_pts_ref, f32[32,128]{1,0:T(8,128)S(1)} %get-tuple-element.24.scale_ref), custom_call_target="tpu_custom_call" | custom-call | tf_op jit(solution)/shard_map/cross_kernel/pallas_call | solution.py:349
  18.9 2.6 %own_late.1 = (f32[64,2048]{1,0:T(8,128)S(1)}, f32[32,2048]{1,0:T(8,128)S(1)}) custom-call(bf16[2048,256]{1,0:T(8,128)(2,1)S(1)} %get-tuple-element.18.left, bf16[256,2048]{1,0:T(8,128)(2,1)S(1)} %get-tuple-element.20.right, bf16[64,2048]{1,0:T(8,128)(2,1)S(1)} %get-tuple-element.19.vecs, f32[64,2048]{1,0:T(8,128)S(1)} %get-tuple-element.27.total_in, ...), custom_call_target="tpu_custom_call" | custom-call | tf_op jit(solution)/shard_map/own_late/pallas_call | solution.py:349
  21.5 7.7 %collective-permute-start.4 = (f32[32,2048]{1,0:T(8,128)S(1)}, f32[32,2048]{1,0:T(8,128)S(1)}, u32[]{:S(2)}, u32[]{:S(2)}) collective-permute-start(f32[32,2048]{1,0:T(8,128)S(1)} %get-tuple-element.30), channel_id=1, source_target_pairs={{0,192},{1,70},{2,65},{3,195},{4,196},{5,74},{6,69},{7,199},{8,200... | collective-permute-start | bytes 786440 | tf_op jit(solution)/shard_map/ppermute | solution.py:299
  29.2 1.9 %collective-permute-start.6 = (f32[32,2048]{1,0:T(8,128)}, f32[32,2048]{1,0:T(8,128)S(1)}, u32[]{:S(2)}, u32[]{:S(2)}) collective-permute-start(f32[32,2048]{1,0:T(8,128)} %res_ref.3), channel_id=1, source_target_pairs={{0,2},{1,3},{2,0},{3,1},{4,6},{5,7},{6,4},{7,5},{8,10},{9,11},{10,... | collective-permute-start | bytes 786440 | tf_op jit(solution)/shard_map/ppermute | solution.py:299
  31.1 0.0 collective-permute-done.3.far_dir_ref
  31.1 4.7 %cross_product.1 = f32[32,2048]{1,0:T(8,128)S(1)} custom-call(f32[2048,2048]{1,0:T(8,128)S(1)} %get-tuple-element.25.kernel_ref, f32[32,2048]{1,0:T(8,128)S(1)} %collective-permute-done.3.far_dir_ref, f32[64,2048]{1,0:T(8,128)S(1)} %get-tuple-element.29.total_ref), custom_call_target="tpu_custom_call" | custom-call | tf_op jit(solution)/shard_map/cross_product/pallas_call | solution.py:349
  35.8 2.9 %collective-permute-done.4 = f32[32,2048]{1,0:T(8,128)S(1)} collective-permute-done((f32[32,2048]{1,0:T(8,128)S(1)}, f32[32,2048]{1,0:T(8,128)S(1)}, u32[]{:S(2)}, u32[]{:S(2)}) %collective-permute-start.4) | collective-permute-done | bytes 262176 | tf_op jit(solution)/shard_map/ppermute | solution.py:299
  38.7 0.6 %collective-permute-start.5 = (f32[32,2048]{1,0:T(8,128)S(1)}, f32[32,2048]{1,0:T(8,128)S(1)}, u32[]{:S(2)}, u32[]{:S(2)}) collective-permute-start(f32[32,2048]{1,0:T(8,128)S(1)} %add.3.part_ref), channel_id=1, source_target_pairs={{0,2},{1,3},{2,0},{3,1},{4,6},{5,7},{6,4},{7,5},{8,10},{9,11},{10,... | collective-permute-start | bytes 786440 | tf_op jit(solution)/shard_map/ppermute | solution.py:299
  39.3 0.0 collective-permute-done.6.swap_res_ref
  39.3 1.2 %collective-permute-done.5.other_ref = f32[32,2048]{1,0:T(8,128)S(1)} collective-permute-done((f32[32,2048]{1,0:T(8,128)S(1)}, f32[32,2048]{1,0:T(8,128)S(1)}, u32[]{:S(2)}, u32[]{:S(2)}) %collective-permute-start.5) | collective-permute-done | bytes 262176 | tf_op jit(solution)/shard_map/ppermute | solution.py:299
  40.5 0.4 sums.1
  40.9 0.1 collective-permute-start.7
  41.0 15.2 %all_to_all.5.sums_ref = f32[128,1,128]{2,1,0:T(1,128)S(1)} all-to-all(f32[128,1,128]{2,1,0:T(1,128)S(1)} %get-tuple-element.31), channel_id=1, replica_groups={{164,228,172,165,161,156,100,236,229,225,220,180,173,169,160,157,153,14..., dimensions={0} | all-to-all | bytes 131072 | tf_op jit(solution)/shard_map/all_to_all | solution.py:332
  56.2 1.4 %update.1 = (f32[32,2048]{1,0:T(8,128)}, f32[32,2048]{1,0:T(8,128)}, f32[32,2048]{1,0:T(8,128)}) custom-call(f32[128,1,128]{2,1,0:T(1,128)S(1)} %all_to_all.5.sums_ref, s32[1,32]{1,0:T(1,128)S(1)} %bitcast.2, f32[32,2048]{1,0:T(8,128)S(1)} %get-tuple-element.32.image_ref, f32[32,2048]{1,0:T(8,128)S(1)} %collective-permute-done.7.other_ref, ...), custom_call_target="tpu_custom_call" | custom-call | tf_op jit(solution)/shard_map/update/pallas_call | solution.py:349
  (9 shorter events, 0.1 us)
Async XLA Ops:
  0.6 39.9 %copy-start = (f32[32,2048]{1,0:T(8,128)S(1)}, f32[32,2048]{1,0:T(8,128)}, u32[]{:S(2)}) copy-start(f32[32,2048]{1,0:T(8,128)} %dir_ref.5) | copy-start | bytes 786436
  0.6 39.9 %copy-start.1 = (f32[32,2048]{1,0:T(8,128)S(1)}, f32[32,2048]{1,0:T(8,128)}, u32[]{:S(2)}) copy-start(f32[32,2048]{1,0:T(8,128)} %res_ref.3) | copy-start | bytes 786436
  0.7 55.5 %copy-start.3 = (s32[32]{0:T(128)S(1)}, s32[32]{0:T(128)}, u32[]{:S(2)}) copy-start(s32[32]{0:T(128)} %param.11) | copy-start | bytes 388
  0.7 55.5 %copy-start.2 = (f32[32,2048]{1,0:T(8,128)S(1)}, f32[32,2048]{1,0:T(8,128)}, u32[]{:S(2)}) copy-start(f32[32,2048]{1,0:T(8,128)} %sol_ref.1) | copy-start | bytes 786436
  0.7 4.7 %collective-permute-start.1 = (f32[32,2048]{1,0:T(8,128)}, f32[32,2048]{1,0:T(8,128)S(1)}, u32[]{:S(2)}, u32[]{:S(2)}) collective-permute-start(f32[32,2048]{1,0:T(8,128)} %dir_ref.5), channel_id=1, source_target_pairs={{0,2},{1,3},{2,0},{3,1},{4,6},{5,7},{6,4},{7,5},{8,10},{9,11},{10,... | collective-permute-start | bytes 786440 | tf_op jit(solution)/shard_map/ppermute | solution.py:299
  4.0 1.7 %collective-permute-start = (f32[32,2048]{1,0:T(8,128)}, f32[32,2048]{1,0:T(8,128)S(1)}, u32[]{:S(2)}, u32[]{:S(2)}) collective-permute-start(f32[32,2048]{1,0:T(8,128)} %pts_ref.1), channel_id=1, source_target_pairs={{0,2},{1,3},{2,0},{3,1},{4,6},{5,7},{6,4},{7,5},{8,10},{9,11},{10,... | collective-permute-start | bytes 786440 | tf_op jit(solution)/shard_map/ppermute | solution.py:299
  4.1 6.0 %collective-permute-start.2 = (f32[32,2048]{1,0:T(8,128)}, f32[32,2048]{1,0:T(8,128)S(1)}, u32[]{:S(2)}, u32[]{:S(2)}) collective-permute-start(f32[32,2048]{1,0:T(8,128)} %pts_ref.1), channel_id=1, source_target_pairs={{0,189},{1,64},{2,194},{3,67},{4,68},{5,193},{6,198},{7,71},{8,72}... | collective-permute-start | bytes 786440 | tf_op jit(solution)/shard_map/ppermute | solution.py:299
  9.0 22.1 %collective-permute-start.3 = (f32[32,2048]{1,0:T(8,128)}, f32[32,2048]{1,0:T(8,128)S(1)}, u32[]{:S(2)}, u32[]{:S(2)}) collective-permute-start(f32[32,2048]{1,0:T(8,128)} %dir_ref.5), channel_id=1, source_target_pairs={{0,189},{1,64},{2,194},{3,67},{4,68},{5,193},{6,198},{7,71},{8,72}... | collective-permute-start | bytes 786440 | tf_op jit(solution)/shard_map/ppermute | solution.py:299
  21.5 17.2 %collective-permute-start.4 = (f32[32,2048]{1,0:T(8,128)S(1)}, f32[32,2048]{1,0:T(8,128)S(1)}, u32[]{:S(2)}, u32[]{:S(2)}) collective-permute-start(f32[32,2048]{1,0:T(8,128)S(1)} %get-tuple-element.30), channel_id=1, source_target_pairs={{0,192},{1,70},{2,65},{3,195},{4,196},{5,74},{6,69},{7,199},{8,200... | collective-permute-start | bytes 786440 | tf_op jit(solution)/shard_map/ppermute | solution.py:299
  29.2 10.1 %collective-permute-start.6 = (f32[32,2048]{1,0:T(8,128)}, f32[32,2048]{1,0:T(8,128)S(1)}, u32[]{:S(2)}, u32[]{:S(2)}) collective-permute-start(f32[32,2048]{1,0:T(8,128)} %res_ref.3), channel_id=1, source_target_pairs={{0,2},{1,3},{2,0},{3,1},{4,6},{5,7},{6,4},{7,5},{8,10},{9,11},{10,... | collective-permute-start | bytes 786440 | tf_op jit(solution)/shard_map/ppermute | solution.py:299
  38.7 1.8 %collective-permute-start.5 = (f32[32,2048]{1,0:T(8,128)S(1)}, f32[32,2048]{1,0:T(8,128)S(1)}, u32[]{:S(2)}, u32[]{:S(2)}) collective-permute-start(f32[32,2048]{1,0:T(8,128)S(1)} %add.3.part_ref), channel_id=1, source_target_pairs={{0,2},{1,3},{2,0},{3,1},{4,6},{5,7},{6,4},{7,5},{8,10},{9,11},{10,... | collective-permute-start | bytes 786440 | tf_op jit(solution)/shard_map/ppermute | solution.py:299
  40.9 15.3 %collective-permute-start.7 = (f32[32,2048]{1,0:T(8,128)S(1)}, f32[32,2048]{1,0:T(8,128)S(1)}, u32[]{:S(2)}, u32[]{:S(2)}) collective-permute-start(f32[32,2048]{1,0:T(8,128)S(1)} %get-tuple-element.32.image_ref), channel_id=1, source_target_pairs={{0,1},{1,0},{2,3},{3,2},{4,5},{5,4},{6,7},{7,6},{8,9},{9,8},{10,11... | collective-permute-start | bytes 786440 | tf_op jit(solution)/shard_map/ppermute | solution.py:299

commit v10 on v9

--- a/solution.py
+++ b/solution.py
@@ -20,6 +20,7 @@
 TILE = 512
 STEPS = BLOCK // TILE
 WIDTH = 256
+HEIGHT = 1024
 ACROSS = BLOCK // WIDTH
 REST_SCALE = 2.0**14
 LOW_SCALE = 2.0**4
@@ -43,7 +44,7 @@
 
 def left_side(points):
     n = points.shape[1]
-    p = pieces(points, 3)
+    p = [(-2.0 * part.astype(F32)).astype(BF16) for part in pieces(points, 3)]
     m = norm_rows(points)
     row = lax.broadcasted_iota(jnp.int32, (16, n), 0)
     tail = jnp.where(row < 6, 1.0, 0.0)
@@ -55,7 +56,7 @@
 
 def right_side(points):
     n = points.shape[1]
-    p = [(-2.0 * part.astype(F32)).astype(BF16) for part in pieces(points, 3)]
+    p = pieces(points, 3)
     m = norm_rows(points)
     row = lax.broadcasted_iota(jnp.int32, (16, n), 0)
     tail = jnp.where(row < 3, 1.0, 0.0)
@@ -99,6 +100,10 @@
     return pl.ds(pl.multiple_of(index * TILE, TILE), TILE)
 
 
+def tall_span(index):
+    return pl.ds(pl.multiple_of(index * HEIGHT, HEIGHT), HEIGHT)
+
+
 def as_column(row):
     n = row.shape[1]
     square = lax.broadcasted_iota(jnp.int32, (n, n), 0) == lax.broadcasted_iota(jnp.int32, (n, n), 1)
@@ -113,13 +118,15 @@
     return lax.rem(lax.axis_index("blk"), 2) == lax.axis_index("rep")
 
 
-def waits_longest():
-    return jnp.logical_and(lax.rem(lax.axis_index("blk"), 4) == 2, lax.axis_index("rep") == 1)
-
-
-def own_tiles(left, right, vecs, total, first):
-    half = lax.rem(lax.axis_index("blk"), 2)
-
+def this_core():
+    return lax.rem(lax.axis_index("blk"), 2)
+
+
+def far_from_other_z():
+    return jnp.logical_and(lax.rem(lax.axis_index("blk"), 4) >= 2, lax.axis_index("rep") == 1)
+
+
+def own_tiles(left, right, vecs, total, half, first):
     def diagonal(i):
         rows = span(i)
         add_columns(total, rows, vecs, rows, halves(matern(squares(left[rows, :], right[:, rows]))))
@@ -161,25 +168,21 @@
     left[...] = left_side(points).T
     right[...] = right_side(points)
     vecs[...] = both_pieces(jnp.where(mine, dirs[...], swap_dir_ref[...]))
-    own_tiles(left, right, vecs, total, True)
-
-
-def early_kernel(left, right, vecs, total_in, scale_in, total, scale):
-    total[...] = total_in[...]
-    scale[...] = scale_in[...]
-
-    @pl.when(waits_longest())
-    def _():
-        own_tiles(left, right, vecs, total, False)
+    own_tiles(left, right, vecs, total, this_core(), True)
 
 
 def late_kernel(left, right, vecs, total_in, back_in, total, back):
     total[...] = total_in[...]
     back[...] = back_in[...]
-
-    @pl.when(jnp.logical_not(waits_longest()))
+    core = this_core()
+
+    @pl.when(jnp.logical_or(core == 1, jnp.logical_not(far_from_other_z())))
     def _():
-        own_tiles(left, right, vecs, total, False)
+        own_tiles(left, right, vecs, total, core, False)
+
+    @pl.when(jnp.logical_and(core == 1, far_from_other_z()))
+    def _():
+        own_tiles(left, right, vecs, total, 1 - core, False)
 
 
 def kernel_kernel(left, vecs, far_pts_ref, scale_ref, back_ref, kernel_ref, right, total, sq, parts):
@@ -188,10 +191,10 @@
     cols = [slice(c * WIDTH, (c + 1) * WIDTH) for c in range(ACROSS)]
 
     def distances(r, c):
-        sq[c % 2] = squares(left[span(r), :], right[:, cols[c]])
+        sq[c % 2] = squares(left[tall_span(r), :], right[:, cols[c]])
 
     def product(r, c):
-        add_columns(total, cols[c], vecs, span(r), (parts[c % 2, 0], parts[c % 2, 1]))
+        add_columns(total, cols[c], vecs, tall_span(r), (parts[c % 2, 0], parts[c % 2, 1]))
 
     distances(0, 0)
 
@@ -200,16 +203,16 @@
             if c + 1 < ACROSS:
                 distances(r, c + 1)
             else:
-                distances(jnp.minimum(r + 1, STEPS - 1), 0)
+                distances(jnp.minimum(r + 1, BLOCK // HEIGHT - 1), 0)
             kernel = matern(sq[c % 2])
-            kernel_ref[span(r), cols[c]] = kernel
+            kernel_ref[tall_span(r), cols[c]] = kernel
             parts[c % 2, 0], parts[c % 2, 1] = halves(kernel)
             if c > 0:
                 product(r, c - 1)
         product(r, ACROSS - 1)
         return carry
 
-    lax.fori_loop(0, STEPS, some_rows, 0)
+    lax.fori_loop(0, BLOCK // HEIGHT, some_rows, 0)
     back_ref[...] = folded(total[...], SHARE)
 
 
@@ -374,9 +377,6 @@
     )(points, swap_pts, lengths, direction, swap_dir)
     later, scale = lax.optimization_barrier((direction, scale))
     far_dir = permuted(later, to_partner)
-    total, scale = call(
-        early_kernel, [total_shape, (DIM, 128)], "vvvvv", name="own_early"
-    )(left, right, vecs, total, scale)
     back, kernel = call(
         kernel_kernel,
         [whole, (BLOCK, BLOCK)],
@@ -384,8 +384,8 @@
         [
             pltpu.VMEM(*right_shape),
             pltpu.VMEM(*total_shape),
-            pltpu.VMEM((2, TILE, WIDTH), F32),
-            pltpu.VMEM((2, 2, TILE, WIDTH), BF16),
+            pltpu.VMEM((2, HEIGHT, WIDTH), F32),
+            pltpu.VMEM((2, 2, HEIGHT, WIDTH), BF16),
         ],
         "cross_kernel",
     )(left, vecs, far_pts, scale)

time: 58.4 us -> 58.1 us (level)
    pallas_call x7 -> x6, Pallas kernels: 21.1 us -> 21 us  [placed(): run(*(pltpu.with_memory_space_constraint(a, pltpu.HBM) if i == 'h' else a...]
  transfers between devices with their start and end apart: 8 -> 8, of which waited for: 4 -> 4; matrix products, arithmetic and copies ran while one was open for 0% -> 0% of each run, Pallas kernels for 34% -> 33%
where the time goes in v10:
time: 58.1 us; the launch traced here: 57.5 us
  Pallas kernels  21 us (36%)
  starting transfers between devices  15.6 us (27%)
  blocking collectives  15.2 us (26%)
  waiting for transfers between devices  4.73 us (8%)
  between operations  0.88 us (2%)
    pallas_call x6, Pallas kernels, placed(): run(*(pltpu.with_memory_space_constraint(a, pltpu.HBM) if i == 'h' else a...  21 us
    ppermute x8, starting transfers between devices, permuted(): return lax.ppermute(value, AXES, pairs)  15.6 us
    all_to_all x1, blocking collectives, over_chips(): return lax.all_to_all(value, AXES, 0, 0, axis_index_groups=groups)  15.2 us
    ppermute x8, waiting for transfers between devices, permuted(): return lax.ppermute(value, AXES, pairs)  4.73 us
  transfers between devices with their start and end apart: 8, of which 4 were waited for; matrix products, arithmetic and copies ran while one was open for 0% of the time, Pallas kernels for 33%

profile of v10, /device:TPU:1, one launch (start us, length us, event | category | flops | bytes accessed | tf_op | source)
XLA Modules:
  0.0 57.5 jit_solution(1755932875245640966)
XLA Ops:
  0.6 0.0 copy-start
  0.6 0.0 copy-start.1
  0.7 3.3 %collective-permute-start.1 = (f32[32,2048]{1,0:T(8,128)}, f32[32,2048]{1,0:T(8,128)S(1)}, u32[]{:S(2)}, u32[]{:S(2)}) collective-permute-start(f32[32,2048]{1,0:T(8,128)} %dir_ref.5), channel_id=1, source_target_pairs={{0,2},{1,3},{2,0},{3,1},{4,6},{5,7},{6,4},{7,5},{8,10},{9,11},{10,... | collective-permute-start | bytes 786440 | tf_op jit(solution)/shard_map/ppermute | solution.py:302
  4.0 0.1 collective-permute-start
  4.1 1.0 %collective-permute-start.2 = (f32[32,2048]{1,0:T(8,128)}, f32[32,2048]{1,0:T(8,128)S(1)}, u32[]{:S(2)}, u32[]{:S(2)}) collective-permute-start(f32[32,2048]{1,0:T(8,128)} %pts_ref.1), channel_id=1, source_target_pairs={{0,189},{1,64},{2,194},{3,67},{4,68},{5,193},{6,198},{7,71},{8,72}... | collective-permute-start | bytes 786440 | tf_op jit(solution)/shard_map/ppermute | solution.py:302
  5.1 0.3 collective-permute-done.1.swap_dir_ref
  5.4 0.4 collective-permute-done.swap_pts_ref
  5.8 3.3 %own_start.1 = (bf16[2048,256]{1,0:T(8,128)(2,1)S(1)}, bf16[256,2048]{1,0:T(8,128)(2,1)S(1)}, bf16[64,2048]{1,0:T(8,128)(2,1)S(1)}, f32[64,2048]{1,0:T(8,128)S(1)}, f32[32,128]{1,0:T(8,128)S(1)}) custom-call(f32[32,2048]{1,0:T(8,128)} %pts_ref.1, f32[32,2048]{1,0:T(8,128)S(1)} %collective-permute-done.swap_pts_ref, f32[1,32]{1,0:T(1,128)} %bitcast.3, ...), custom_call_target="tpu_custom_call" | custom-call | tf_op jit(solution)/shard_map/own_start/pallas_call | solution.py:352
  9.0 1.1 %collective-permute-start.3 = (f32[32,2048]{1,0:T(8,128)}, f32[32,2048]{1,0:T(8,128)S(1)}, u32[]{:S(2)}, u32[]{:S(2)}) collective-permute-start(f32[32,2048]{1,0:T(8,128)} %dir_ref.5), channel_id=1, source_target_pairs={{0,189},{1,64},{2,194},{3,67},{4,68},{5,193},{6,198},{7,71},{8,72}... | collective-permute-start | bytes 786440 | tf_op jit(solution)/shard_map/ppermute | solution.py:302
  10.1 0.0 collective-permute-done.2.far_pts_ref
  10.1 8.5 %cross_kernel.1 = (f32[32,2048]{1,0:T(8,128)S(1)}, f32[2048,2048]{1,0:T(8,128)S(1)}) custom-call(bf16[2048,256]{1,0:T(8,128)(2,1)S(1)} %get-tuple-element.16.left, bf16[64,2048]{1,0:T(8,128)(2,1)S(1)} %get-tuple-element.17.vecs, f32[32,2048]{1,0:T(8,128)S(1)} %collective-permute-done.2.far_pts_ref, f32[32,128]{1,0:T(8,128)S(1)} %get-tuple-element.19.scale_ref), custom_call_target="tpu_custom_call" | custom-call | tf_op jit(solution)/shard_map/cross_kernel/pallas_call | solution.py:352
  18.7 2.7 %own_late.1 = (f32[64,2048]{1,0:T(8,128)S(1)}, f32[32,2048]{1,0:T(8,128)S(1)}) custom-call(bf16[2048,256]{1,0:T(8,128)(2,1)S(1)} %get-tuple-element.16.left, bf16[256,2048]{1,0:T(8,128)(2,1)S(1)} %get-tuple-element.22.right, bf16[64,2048]{1,0:T(8,128)(2,1)S(1)} %get-tuple-element.17.vecs, f32[64,2048]{1,0:T(8,128)S(1)} %get-tuple-element.23.total_in, ...), custom_call_target="tpu_custom_call" | custom-call | tf_op jit(solution)/shard_map/own_late/pallas_call | solution.py:352
  21.4 7.6 %collective-permute-start.4 = (f32[32,2048]{1,0:T(8,128)S(1)}, f32[32,2048]{1,0:T(8,128)S(1)}, u32[]{:S(2)}, u32[]{:S(2)}) collective-permute-start(f32[32,2048]{1,0:T(8,128)S(1)} %get-tuple-element.26), channel_id=1, source_target_pairs={{0,192},{1,70},{2,65},{3,195},{4,196},{5,74},{6,69},{7,199},{8,200... | collective-permute-start | bytes 786440 | tf_op jit(solution)/shard_map/ppermute | solution.py:302
  29.0 1.8 %collective-permute-start.6 = (f32[32,2048]{1,0:T(8,128)}, f32[32,2048]{1,0:T(8,128)S(1)}, u32[]{:S(2)}, u32[]{:S(2)}) collective-permute-start(f32[32,2048]{1,0:T(8,128)} %res_ref.3), channel_id=1, source_target_pairs={{0,2},{1,3},{2,0},{3,1},{4,6},{5,7},{6,4},{7,5},{8,10},{9,11},{10,... | collective-permute-start | bytes 786440 | tf_op jit(solution)/shard_map/ppermute | solution.py:302
  30.8 0.0 collective-permute-done.3.far_dir_ref
  30.8 4.7 %cross_product.1 = f32[32,2048]{1,0:T(8,128)S(1)} custom-call(f32[2048,2048]{1,0:T(8,128)S(1)} %get-tuple-element.20.kernel_ref, f32[32,2048]{1,0:T(8,128)S(1)} %collective-permute-done.3.far_dir_ref, f32[64,2048]{1,0:T(8,128)S(1)} %get-tuple-element.25.total_ref), custom_call_target="tpu_custom_call" | custom-call | tf_op jit(solution)/shard_map/cross_product/pallas_call | solution.py:352
  35.6 2.9 %collective-permute-done.4 = f32[32,2048]{1,0:T(8,128)S(1)} collective-permute-done((f32[32,2048]{1,0:T(8,128)S(1)}, f32[32,2048]{1,0:T(8,128)S(1)}, u32[]{:S(2)}, u32[]{:S(2)}) %collective-permute-start.4) | collective-permute-done | bytes 262176 | tf_op jit(solution)/shard_map/ppermute | solution.py:302
  38.5 0.6 %collective-permute-start.5 = (f32[32,2048]{1,0:T(8,128)S(1)}, f32[32,2048]{1,0:T(8,128)S(1)}, u32[]{:S(2)}, u32[]{:S(2)}) collective-permute-start(f32[32,2048]{1,0:T(8,128)S(1)} %add.3.part_ref), channel_id=1, source_target_pairs={{0,2},{1,3},{2,0},{3,1},{4,6},{5,7},{6,4},{7,5},{8,10},{9,11},{10,... | collective-permute-start | bytes 786440 | tf_op jit(solution)/shard_map/ppermute | solution.py:302
  39.1 0.0 collective-permute-done.6.swap_res_ref
  39.1 1.2 %collective-permute-done.5.other_ref = f32[32,2048]{1,0:T(8,128)S(1)} collective-permute-done((f32[32,2048]{1,0:T(8,128)S(1)}, f32[32,2048]{1,0:T(8,128)S(1)}, u32[]{:S(2)}, u32[]{:S(2)}) %collective-permute-start.5) | collective-permute-done | bytes 262176 | tf_op jit(solution)/shard_map/ppermute | solution.py:302
  40.3 0.4 sums.1
  40.6 0.1 collective-permute-start.7
  40.7 15.2 %all_to_all.5.sums_ref = f32[128,1,128]{2,1,0:T(1,128)S(1)} all-to-all(f32[128,1,128]{2,1,0:T(1,128)S(1)} %get-tuple-element.27), channel_id=1, replica_groups={{164,228,172,165,161,156,100,236,229,225,220,180,173,169,160,157,153,14..., dimensions={0} | all-to-all | bytes 131072 | tf_op jit(solution)/shard_map/all_to_all | solution.py:335
  55.9 1.4 %update.1 = (f32[32,2048]{1,0:T(8,128)}, f32[32,2048]{1,0:T(8,128)}, f32[32,2048]{1,0:T(8,128)}) custom-call(f32[128,1,128]{2,1,0:T(1,128)S(1)} %all_to_all.5.sums_ref, s32[1,32]{1,0:T(1,128)S(1)} %bitcast.2, f32[32,2048]{1,0:T(8,128)S(1)} %get-tuple-element.28.image_ref, f32[32,2048]{1,0:T(8,128)S(1)} %collective-permute-done.7.other_ref, ...), custom_call_target="tpu_custom_call" | custom-call | tf_op jit(solution)/shard_map/update/pallas_call | solution.py:352
  (8 shorter events, 0.1 us)
Async XLA Ops:
  0.6 39.6 %copy-start = (f32[32,2048]{1,0:T(8,128)S(1)}, f32[32,2048]{1,0:T(8,128)}, u32[]{:S(2)}) copy-start(f32[32,2048]{1,0:T(8,128)} %dir_ref.5) | copy-start | bytes 786436
  0.6 39.6 %copy-start.1 = (f32[32,2048]{1,0:T(8,128)S(1)}, f32[32,2048]{1,0:T(8,128)}, u32[]{:S(2)}) copy-start(f32[32,2048]{1,0:T(8,128)} %res_ref.3) | copy-start | bytes 786436
  0.7 55.3 %copy-start.3 = (s32[32]{0:T(128)S(1)}, s32[32]{0:T(128)}, u32[]{:S(2)}) copy-start(s32[32]{0:T(128)} %param.11) | copy-start | bytes 388
  0.7 55.3 %copy-start.2 = (f32[32,2048]{1,0:T(8,128)S(1)}, f32[32,2048]{1,0:T(8,128)}, u32[]{:S(2)}) copy-start(f32[32,2048]{1,0:T(8,128)} %sol_ref.1) | copy-start | bytes 786436
  0.7 4.7 %collective-permute-start.1 = (f32[32,2048]{1,0:T(8,128)}, f32[32,2048]{1,0:T(8,128)S(1)}, u32[]{:S(2)}, u32[]{:S(2)}) collective-permute-start(f32[32,2048]{1,0:T(8,128)} %dir_ref.5), channel_id=1, source_target_pairs={{0,2},{1,3},{2,0},{3,1},{4,6},{5,7},{6,4},{7,5},{8,10},{9,11},{10,... | collective-permute-start | bytes 786440 | tf_op jit(solution)/shard_map/ppermute | solution.py:302
  4.0 1.7 %collective-permute-start = (f32[32,2048]{1,0:T(8,128)}, f32[32,2048]{1,0:T(8,128)S(1)}, u32[]{:S(2)}, u32[]{:S(2)}) collective-permute-start(f32[32,2048]{1,0:T(8,128)} %pts_ref.1), channel_id=1, source_target_pairs={{0,2},{1,3},{2,0},{3,1},{4,6},{5,7},{6,4},{7,5},{8,10},{9,11},{10,... | collective-permute-start | bytes 786440 | tf_op jit(solution)/shard_map/ppermute | solution.py:302
  4.1 6.0 %collective-permute-start.2 = (f32[32,2048]{1,0:T(8,128)}, f32[32,2048]{1,0:T(8,128)S(1)}, u32[]{:S(2)}, u32[]{:S(2)}) collective-permute-start(f32[32,2048]{1,0:T(8,128)} %pts_ref.1), channel_id=1, source_target_pairs={{0,189},{1,64},{2,194},{3,67},{4,68},{5,193},{6,198},{7,71},{8,72}... | collective-permute-start | bytes 786440 | tf_op jit(solution)/shard_map/ppermute | solution.py:302
  9.0 21.8 %collective-permute-start.3 = (f32[32,2048]{1,0:T(8,128)}, f32[32,2048]{1,0:T(8,128)S(1)}, u32[]{:S(2)}, u32[]{:S(2)}) collective-permute-start(f32[32,2048]{1,0:T(8,128)} %dir_ref.5), channel_id=1, source_target_pairs={{0,189},{1,64},{2,194},{3,67},{4,68},{5,193},{6,198},{7,71},{8,72}... | collective-permute-start | bytes 786440 | tf_op jit(solution)/shard_map/ppermute | solution.py:302
  21.4 17.1 %collective-permute-start.4 = (f32[32,2048]{1,0:T(8,128)S(1)}, f32[32,2048]{1,0:T(8,128)S(1)}, u32[]{:S(2)}, u32[]{:S(2)}) collective-permute-start(f32[32,2048]{1,0:T(8,128)S(1)} %get-tuple-element.26), channel_id=1, source_target_pairs={{0,192},{1,70},{2,65},{3,195},{4,196},{5,74},{6,69},{7,199},{8,200... | collective-permute-start | bytes 786440 | tf_op jit(solution)/shard_map/ppermute | solution.py:302
  29.0 10.1 %collective-permute-start.6 = (f32[32,2048]{1,0:T(8,128)}, f32[32,2048]{1,0:T(8,128)S(1)}, u32[]{:S(2)}, u32[]{:S(2)}) collective-permute-start(f32[32,2048]{1,0:T(8,128)} %res_ref.3), channel_id=1, source_target_pairs={{0,2},{1,3},{2,0},{3,1},{4,6},{5,7},{6,4},{7,5},{8,10},{9,11},{10,... | collective-permute-start | bytes 786440 | tf_op jit(solution)/shard_map/ppermute | solution.py:302
  38.5 1.7 %collective-permute-start.5 = (f32[32,2048]{1,0:T(8,128)S(1)}, f32[32,2048]{1,0:T(8,128)S(1)}, u32[]{:S(2)}, u32[]{:S(2)}) collective-permute-start(f32[32,2048]{1,0:T(8,128)S(1)} %add.3.part_ref), channel_id=1, source_target_pairs={{0,2},{1,3},{2,0},{3,1},{4,6},{5,7},{6,4},{7,5},{8,10},{9,11},{10,... | collective-permute-start | bytes 786440 | tf_op jit(solution)/shard_map/ppermute | solution.py:302
  40.6 15.3 %collective-permute-start.7 = (f32[32,2048]{1,0:T(8,128)S(1)}, f32[32,2048]{1,0:T(8,128)S(1)}, u32[]{:S(2)}, u32[]{:S(2)}) collective-permute-start(f32[32,2048]{1,0:T(8,128)S(1)} %get-tuple-element.28.image_ref), channel_id=1, source_target_pairs={{0,1},{1,0},{2,3},{3,2},{4,5},{5,4},{6,7},{7,6},{8,9},{9,8},{10,11... | collective-permute-start | bytes 786440 | tf_op jit(solution)/shard_map/ppermute | solution.py:302

commit v11 on v10

--- a/solution.py
+++ b/solution.py
@@ -171,9 +171,7 @@
     own_tiles(left, right, vecs, total, this_core(), True)
 
 
-def late_kernel(left, right, vecs, total_in, back_in, total, back):
-    total[...] = total_in[...]
-    back[...] = back_in[...]
+def own_rest(left, right, vecs, total):
     core = this_core()
 
     @pl.when(jnp.logical_or(core == 1, jnp.logical_not(far_from_other_z())))
@@ -185,7 +183,9 @@
         own_tiles(left, right, vecs, total, 1 - core, False)
 
 
-def kernel_kernel(left, vecs, far_pts_ref, scale_ref, back_ref, kernel_ref, right, total, sq, parts):
+def kernel_kernel(
+    left, vecs, far_pts_ref, scale_ref, own_right, own_in, back_ref, kernel_ref, own_total, right, total, sq, parts
+):
     right[...] = right_side(far_pts_ref[...] * scale_ref[:, 0:1])
     total[...] = jnp.zeros_like(total)
     cols = [slice(c * WIDTH, (c + 1) * WIDTH) for c in range(ACROSS)]
@@ -214,6 +214,8 @@
 
     lax.fori_loop(0, BLOCK // HEIGHT, some_rows, 0)
     back_ref[...] = folded(total[...], SHARE)
+    own_total[...] = own_in[...]
+    own_rest(left, own_right, vecs, own_total)
 
 
 def product_kernel(kernel_ref, far_dir_ref, total_ref, own_ref, far_vecs, far_coarse, tall):
@@ -377,10 +379,10 @@
     )(points, swap_pts, lengths, direction, swap_dir)
     later, scale = lax.optimization_barrier((direction, scale))
     far_dir = permuted(later, to_partner)
-    back, kernel = call(
+    back, kernel, total = call(
         kernel_kernel,
-        [whole, (BLOCK, BLOCK)],
-        "vvvv",
+        [whole, (BLOCK, BLOCK), total_shape],
+        "vvvvvv",
         [
             pltpu.VMEM(*right_shape),
             pltpu.VMEM(*total_shape),
@@ -388,10 +390,7 @@
             pltpu.VMEM((2, 2, HEIGHT, WIDTH), BF16),
         ],
         "cross_kernel",
-    )(left, vecs, far_pts, scale)
-    total, back = call(late_kernel, [total_shape, whole], "vvvvv", name="own_late")(
-        left, right, vecs, total, back
-    )
+    )(left, vecs, far_pts, scale, right, total)
     back = permuted(back, to_home)
     tall = (BLOCK, 128)
     (own,) = call(

time: 58.1 us -> 58.1 us (level)
    pallas_call x6 -> x5, Pallas kernels: 21 us -> 21 us  [placed(): run(*(pltpu.with_memory_space_constraint(a, pltpu.HBM) if i == 'h' else a...]
  transfers between devices with their start and end apart: 8 -> 8, of which waited for: 4 -> 4; matrix products, arithmetic and copies ran while one was open for 0% -> 0% of each run, Pallas kernels for 33% -> 34%
where the time goes in v11:
time: 58.1 us; the launch traced here: 57.4 us
  Pallas kernels  21 us (36%)
  starting transfers between devices  15.6 us (27%)
  blocking collectives  15.2 us (26%)
  waiting for transfers between devices  4.71 us (8%)
  between operations  0.88 us (2%)
    pallas_call x5, Pallas kernels, placed(): run(*(pltpu.with_memory_space_constraint(a, pltpu.HBM) if i == 'h' else a...  21 us
    ppermute x8, starting transfers between devices, permuted(): return lax.ppermute(value, AXES, pairs)  15.6 us
    all_to_all x1, blocking collectives, over_chips(): return lax.all_to_all(value, AXES, 0, 0, axis_index_groups=groups)  15.2 us
    ppermute x8, waiting for transfers between devices, permuted(): return lax.ppermute(value, AXES, pairs)  4.71 us
  transfers between devices with their start and end apart: 8, of which 4 were waited for; matrix products, arithmetic and copies ran while one was open for 0% of the time, Pallas kernels for 34%

profile of v11, /device:TPU:1, one launch (start us, length us, event | category | flops | bytes accessed | tf_op | source)
XLA Modules:
  0.0 57.4 jit_solution(8918822088968628748)
XLA Ops:
  0.6 0.0 copy-start
  0.6 0.0 copy-start.1
  0.7 3.3 %collective-permute-start.1 = (f32[32,2048]{1,0:T(8,128)}, f32[32,2048]{1,0:T(8,128)S(1)}, u32[]{:S(2)}, u32[]{:S(2)}) collective-permute-start(f32[32,2048]{1,0:T(8,128)} %dir_ref.5), channel_id=1, source_target_pairs={{0,2},{1,3},{2,0},{3,1},{4,6},{5,7},{6,4},{7,5},{8,10},{9,11},{10,... | collective-permute-start | bytes 786440 | tf_op jit(solution)/shard_map/ppermute | solution.py:304
  4.0 0.1 collective-permute-start
  4.1 1.0 %collective-permute-start.2 = (f32[32,2048]{1,0:T(8,128)}, f32[32,2048]{1,0:T(8,128)S(1)}, u32[]{:S(2)}, u32[]{:S(2)}) collective-permute-start(f32[32,2048]{1,0:T(8,128)} %pts_ref.1), channel_id=1, source_target_pairs={{0,189},{1,64},{2,194},{3,67},{4,68},{5,193},{6,198},{7,71},{8,72}... | collective-permute-start | bytes 786440 | tf_op jit(solution)/shard_map/ppermute | solution.py:304
  5.1 0.3 collective-permute-done.1.swap_dir_ref
  5.4 0.4 collective-permute-done.swap_pts_ref
  5.8 3.3 %own_start.1 = (bf16[2048,256]{1,0:T(8,128)(2,1)S(1)}, bf16[256,2048]{1,0:T(8,128)(2,1)S(1)}, bf16[64,2048]{1,0:T(8,128)(2,1)S(1)}, f32[64,2048]{1,0:T(8,128)S(1)}, f32[32,128]{1,0:T(8,128)S(1)}) custom-call(f32[32,2048]{1,0:T(8,128)} %pts_ref.1, f32[32,2048]{1,0:T(8,128)S(1)} %collective-permute-done.swap_pts_ref, f32[1,32]{1,0:T(1,128)} %bitcast.3, ...), custom_call_target="tpu_custom_call" | custom-call | tf_op jit(solution)/shard_map/own_start/pallas_call | solution.py:354
  9.0 1.1 %collective-permute-start.3 = (f32[32,2048]{1,0:T(8,128)}, f32[32,2048]{1,0:T(8,128)S(1)}, u32[]{:S(2)}, u32[]{:S(2)}) collective-permute-start(f32[32,2048]{1,0:T(8,128)} %dir_ref.5), channel_id=1, source_target_pairs={{0,189},{1,64},{2,194},{3,67},{4,68},{5,193},{6,198},{7,71},{8,72}... | collective-permute-start | bytes 786440 | tf_op jit(solution)/shard_map/ppermute | solution.py:304
  10.1 0.0 collective-permute-done.2.far_pts_ref
  10.1 11.2 %cross_kernel.1 = (f32[32,2048]{1,0:T(8,128)S(1)}, f32[2048,2048]{1,0:T(8,128)S(1)}, f32[64,2048]{1,0:T(8,128)S(1)}) custom-call(bf16[2048,256]{1,0:T(8,128)(2,1)S(1)} %get-tuple-element.15.left, bf16[64,2048]{1,0:T(8,128)(2,1)S(1)} %get-tuple-element.16.vecs, f32[32,2048]{1,0:T(8,128)S(1)} %collective-permute-done.2.far_pts_ref, ...), custom_call_target="tpu_custom_call" | custom-call | tf_op jit(solution)/shard_map/cross_kernel/pallas_call | solution.py:354
  21.4 7.6 %collective-permute-start.4 = (f32[32,2048]{1,0:T(8,128)S(1)}, f32[32,2048]{1,0:T(8,128)S(1)}, u32[]{:S(2)}, u32[]{:S(2)}) collective-permute-start(f32[32,2048]{1,0:T(8,128)S(1)} %get-tuple-element.24), channel_id=1, source_target_pairs={{0,192},{1,70},{2,65},{3,195},{4,196},{5,74},{6,69},{7,199},{8,200... | collective-permute-start | bytes 786440 | tf_op jit(solution)/shard_map/ppermute | solution.py:304
  28.9 1.9 %collective-permute-start.6 = (f32[32,2048]{1,0:T(8,128)}, f32[32,2048]{1,0:T(8,128)S(1)}, u32[]{:S(2)}, u32[]{:S(2)}) collective-permute-start(f32[32,2048]{1,0:T(8,128)} %res_ref.3), channel_id=1, source_target_pairs={{0,2},{1,3},{2,0},{3,1},{4,6},{5,7},{6,4},{7,5},{8,10},{9,11},{10,... | collective-permute-start | bytes 786440 | tf_op jit(solution)/shard_map/ppermute | solution.py:304
  30.8 0.0 collective-permute-done.3.far_dir_ref
  30.8 4.7 %cross_product.1 = f32[32,2048]{1,0:T(8,128)S(1)} custom-call(f32[2048,2048]{1,0:T(8,128)S(1)} %get-tuple-element.21.kernel_ref, f32[32,2048]{1,0:T(8,128)S(1)} %collective-permute-done.3.far_dir_ref, f32[64,2048]{1,0:T(8,128)S(1)} %get-tuple-element.23.total_ref), custom_call_target="tpu_custom_call" | custom-call | tf_op jit(solution)/shard_map/cross_product/pallas_call | solution.py:354
  35.5 2.9 %collective-permute-done.4 = f32[32,2048]{1,0:T(8,128)S(1)} collective-permute-done((f32[32,2048]{1,0:T(8,128)S(1)}, f32[32,2048]{1,0:T(8,128)S(1)}, u32[]{:S(2)}, u32[]{:S(2)}) %collective-permute-start.4) | collective-permute-done | bytes 262176 | tf_op jit(solution)/shard_map/ppermute | solution.py:304
  38.5 0.6 collective-permute-start.5
  39.0 0.0 collective-permute-done.6.swap_res_ref
  39.0 1.2 %collective-permute-done.5.other_ref = f32[32,2048]{1,0:T(8,128)S(1)} collective-permute-done((f32[32,2048]{1,0:T(8,128)S(1)}, f32[32,2048]{1,0:T(8,128)S(1)}, u32[]{:S(2)}, u32[]{:S(2)}) %collective-permute-start.5) | collective-permute-done | bytes 262176 | tf_op jit(solution)/shard_map/ppermute | solution.py:304
  40.2 0.4 sums.1
  40.6 0.1 collective-permute-start.7
  40.7 15.2 %all_to_all.5.sums_ref = f32[128,1,128]{2,1,0:T(1,128)S(1)} all-to-all(f32[128,1,128]{2,1,0:T(1,128)S(1)} %get-tuple-element.25), channel_id=1, replica_groups={{164,228,172,165,161,156,100,236,229,225,220,180,173,169,160,157,153,14..., dimensions={0} | all-to-all | bytes 131072 | tf_op jit(solution)/shard_map/all_to_all | solution.py:337
  55.9 0.0 collective-permute-done.7.other_ref
  55.9 1.4 %update.1 = (f32[32,2048]{1,0:T(8,128)}, f32[32,2048]{1,0:T(8,128)}, f32[32,2048]{1,0:T(8,128)}) custom-call(f32[128,1,128]{2,1,0:T(1,128)S(1)} %all_to_all.5.sums_ref, s32[1,32]{1,0:T(1,128)S(1)} %bitcast.2, f32[32,2048]{1,0:T(8,128)S(1)} %get-tuple-element.26.image_ref, f32[32,2048]{1,0:T(8,128)S(1)} %collective-permute-done.7.other_ref, ...), custom_call_target="tpu_custom_call" | custom-call | tf_op jit(solution)/shard_map/update/pallas_call | solution.py:354
  (7 shorter events, 0.0 us)
Async XLA Ops:
  0.6 39.6 %copy-start = (f32[32,2048]{1,0:T(8,128)S(1)}, f32[32,2048]{1,0:T(8,128)}, u32[]{:S(2)}) copy-start(f32[32,2048]{1,0:T(8,128)} %dir_ref.5) | copy-start | bytes 786436
  0.6 39.6 %copy-start.1 = (f32[32,2048]{1,0:T(8,128)S(1)}, f32[32,2048]{1,0:T(8,128)}, u32[]{:S(2)}) copy-start(f32[32,2048]{1,0:T(8,128)} %res_ref.3) | copy-start | bytes 786436
  0.7 55.2 %copy-start.3 = (s32[32]{0:T(128)S(1)}, s32[32]{0:T(128)}, u32[]{:S(2)}) copy-start(s32[32]{0:T(128)} %param.11) | copy-start | bytes 388
  0.7 55.2 %copy-start.2 = (f32[32,2048]{1,0:T(8,128)S(1)}, f32[32,2048]{1,0:T(8,128)}, u32[]{:S(2)}) copy-start(f32[32,2048]{1,0:T(8,128)} %sol_ref.1) | copy-start | bytes 786436
  0.7 4.7 %collective-permute-start.1 = (f32[32,2048]{1,0:T(8,128)}, f32[32,2048]{1,0:T(8,128)S(1)}, u32[]{:S(2)}, u32[]{:S(2)}) collective-permute-start(f32[32,2048]{1,0:T(8,128)} %dir_ref.5), channel_id=1, source_target_pairs={{0,2},{1,3},{2,0},{3,1},{4,6},{5,7},{6,4},{7,5},{8,10},{9,11},{10,... | collective-permute-start | bytes 786440 | tf_op jit(solution)/shard_map/ppermute | solution.py:304
  4.0 1.7 %collective-permute-start = (f32[32,2048]{1,0:T(8,128)}, f32[32,2048]{1,0:T(8,128)S(1)}, u32[]{:S(2)}, u32[]{:S(2)}) collective-permute-start(f32[32,2048]{1,0:T(8,128)} %pts_ref.1), channel_id=1, source_target_pairs={{0,2},{1,3},{2,0},{3,1},{4,6},{5,7},{6,4},{7,5},{8,10},{9,11},{10,... | collective-permute-start | bytes 786440 | tf_op jit(solution)/shard_map/ppermute | solution.py:304
  4.1 6.0 %collective-permute-start.2 = (f32[32,2048]{1,0:T(8,128)}, f32[32,2048]{1,0:T(8,128)S(1)}, u32[]{:S(2)}, u32[]{:S(2)}) collective-permute-start(f32[32,2048]{1,0:T(8,128)} %pts_ref.1), channel_id=1, source_target_pairs={{0,189},{1,64},{2,194},{3,67},{4,68},{5,193},{6,198},{7,71},{8,72}... | collective-permute-start | bytes 786440 | tf_op jit(solution)/shard_map/ppermute | solution.py:304
  9.0 21.8 %collective-permute-start.3 = (f32[32,2048]{1,0:T(8,128)}, f32[32,2048]{1,0:T(8,128)S(1)}, u32[]{:S(2)}, u32[]{:S(2)}) collective-permute-start(f32[32,2048]{1,0:T(8,128)} %dir_ref.5), channel_id=1, source_target_pairs={{0,189},{1,64},{2,194},{3,67},{4,68},{5,193},{6,198},{7,71},{8,72}... | collective-permute-start | bytes 786440 | tf_op jit(solution)/shard_map/ppermute | solution.py:304
  21.4 17.1 %collective-permute-start.4 = (f32[32,2048]{1,0:T(8,128)S(1)}, f32[32,2048]{1,0:T(8,128)S(1)}, u32[]{:S(2)}, u32[]{:S(2)}) collective-permute-start(f32[32,2048]{1,0:T(8,128)S(1)} %get-tuple-element.24), channel_id=1, source_target_pairs={{0,192},{1,70},{2,65},{3,195},{4,196},{5,74},{6,69},{7,199},{8,200... | collective-permute-start | bytes 786440 | tf_op jit(solution)/shard_map/ppermute | solution.py:304
  28.9 10.1 %collective-permute-start.6 = (f32[32,2048]{1,0:T(8,128)}, f32[32,2048]{1,0:T(8,128)S(1)}, u32[]{:S(2)}, u32[]{:S(2)}) collective-permute-start(f32[32,2048]{1,0:T(8,128)} %res_ref.3), channel_id=1, source_target_pairs={{0,2},{1,3},{2,0},{3,1},{4,6},{5,7},{6,4},{7,5},{8,10},{9,11},{10,... | collective-permute-start | bytes 786440 | tf_op jit(solution)/shard_map/ppermute | solution.py:304
  38.5 1.7 %collective-permute-start.5 = (f32[32,2048]{1,0:T(8,128)S(1)}, f32[32,2048]{1,0:T(8,128)S(1)}, u32[]{:S(2)}, u32[]{:S(2)}) collective-permute-start(f32[32,2048]{1,0:T(8,128)S(1)} %add.3.part_ref), channel_id=1, source_target_pairs={{0,2},{1,3},{2,0},{3,1},{4,6},{5,7},{6,4},{7,5},{8,10},{9,11},{10,... | collective-permute-start | bytes 786440 | tf_op jit(solution)/shard_map/ppermute | solution.py:304
  40.6 15.3 %collective-permute-start.7 = (f32[32,2048]{1,0:T(8,128)S(1)}, f32[32,2048]{1,0:T(8,128)S(1)}, u32[]{:S(2)}, u32[]{:S(2)}) collective-permute-start(f32[32,2048]{1,0:T(8,128)S(1)} %get-tuple-element.26.image_ref), channel_id=1, source_target_pairs={{0,1},{1,0},{2,3},{3,2},{4,5},{5,4},{6,7},{7,6},{8,9},{9,8},{10,11... | collective-permute-start | bytes 786440 | tf_op jit(solution)/shard_map/ppermute | solution.py:304
